TPU v7x, 32 devices: a whole 2x2x4 slice. The times are simulated.
32 devices in a mesh: groups: 2 (over y), pool: 4 (over z), tensor: 4 (over x, core).
Axes of the slice: x: 2, y: 2, z: 4, core: 2. Of those that a mesh axis runs over, the one named last changes fastest.
Arguments:
- hidden: bfloat16 [1024, 4096], P(('groups', 'pool')), parts along dimension 0, may hold values from -6 to 6
- w_x: bfloat16 [4096, 4096], P(None, 'tensor'), may hold values from -0.09375 to 0.09375
- w_bc: bfloat16 [4096, 2048], P(None, 'tensor'), may hold values from -0.09375 to 0.09375
- w_dt: bfloat16 [4096, 64], P(None, 'tensor'), may hold values from -0.09375 to 0.09375
- conv_x: float32 [4, 4096], P(None, 'tensor'), may hold values from -3 to 3
- conv_bc: float32 [4, 2048], P(None, 'tensor'), may hold values from -3 to 3
- dt_bias: float32 [64], P('tensor'), may hold values from -4 to -1
- a_log: float32 [64], P('tensor'), may hold values from 0 to 2.77
- d_skip: float32 [64], P('tensor'), may hold values from 0.5 to 1.5
- norm_gain: float32 [4096], P('tensor'), may hold values from 0.5 to 1.5
- w_out: bfloat16 [4096, 4096], P('tensor'), may hold values from -0.09375 to 0.09375
- ssm_pool: bfloat16 [144, 64, 64, 128], P(('groups', 'pool'), 'tensor'), parts along dimension 0, may hold values from -0.59765625 to 0.59765625
- conv_pool_x: bfloat16 [144, 3, 4096], P(('groups', 'pool'), None, 'tensor'), parts along dimension 0, may hold values from -6 to 6
- conv_pool_bc: bfloat16 [144, 3, 2048], P(('groups', 'pool'), None, 'tensor'), parts along dimension 0, may hold values from -6 to 6
- owners: int32 [128], P('groups'), parts along dimension 0, may hold values from 0 to 3, as said below
- slots: int32 [128], P('groups'), parts along dimension 0, may hold values from 0 to 17, as said below
- accepted: int32 [128], P('groups'), parts along dimension 0, may hold values from 1 to 8
Outputs:
- mixed: bfloat16 [1024, 4096], P(('groups', 'pool'), 'tensor'), parts along dimension 0
- new_ssm_pool: bfloat16 [144, 64, 64, 128], P(('groups', 'pool'), 'tensor'), parts along dimension 0
- new_conv_x: bfloat16 [144, 3, 4096], P(('groups', 'pool'), None, 'tensor'), parts along dimension 0
- new_conv_bc: bfloat16 [144, 3, 2048], P(('groups', 'pool'), None, 'tensor'), parts along dimension 0
There are 2 independent parts, one for each index of `groups`. A program takes and returns all parts, laid end to end along the dimension named above; an argument that names none is the same for every part. Nothing has to cross between parts.
Inputs may be any that keep to these rules, and one draw needn't show every extreme that they name: `owners`: of the requests of one pool index (aligned blocks of 16), at most 6 have their states on one pool index, and exactly 6 do for some pool index; every pool index holds the states of exactly 16 requests. `slots`: no two requests share an owner and a slot.
All inputs are finite; a program needn't handle non-finite values.
Results may differ from a plain program's by a relative error of at most 0.0071.
Values may be sent and summed in bfloat16 or wider, within the bound.
No kernel may reach another device: no remote copies, remote signals or barrier semaphores. Data moves between devices by JAX's collectives and lax.ppermute only.
A program may use at most 128 MiB of HBM per device.

v0:
```python
import jax
import jax.numpy as jnp
from jax import lax
from jax.sharding import PartitionSpec as P

HEADS = 64
HEAD_DIM = 64
STATE = 128
GROUPS = 8
DRAFT = 8


EPS = 1e-05


def conv_part(state_rows, raw_rows, weight, accepted):
    window = state_rows.shape[1]
    length_new = raw_rows.shape[1]
    joined = jnp.concatenate([state_rows, raw_rows], axis=1)
    summed = jnp.zeros(raw_rows.shape, jnp.float32)
    for offset in range(window + 1):
        summed = summed + weight[offset] * joined[:, offset : offset + length_new].astype(
            jnp.float32
        )
    picks = accepted[:, None] + jnp.arange(window, dtype=jnp.int32)[None, :]
    picks = jnp.broadcast_to(picks[:, :, None], (joined.shape[0], window, joined.shape[2]))
    kept_rows = jnp.take_along_axis(joined, picks, axis=1)
    return (jax.nn.silu(summed), kept_rows)


def zero_unused(values, valid):
    shaped = valid.reshape((valid.shape[0],) + (1,) * (values.ndim - 1))
    return jnp.where(shaped, values, jnp.zeros((), values.dtype))


def verify(rows, ssm_in, convx_in, convbc_in, accepted, params):
    w_x, w_bc, w_dt, conv_x, conv_bc, dt_bias, a_log, d_skip, norm_gain, w_out = params
    tok_rows = rows.shape[0]
    req_rows = tok_rows // DRAFT
    width_x = w_x.shape[1]
    width_bc = w_bc.shape[1]
    head_local = w_dt.shape[1]
    raw_x = jnp.dot(rows, w_x, preferred_element_type=jnp.float32).astype(jnp.bfloat16)
    raw_bc = jnp.dot(rows, w_bc, preferred_element_type=jnp.float32).astype(jnp.bfloat16)
    dt_raw = jnp.dot(rows, w_dt, preferred_element_type=jnp.float32)
    conv_out_x, kept_x = conv_part(
        convx_in, raw_x.reshape(req_rows, DRAFT, width_x), conv_x, accepted
    )
    conv_out_bc, kept_bc = conv_part(
        convbc_in, raw_bc.reshape(req_rows, DRAFT, width_bc), conv_bc, accepted
    )
    bc_share = conv_out_bc.astype(jnp.bfloat16).reshape(tok_rows, width_bc)
    bc_whole = lax.all_gather(bc_share, "tensor", axis=1, tiled=True)
    per_group = HEADS // GROUPS
    tensor_rank = lax.axis_index("tensor")
    first_group = tensor_rank * head_local // per_group
    group_span = max(1, head_local // per_group)
    bc_groups = bc_whole.reshape(req_rows, DRAFT, 2, GROUPS, STATE)
    bc_local = lax.dynamic_slice_in_dim(bc_groups, first_group, group_span, axis=3)
    bc_heads = jnp.repeat(bc_local, min(head_local, per_group), axis=3).astype(jnp.float32)
    b_heads = bc_heads[:, :, 0]
    c_heads = bc_heads[:, :, 1]
    step_size = jax.nn.softplus(dt_raw + dt_bias).reshape(req_rows, DRAFT, head_local)
    decay = jnp.exp(-step_size * jnp.exp(a_log))
    inputs = conv_out_x.reshape(req_rows, DRAFT, head_local, HEAD_DIM)
    carried = ssm_in.astype(jnp.float32)
    kept_state = jnp.zeros(carried.shape, jnp.float32)
    outputs = []
    for position in range(DRAFT):
        carried = (
            carried * decay[:, position, :, None, None]
            + (step_size[:, position, :, None] * inputs[:, position])[..., None]
            * b_heads[:, position, :, None, :]
        )
        readout = jnp.einsum(
            "rhpn,rhn->rhp", carried, c_heads[:, position], precision=lax.Precision.HIGHEST
        )
        outputs.append(readout + d_skip[None, :, None] * inputs[:, position])
        kept_state = jnp.where((accepted == position + 1)[:, None, None, None], carried, kept_state)
    ssm_y = jnp.stack(outputs, axis=1).reshape(tok_rows, head_local, HEAD_DIM)
    mean_sq = jnp.mean(ssm_y * ssm_y, axis=2)
    scale = lax.rsqrt(mean_sq + EPS)
    normed = ((ssm_y * scale[:, :, None]).reshape(tok_rows, width_x) * norm_gain).astype(
        jnp.bfloat16
    )
    partial_value = jnp.dot(normed, w_out, preferred_element_type=jnp.float32)
    mixed = lax.psum_scatter(partial_value, "tensor", scatter_dimension=1, tiled=True).astype(
        jnp.bfloat16
    )
    return (mixed, kept_state.astype(jnp.bfloat16), kept_x, kept_bc)


def body(
    hidden,
    w_x,
    w_bc,
    w_dt,
    conv_x,
    conv_bc,
    dt_bias,
    a_log,
    d_skip,
    norm_gain,
    w_out,
    ssm_pool,
    conv_pool_x,
    conv_pool_bc,
    owners,
    slots,
    accepted,
):
    params = (w_x, w_bc, w_dt, conv_x, conv_bc, dt_bias, a_log, d_skip, norm_gain, w_out)
    pool_count = lax.axis_size("pool")
    pool_rank = lax.axis_index("pool")
    tok_rows = hidden.shape[0]
    req_count = tok_rows // DRAFT
    request_count = owners.shape[0]
    share = req_count // pool_count
    capacity = share + share // 2
    slot_count = ssm_pool.shape[0]
    members = jnp.arange(request_count, dtype=jnp.int32)
    requester = members // req_count
    owner_hot = (owners[:, None] == jnp.arange(pool_count, dtype=jnp.int32)[None, :]).astype(
        jnp.int32
    )
    per_block = owner_hot.reshape(pool_count, req_count, pool_count)
    earlier = (jnp.cumsum(per_block, axis=1) - per_block).reshape(request_count, pool_count)
    rank_pair = jnp.sum(earlier * owner_hot, axis=1)
    at_owner = requester * capacity + rank_pair
    at_requester = owners * capacity + rank_pair
    places = jnp.arange(pool_count * capacity, dtype=jnp.int32)
    owned = owners == pool_rank
    owner_match = owned[None, :] & (at_owner[None, :] == places[:, None])
    owner_valid = jnp.any(owner_match, axis=1)
    owner_slot = jnp.sum(jnp.where(owner_match, slots[None, :], 0), axis=1)
    first_row = pool_rank * req_count
    my_place = lax.dynamic_slice_in_dim(at_requester, first_row, req_count)
    my_accept = lax.dynamic_slice_in_dim(accepted, first_row, req_count)
    local_ids = jnp.arange(req_count, dtype=jnp.int32)
    back_match = my_place[None, :] == places[:, None]
    back_valid = jnp.any(back_match, axis=1)
    back_index = jnp.sum(jnp.where(back_match, local_ids[None, :], 0), axis=1)
    sent = (
        zero_unused(ssm_pool[owner_slot], owner_valid),
        zero_unused(conv_pool_x[owner_slot], owner_valid),
        zero_unused(conv_pool_bc[owner_slot], owner_valid),
    )
    fetched = (
        lax.all_to_all(sent[0], "pool", split_axis=0, concat_axis=0, tiled=True),
        lax.all_to_all(sent[1], "pool", split_axis=0, concat_axis=0, tiled=True),
        lax.all_to_all(sent[2], "pool", split_axis=0, concat_axis=0, tiled=True),
    )
    mixed, new_state, new_cx, new_cbc = verify(
        hidden, fetched[0][my_place], fetched[1][my_place], fetched[2][my_place], my_accept, params
    )
    going_home = (
        zero_unused(new_state[back_index], back_valid),
        zero_unused(new_cx[back_index], back_valid),
        zero_unused(new_cbc[back_index], back_valid),
    )
    arrived = (
        lax.all_to_all(going_home[0], "pool", split_axis=0, concat_axis=0, tiled=True),
        lax.all_to_all(going_home[1], "pool", split_axis=0, concat_axis=0, tiled=True),
        lax.all_to_all(going_home[2], "pool", split_axis=0, concat_axis=0, tiled=True),
    )
    target = jnp.where(owner_valid, owner_slot, slot_count)
    ssm_out = ssm_pool.at[target].set(arrived[0], mode="drop")
    conv_x_out = conv_pool_x.at[target].set(arrived[1], mode="drop")
    conv_bc_out = conv_pool_bc.at[target].set(arrived[2], mode="drop")
    return (mixed, ssm_out, conv_x_out, conv_bc_out)


def solution(mesh):
    in_specs = (
        P(("groups", "pool"), None),
        P(None, "tensor"),
        P(None, "tensor"),
        P(None, "tensor"),
        P(None, "tensor"),
        P(None, "tensor"),
        P("tensor"),
        P("tensor"),
        P("tensor"),
        P("tensor"),
        P("tensor", None),
        P(("groups", "pool"), "tensor", None, None),
        P(("groups", "pool"), None, "tensor"),
        P(("groups", "pool"), None, "tensor"),
        P("groups"),
        P("groups"),
        P("groups"),
    )
    out_specs = (
        P(("groups", "pool"), "tensor"),
        P(("groups", "pool"), "tensor", None, None),
        P(("groups", "pool"), None, "tensor"),
        P(("groups", "pool"), None, "tensor"),
    )
    return jax.shard_map(body, mesh=mesh, in_specs=in_specs, out_specs=out_specs, check_vma=False)
```

profile of v0, /device:TPU:0, one launch (start us, length us, event | category | flops | bytes accessed | tf_op | source)
XLA Modules:
  0.0 1128.5 jit_solution(15873208274539055675)
XLA Ops:
  7.2 1.0 copy.161
  8.2 0.9 copy.160
  9.1 6.0 copy.159
  17.2 0.8 broadcast_select_fusion.5
  17.9 6.3 all-to-all-start.2
  25.0 0.8 broadcast_select_fusion.3
  25.8 6.9 gather_fusion
  32.7 5.1 all-to-all-start.1
  37.8 6.0 broadcast_select_fusion.1
  43.8 1.2 all-to-all-done.1
  45.1 5.2 all-to-all-start
  54.4 2.9 fusion.38
  57.3 4.6 fusion.37
  62.9 7.2 all_gather.3
  70.3 239.2 %gather_fusion.10 = bf16[24576]{0:T(1024)(128)(2,1)S(1)} fusion(bf16[16,11,512]{2,1,0:T(8,128)(2,1)S(1)} %pad_maximum_fusion.1, s32[24576]{0:T(1024)S(1)} %reshape.363), kind=kCustom, calls=%fused_computation.10 | custom fusion | bytes 393216 | tf_op jit(solution)/shard_map/jit(take_along_axis)/gather | solution.py:27
  310.3 0.7 broadcast_select_fusion.4
  311.5 0.8 slice_bitcast_fusion.18
  312.3 0.8 slice_bitcast_fusion.2
  313.0 0.8 gather_fusion.3
  314.9 477.9 %gather_fusion.9 = bf16[49152]{0:T(1024)(128)(2,1)S(1)} fusion(bf16[16,11,1024]{2,1,0:T(8,128)(2,1)S(1)} %pad_maximum_fusion, s32[49152]{0:T(1024)S(1)} %reshape.357), kind=kCustom, calls=%fused_computation.9 | custom fusion | bytes 786432 | tf_op jit(solution)/shard_map/jit(take_along_axis)/gather | solution.py:27
  793.0 0.8 gather_fusion.7
  793.9 0.8 broadcast_select_fusion.2
  795.2 5.0 all-to-all-start.5
  800.2 6.0 gather_fusion.1
  806.2 9.8 fusion.4
  816.0 13.0 %fusion.5 = f32[16,16,1,64]{3,2,1,0:T(1,128)} fusion(bf16[16,16,64,128]{3,2,1,0:T(8,128)(2,1)S(1)} %copy-done.2, f32[16,16,128]{2,1,0:T(8,128)S(1)} %get-tuple-element.22, f32[16,16,64]{2,1,0:T(8,128)S(1)} %get-tuple-element.14, f32[16,16]{1,0:T(8,128)S(1)} %bitcast.266, f32[16,16,128]{2,1,0:T(8,128)S(1)} %copy-done.10, ...), kind=kOutput, calls=%fused_computation.28 | convolution fusion | flops 39845888 | bytes 4720640 | tf_op jit(solution)/shard_map/rhpn,rhn->rhp/dot_general | solution.py:75
  829.1 15.5 %fusion.3 = f32[16,16,1,64]{3,2,1,0:T(1,128)} fusion(bf16[16,16,64,128]{3,2,1,0:T(8,128)(2,1)S(1)} %copy-done.2, f32[16,16,128]{2,1,0:T(8,128)S(1)} %get-tuple-element.21, f32[16,16,64]{2,1,0:T(8,128)S(1)} %get-tuple-element.13, f32[16,16]{1,0:T(8,128)S(1)} %bitcast.259, f32[16,16,128]{2,1,0:T(8,128)S(1)} %get-tuple-element.22, ...), kind=kOutput, calls=%fused_computation.24 | convolution fusion | flops 46137344 | bytes 4918272 | tf_op jit(solution)/shard_map/rhpn,rhn->rhp/dot_general | solution.py:75
  844.6 21.0 %fusion.54 = f32[16,16,1,64]{3,2,1,0:T(1,128)} fusion(bf16[16,16,128,1]{2,1,0,3:T(8,128)(2,1)S(1)} %copy-done.36, bf16[16,16,64,128]{3,2,1,0:T(8,128)(2,1)S(1)} %copy-done.2, f32[16,16,128]{2,1,0:T(8,128)S(1)} %get-tuple-element.20, f32[16,16,64]{2,1,0:T(8,128)S(1)} %get-tuple-element.12, f32[16,16]{1,0:T(8,128)S(1)} %bitcast.253, ...), kind=kOutput, calls=%fused_computation.134 | convolution fusion | flops 52428800 | bytes 5115904 | tf_op jit(solution)/shard_map/rhpn,rhn->rhp/dot_general | solution.py:75
  865.6 23.6 %fusion.2 = f32[16,16,1,64]{3,2,1,0:T(1,128)} fusion(f32[16,16,128]{2,1,0:T(8,128)S(1)} %get-tuple-element.19, f32[16,16,64]{2,1,0:T(8,128)S(1)} %get-tuple-element.11, f32[16,16]{1,0:T(8,128)S(1)} %bitcast.248, bf16[16,16,128,1]{2,1,0,3:T(8,128)(2,1)S(1)} %copy-done.35, bf16[16,16,64,128]{3,2,1,0:T(8,128)(2,1)S(1)} %copy-done.2, ...), kind=kOutput, calls=%fused_computation.21 | convolution fusion | flops 58720256 | bytes 5313536 | tf_op jit(solution)/shard_map/rhpn,rhn->rhp/dot_general | solution.py:75
  889.3 25.9 %fusion.36 = f32[16,16,1,64]{3,2,1,0:T(1,128)} fusion(f32[16,16,128]{2,1,0:T(8,128)S(1)} %get-tuple-element.18, f32[16,16,64]{2,1,0:T(8,128)S(1)} %get-tuple-element.10, f32[16,16]{1,0:T(8,128)S(1)} %bitcast.244, f32[16,16,128]{2,1,0:T(8,128)S(1)} %get-tuple-element.19, f32[16,16,64]{2,1,0:T(8,128)S(1)} %get-tuple-element.11, f32[16,16]{1,0:T(8,128)S(1)} %bitcast.249, ...), kind=kOutput, calls=%fused_computation.61 | convolution fusion | flops 65011712 | bytes 5511168 | tf_op jit(solution)/shard_map/rhpn,rhn->rhp/dot_general | solution.py:75
  915.4 24.1 %select_convert_fusion = bf16[16,16,64,128]{3,2,1,0:T(8,128)(2,1)} fusion(bf16[16,16,64,128]{3,2,1,0:T(8,128)(2,1)S(1)} %copy-done.2, f32[16,16,128]{2,1,0:T(8,128)S(1)} %get-tuple-element.16, f32[16,16,64]{2,1,0:T(8,128)S(1)} %get-tuple-element.8, f32[16,16]{1,0:T(8,128)S(1)} %bitcast.238, f32[16,16,128]{2,1,0:T(8,128)S(1)} %get-tuple-element.17, ...), kind=kLoop, calls=%fused_computation.14 | loop fusion | flops 71303168 | bytes 9969792 | tf_op jit(solution)/shard_map/convert_element_type | solution.py:90
  939.5 6.8 gather_fusion.6
  946.3 6.0 broadcast_select_fusion
  952.6 5.1 all-to-all-start.4
  957.7 1.0 bitcast_dynamic-update-slice_fusion.3
  958.7 6.4 all-to-all-done.4
  965.2 5.2 all-to-all-start.3
  970.7 1.0 bitcast_dynamic-update-slice_fusion.2
  971.6 1.0 bitcast_dynamic-update-slice_fusion.1
  972.8 26.6 %fusion.1 = f32[16,16,1,64]{3,2,1,0:T(1,128)S(1)} fusion(f32[16,16,128]{2,1,0:T(8,128)S(1)} %get-tuple-element.17, f32[16,16,64]{2,1,0:T(8,128)} %copy-done.14, f32[16,16]{1,0:T(8,128)} %bitcast.240, f32[16,16,128]{2,1,0:T(8,128)S(1)} %get-tuple-element.18, f32[16,16,64]{2,1,0:T(8,128)} %copy-done.16, f32[16,16]{1,0:T(8,128)} %bitcast.243, ...), kind=kOutput, calls=%fused_computation.18 | convolution fusion | flops 71303168 | bytes 5708800 | tf_op jit(solution)/shard_map/rhpn,rhn->rhp/dot_general | solution.py:75
  999.7 36.5 %fusion = f32[16,16,1,64]{3,2,1,0:T(1,128)S(1)} fusion(f32[16,16,128]{2,1,0:T(8,128)S(1)} %get-tuple-element.16, f32[16,16,64]{2,1,0:T(8,128)S(1)} %copy-done.13, f32[16,16]{1,0:T(8,128)S(1)} %bitcast.239, f32[16,16,128]{2,1,0:T(8,128)S(1)} %get-tuple-element.17, f32[16,16,64]{2,1,0:T(8,128)S(1)} %copy-done.15, f32[16,16]{1,0:T(8,128)S(1)} %bitcast.242, ...), kind=kOutput, calls=%fused_computation.16 | convolution fusion | flops 77594624 | bytes 5906432 | tf_op jit(solution)/shard_map/rhpn,rhn->rhp/dot_general | solution.py:75
  1037.3 6.0 fusion.40
  1043.4 3.1 scatter_fusion.2
  1046.5 1.6 scatter_fusion.1
  1048.1 27.4 %reduce-scatter.2.cloned.1.call-done = f32[128,1024]{1,0:T(8,128)} async-done(((f32[128,4096]{1,0:T(8,128)}), f32[128,1024]{1,0:T(8,128)}) %reduce-scatter.2.cloned.1.call-update) | async-done | bytes 524304 | tf_op jit(solution)/shard_map/reduce_scatter | solution.py:87
  1075.4 1.9 convert_element_type.66
  1077.3 29.0 %all-to-all-done.3 = bf16[24,16,64,128]{3,2,1,0:T(8,128)(2,1)} async-done(((bf16[24,16,64,128]{3,2,1,0:T(8,128)(2,1)}), bf16[24,16,64,128]{3,2,1,0:T(8,128)(2,1)}, u32[]{:S(2)}, u32[]{:S(2)}) %all-to-all-start.3) | async-done | bytes 6291488 | tf_op jit(solution)/shard_map/all_to_all | solution.py:162
  1106.3 15.3 %scatter_fusion = bf16[18,16,64,128]{3,2,1,0:T(8,128)(2,1)} fusion(bf16[18,16,64,128]{3,2,1,0:T(8,128)(2,1)} %copy.159, s32[24]{0:T(128)S(1)} %copy-done.68, bf16[24,16,64,128]{3,2,1,0:T(8,128)(2,1)} %all-to-all-done.3), kind=kCustom, calls=%fused_computation.11 | custom fusion | bytes 18874464 | tf_op jit(solution)/shard_map/scatter | solution.py:167
  (239 shorter events, 12.4 us)
Async XLA Ops:
  7.2 43.1 %copy-start = (bf16[128,4096]{1,0:T(8,128)(2,1)S(1)}, bf16[128,4096]{1,0:T(8,128)(2,1)}, u32[]{:S(2)}) copy-start(bf16[128,4096]{1,0:T(8,128)(2,1)} %param.17) | copy-start | bytes 3145732
  17.9 14.7 %all-to-all-start.2 = ((bf16[24,3,512]{2,1,0:T(4,128)(2,1)}), bf16[24,3,512]{2,1,0:T(4,128)(2,1)S(1)}, u32[]{:S(2)}, u32[]{:S(2)}) async-start(bf16[24,3,512]{2,1,0:T(4,128)(2,1)} %broadcast_select_fusion.5), calls=%async_computation.2 | async-start | bytes 196608 | tf_op jit(solution)/shard_map/all_to_all | solution.py:151
  32.7 12.4 %all-to-all-start.1 = ((bf16[24,3,1024]{2,1,0:T(4,128)(2,1)}), bf16[24,3,1024]{2,1,0:T(4,128)(2,1)S(1)}, u32[]{:S(2)}, u32[]{:S(2)}) async-start(bf16[24,3,1024]{2,1,0:T(4,128)(2,1)} %broadcast_select_fusion.3), calls=%async_computation.1 | async-start | bytes 393216 | tf_op jit(solution)/shard_map/all_to_all | solution.py:150
  45.1 750.1 %all-to-all-start = ((bf16[24,16,64,128]{3,2,1,0:T(8,128)(2,1)}), bf16[24,16,64,128]{3,2,1,0:T(8,128)(2,1)}, u32[]{:S(2)}, u32[]{:S(2)}) async-start(bf16[24,16,64,128]{3,2,1,0:T(8,128)(2,1)} %broadcast_select_fusion.1), calls=%async_computation | async-start | bytes 12582912 | tf_op jit(solution)/shard_map/all_to_all | solution.py:149
  51.5 258.0 %copy-start.40 = (pred[16,3]{1,0:T(8,128)(4,1)}, pred[16,3]{1,0:T(8,128)(4,1)S(1)}, u32[]{:S(2)}) copy-start(pred[16,3]{1,0:T(8,128)(4,1)S(1)} %fusion.75) | copy-start | bytes 148
  52.3 257.4 %copy-start.69 = (s32[1024]{0:T(1024)}, s32[1024]{0:T(1024)S(1)}, u32[]{:S(2)}) copy-start(s32[1024]{0:T(1024)S(1)} %pad_clamp_fusion) | copy-start | bytes 12292
  52.4 257.9 %copy-start.71 = (pred[24]{0:T(512)(128)(4,1)}, pred[24]{0:T(512)(128)(4,1)S(1)}, u32[]{:S(2)}) copy-start(pred[24]{0:T(512)(128)(4,1)S(1)} %fusion.73) | copy-start | bytes 76
  314.8 478.1 %copy-start.41 = (pred[16,3]{1,0:T(8,128)(4,1)S(1)}, pred[16,3]{1,0:T(8,128)(4,1)}, u32[]{:S(2)}) copy-start(pred[16,3]{1,0:T(8,128)(4,1)} %copy-done.40) | copy-start | bytes 148
  314.8 479.1 %copy-start.72 = (pred[24]{0:T(512)(128)(4,1)S(1)}, pred[24]{0:T(512)(128)(4,1)}, u32[]{:S(2)}) copy-start(pred[24]{0:T(512)(128)(4,1)} %copy-done.71) | copy-start | bytes 76
  314.8 479.9 %copy-start.58 = (f32[16,1,16]{2,1,0:T(1,128)S(1)}, f32[16,1,16]{2,1,0:T(1,128)}, u32[]{:S(2)}) copy-start(f32[16,1,16]{2,1,0:T(1,128)} %get-tuple-element.42) | copy-start | bytes 3076
  314.8 479.9 %copy-start.59 = (f32[16,1,16]{2,1,0:T(1,128)S(1)}, f32[16,1,16]{2,1,0:T(1,128)}, u32[]{:S(2)}) copy-start(f32[16,1,16]{2,1,0:T(1,128)} %get-tuple-element.43) | copy-start | bytes 3076
  314.8 479.9 %copy-start.60 = (f32[16,1,16]{2,1,0:T(1,128)S(1)}, f32[16,1,16]{2,1,0:T(1,128)}, u32[]{:S(2)}) copy-start(f32[16,1,16]{2,1,0:T(1,128)} %get-tuple-element.44) | copy-start | bytes 3076
  314.8 479.9 %copy-start.61 = (f32[16,1,16]{2,1,0:T(1,128)S(1)}, f32[16,1,16]{2,1,0:T(1,128)}, u32[]{:S(2)}) copy-start(f32[16,1,16]{2,1,0:T(1,128)} %get-tuple-element.45) | copy-start | bytes 3076
  314.8 479.9 %copy-start.62 = (f32[16,1,16]{2,1,0:T(1,128)S(1)}, f32[16,1,16]{2,1,0:T(1,128)}, u32[]{:S(2)}) copy-start(f32[16,1,16]{2,1,0:T(1,128)} %get-tuple-element.46) | copy-start | bytes 3076
  314.8 479.9 %copy-start.63 = (f32[16,1,16]{2,1,0:T(1,128)S(1)}, f32[16,1,16]{2,1,0:T(1,128)}, u32[]{:S(2)}) copy-start(f32[16,1,16]{2,1,0:T(1,128)} %get-tuple-element.47) | copy-start | bytes 3076
  314.8 479.9 %copy-start.64 = (f32[16,1,16]{2,1,0:T(1,128)S(1)}, f32[16,1,16]{2,1,0:T(1,128)}, u32[]{:S(2)}) copy-start(f32[16,1,16]{2,1,0:T(1,128)} %get-tuple-element.48) | copy-start | bytes 3076
  314.8 479.9 %copy-start.65 = (f32[16,1,16]{2,1,0:T(1,128)S(1)}, f32[16,1,16]{2,1,0:T(1,128)}, u32[]{:S(2)}) copy-start(f32[16,1,16]{2,1,0:T(1,128)} %get-tuple-element.49) | copy-start | bytes 3076
  795.1 120.1 %copy-start.12 = (f32[16,16,64]{2,1,0:T(8,128)}, f32[16,16,64]{2,1,0:T(8,128)S(1)}, u32[]{:S(2)}) copy-start(f32[16,16,64]{2,1,0:T(8,128)S(1)} %get-tuple-element.8) | copy-start | bytes 196612
  795.1 120.1 %copy-start.14 = (f32[16,16,64]{2,1,0:T(8,128)}, f32[16,16,64]{2,1,0:T(8,128)S(1)}, u32[]{:S(2)}) copy-start(f32[16,16,64]{2,1,0:T(8,128)S(1)} %get-tuple-element.9) | copy-start | bytes 196612
  795.1 120.1 %copy-start.16 = (f32[16,16,64]{2,1,0:T(8,128)}, f32[16,16,64]{2,1,0:T(8,128)S(1)}, u32[]{:S(2)}) copy-start(f32[16,16,64]{2,1,0:T(8,128)S(1)} %get-tuple-element.10) | copy-start | bytes 196612
  795.1 120.1 %copy-start.18 = (f32[16,16,64]{2,1,0:T(8,128)}, f32[16,16,64]{2,1,0:T(8,128)S(1)}, u32[]{:S(2)}) copy-start(f32[16,16,64]{2,1,0:T(8,128)S(1)} %get-tuple-element.11) | copy-start | bytes 196612
  795.2 120.1 %copy-start.20 = (f32[16,16,64]{2,1,0:T(8,128)}, f32[16,16,64]{2,1,0:T(8,128)S(1)}, u32[]{:S(2)}) copy-start(f32[16,16,64]{2,1,0:T(8,128)S(1)} %get-tuple-element.12) | copy-start | bytes 196612
  795.2 120.1 %copy-start.22 = (f32[16,16,64]{2,1,0:T(8,128)}, f32[16,16,64]{2,1,0:T(8,128)S(1)}, u32[]{:S(2)}) copy-start(f32[16,16,64]{2,1,0:T(8,128)S(1)} %get-tuple-element.13) | copy-start | bytes 196612
  795.2 120.1 %copy-start.24 = (f32[16,16,64]{2,1,0:T(8,128)}, f32[16,16,64]{2,1,0:T(8,128)S(1)}, u32[]{:S(2)}) copy-start(f32[16,16,64]{2,1,0:T(8,128)S(1)} %get-tuple-element.14) | copy-start | bytes 196612
  795.2 120.1 %copy-start.26 = (f32[16,16,64]{2,1,0:T(8,128)}, f32[16,16,64]{2,1,0:T(8,128)S(1)}, u32[]{:S(2)}) copy-start(f32[16,16,64]{2,1,0:T(8,128)S(1)} %get-tuple-element.15) | copy-start | bytes 196612
  795.2 157.4 %all-to-all-start.5 = ((bf16[24,3,512]{2,1,0:T(4,128)(2,1)}), bf16[24,3,512]{2,1,0:T(4,128)(2,1)}, u32[]{:S(2)}, u32[]{:S(2)}) async-start(bf16[24,3,512]{2,1,0:T(4,128)(2,1)} %broadcast_select_fusion.4), calls=%async_computation.6 | async-start | bytes 196608 | tf_op jit(solution)/shard_map/all_to_all | solution.py:164
  952.6 12.5 %all-to-all-start.4 = ((bf16[24,3,1024]{2,1,0:T(4,128)(2,1)}), bf16[24,3,1024]{2,1,0:T(4,128)(2,1)S(1)}, u32[]{:S(2)}, u32[]{:S(2)}) async-start(bf16[24,3,1024]{2,1,0:T(4,128)(2,1)} %broadcast_select_fusion.2), calls=%async_computation.5 | async-start | bytes 393216 | tf_op jit(solution)/shard_map/all_to_all | solution.py:163
  965.2 141.1 %all-to-all-start.3 = ((bf16[24,16,64,128]{3,2,1,0:T(8,128)(2,1)}), bf16[24,16,64,128]{3,2,1,0:T(8,128)(2,1)}, u32[]{:S(2)}, u32[]{:S(2)}) async-start(bf16[24,16,64,128]{3,2,1,0:T(8,128)(2,1)} %broadcast_select_fusion), calls=%async_computation.4 | async-start | bytes 12582912 | tf_op jit(solution)/shard_map/all_to_all | solution.py:162
  970.4 105.0 %reduce-scatter.2.cloned.1.call-start = ((), (), s32[]{:S(2)}) async-start(), calls=%async_computation.7 | async-start | bytes 2621440 | tf_op jit(solution)/shard_map/reduce_scatter | solution.py:87
  972.7 26.9 %copy-start.3 = (bf16[16,16,64,128]{3,2,1,0:T(8,128)(2,1)S(1)}, bf16[16,16,64,128]{3,2,1,0:T(8,128)(2,1)}, u32[]{:S(2)}) copy-start(bf16[16,16,64,128]{3,2,1,0:T(8,128)(2,1)} %gather_fusion.1) | copy-start | bytes 12582916
  972.7 26.9 %copy-start.13 = (f32[16,16,64]{2,1,0:T(8,128)S(1)}, f32[16,16,64]{2,1,0:T(8,128)}, u32[]{:S(2)}) copy-start(f32[16,16,64]{2,1,0:T(8,128)} %copy-done.12) | copy-start | bytes 196612
  972.7 26.9 %copy-start.15 = (f32[16,16,64]{2,1,0:T(8,128)S(1)}, f32[16,16,64]{2,1,0:T(8,128)}, u32[]{:S(2)}) copy-start(f32[16,16,64]{2,1,0:T(8,128)} %copy-done.14) | copy-start | bytes 196612
  972.7 26.9 %copy-start.17 = (f32[16,16,64]{2,1,0:T(8,128)S(1)}, f32[16,16,64]{2,1,0:T(8,128)}, u32[]{:S(2)}) copy-start(f32[16,16,64]{2,1,0:T(8,128)} %copy-done.16) | copy-start | bytes 196612
  972.7 26.9 %copy-start.19 = (f32[16,16,64]{2,1,0:T(8,128)S(1)}, f32[16,16,64]{2,1,0:T(8,128)}, u32[]{:S(2)}) copy-start(f32[16,16,64]{2,1,0:T(8,128)} %copy-done.18) | copy-start | bytes 196612
  972.7 26.9 %copy-start.21 = (f32[16,16,64]{2,1,0:T(8,128)S(1)}, f32[16,16,64]{2,1,0:T(8,128)}, u32[]{:S(2)}) copy-start(f32[16,16,64]{2,1,0:T(8,128)} %copy-done.20) | copy-start | bytes 196612
  972.7 26.9 %copy-start.23 = (f32[16,16,64]{2,1,0:T(8,128)S(1)}, f32[16,16,64]{2,1,0:T(8,128)}, u32[]{:S(2)}) copy-start(f32[16,16,64]{2,1,0:T(8,128)} %copy-done.22) | copy-start | bytes 196612
  972.7 26.9 %copy-start.25 = (f32[16,16,64]{2,1,0:T(8,128)S(1)}, f32[16,16,64]{2,1,0:T(8,128)}, u32[]{:S(2)}) copy-start(f32[16,16,64]{2,1,0:T(8,128)} %copy-done.24) | copy-start | bytes 196612
  972.7 26.9 %copy-start.27 = (f32[16,16,64]{2,1,0:T(8,128)S(1)}, f32[16,16,64]{2,1,0:T(8,128)}, u32[]{:S(2)}) copy-start(f32[16,16,64]{2,1,0:T(8,128)} %copy-done.26) | copy-start | bytes 196612
  972.7 26.9 %copy-start.45 = (f32[16,1,16]{2,1,0:T(1,128)S(1)}, f32[16,1,16]{2,1,0:T(1,128)}, u32[]{:S(2)}) copy-start(f32[16,1,16]{2,1,0:T(1,128)} %get-tuple-element.35) | copy-start | bytes 3076
  972.8 26.9 %copy-start.47 = (f32[16,1,16]{2,1,0:T(1,128)S(1)}, f32[16,1,16]{2,1,0:T(1,128)}, u32[]{:S(2)}) copy-start(f32[16,1,16]{2,1,0:T(1,128)} %get-tuple-element.36) | copy-start | bytes 3076
  972.8 26.9 %copy-start.49 = (f32[16,1,16]{2,1,0:T(1,128)S(1)}, f32[16,1,16]{2,1,0:T(1,128)}, u32[]{:S(2)}) copy-start(f32[16,1,16]{2,1,0:T(1,128)} %get-tuple-element.37) | copy-start | bytes 3076
  972.8 26.9 %copy-start.51 = (f32[16,1,16]{2,1,0:T(1,128)S(1)}, f32[16,1,16]{2,1,0:T(1,128)}, u32[]{:S(2)}) copy-start(f32[16,1,16]{2,1,0:T(1,128)} %get-tuple-element.38) | copy-start | bytes 3076
  972.8 26.9 %copy-start.53 = (f32[16,1,16]{2,1,0:T(1,128)S(1)}, f32[16,1,16]{2,1,0:T(1,128)}, u32[]{:S(2)}) copy-start(f32[16,1,16]{2,1,0:T(1,128)} %get-tuple-element.39) | copy-start | bytes 3076
  972.8 26.9 %copy-start.55 = (f32[16,1,16]{2,1,0:T(1,128)S(1)}, f32[16,1,16]{2,1,0:T(1,128)}, u32[]{:S(2)}) copy-start(f32[16,1,16]{2,1,0:T(1,128)} %get-tuple-element.40) | copy-start | bytes 3076
  999.7 37.6 %copy-start.32 = (f32[1024]{0:T(1024)S(1)}, f32[1024]{0:T(1024)}, u32[]{:S(2)}) copy-start(f32[1024]{0:T(1024)} %param.26) | copy-start | bytes 12292
  1046.5 75.1 %copy-start.9 = (bf16[18,3,512]{2,1,0:T(4,128)(2,1)}, bf16[18,3,512]{2,1,0:T(4,128)(2,1)S(1)}, u32[]{:S(2)}) copy-start(bf16[18,3,512]{2,1,0:T(4,128)(2,1)S(1)} %scatter_fusion.2) | copy-start | bytes 165892
  1048.0 73.5 %copy-start.6 = (bf16[18,3,1024]{2,1,0:T(4,128)(2,1)}, bf16[18,3,1024]{2,1,0:T(4,128)(2,1)S(1)}, u32[]{:S(2)}) copy-start(bf16[18,3,1024]{2,1,0:T(4,128)(2,1)S(1)} %scatter_fusion.1) | copy-start | bytes 331780
  1075.4 46.2 %copy-start.1 = (bf16[128,4096]{1,0:T(8,128)(2,1)S(1)}, bf16[128,4096]{1,0:T(8,128)(2,1)}, u32[]{:S(2)}) copy-start(bf16[128,4096]{1,0:T(8,128)(2,1)} %param.17) | copy-start | bytes 3145732
  (45 other events, 722.2 us)
Sparse Core Ops, SparseCore 0:
  1043.5 31.9 reduce-scatter.1
where the time goes:
time: 1130 us
  local copies, waits for them, and re-layouts  774 us (68%)
  matrix products  186 us (16%)
  waiting for transfers between devices  64 us (6%)
  other arithmetic  49.8 us (4%)
  starting transfers between devices  32.2 us (3%)
  between operations  15.5 us (1%)
    gather x6, local copies, waits for them, and re-layouts, conv_part(): kept_rows = jnp.take_along_axis(joined, picks, axis=1)  717 us
    dot_general x8, matrix products, verify(): jnp.einsum('rhpn,rhn->rhp', carried, c_heads[:, position], precision=lax....  172 us
    all_to_all x1, waiting for transfers between devices, body(): lax.all_to_all(going_home[0], 'pool', split_axis=0, concat_axis=0, tiled=...  29 us
    reduce_scatter x1, waiting for transfers between devices, verify(): lax.psum_scatter(partial_value, 'tensor', scatter_dimension=1, tiled=True)  27.4 us
    convert_element_type x1, other arithmetic, verify(): return (mixed, kept_state.astype(jnp.bfloat16), kept_x, kept_bc)  24.1 us
  transfers between devices with their start and end apart: 7, of which 4 were waited for; matrix products, arithmetic and copies ran while one was open for 87% of the time, Pallas kernels for 0%

commit v1 on v0

v1 whole, which is shorter than its diff:
```python
import functools

import jax
import jax.numpy as jnp
from jax import lax
from jax.experimental import pallas as pl
from jax.experimental.pallas import tpu as pltpu
from jax.sharding import PartitionSpec as P

HEADS = 64
HEAD_DIM = 64
STATE = 128
GROUPS = 8
DRAFT = 8
SHIFT = 3
EPS = 1e-05
FAR = 4096.0

F32 = jnp.float32
BF16 = jnp.bfloat16
ANY = pl.BlockSpec(memory_space=pl.ANY)
VMEM = pl.BlockSpec(memory_space=pltpu.VMEM)
SMEM = pl.BlockSpec(memory_space=pltpu.SMEM)


def params(mib, **more):
    return pltpu.CompilerParams(vmem_limit_bytes=mib * 2**20, **more)


def cost(flops, moved):
    return pl.CostEstimate(flops=int(flops), bytes_accessed=int(moved), transcendentals=0)


def iota(shape, dim):
    return lax.broadcasted_iota(jnp.int32, shape, dim)


def dot(a, b):
    return jnp.dot(a, b, preferred_element_type=F32)


def dot_t(a, b):
    return lax.dot_general(a, b, (((1,), (1,)), ((), ())), preferred_element_type=F32)


def as_col(row):
    n = row.shape[1]
    eye = iota((n, n), 0) == iota((n, n), 1)
    return jnp.sum(jnp.where(eye, jnp.broadcast_to(row, (n, n)), 0.0), axis=1, keepdims=True)


def wrap(value, n):
    return jnp.where(value < 0, value + n, value)


def block_shift(req):
    return req.bit_length() - 1


def ranks(orow, ocol, req):
    n = orow.shape[1]
    sub, lane = iota((n, n), 0), iota((n, n), 1)
    sh = block_shift(req)
    same = (ocol == orow) & ((sub >> sh) == (lane >> sh))
    row = jnp.sum(jnp.where(same & (sub < lane), 1.0, 0.0), axis=0, keepdims=True)
    col = jnp.sum(jnp.where(same & (lane < sub), 1.0, 0.0), axis=1, keepdims=True)
    return row, col


def hot(mask):
    return jnp.where(mask, 1.0, 0.0).astype(BF16)


def send_matrix(orow, me, n_pool, req, cr):
    ocol = as_col(orow)
    _, rank_col = ranks(orow, ocol, req)
    total, tokens = orow.shape[1], req * DRAFT
    place_col = wrap(ocol - me.astype(F32), n_pool) * cr + rank_col * DRAFT
    token = iota((total, tokens), 1)
    mine = (iota((total, tokens), 0) - me * req) == (token >> SHIFT)
    place = jnp.sum(jnp.where(mine, jnp.broadcast_to(place_col, (total, tokens)), 0.0), axis=0, keepdims=True)
    place = place + (iota((1, tokens), 1) & (DRAFT - 1)).astype(F32)
    return hot(iota((n_pool * cr, tokens), 0).astype(F32) == place)


def collect_matrix(orow, me, n_pool, req, cr):
    ocol = as_col(orow)
    rank_row, _ = ranks(orow, ocol, req)
    total, tokens = orow.shape[1], req * DRAFT
    place_row = wrap(orow - me.astype(F32), n_pool) * cr + rank_row * DRAFT
    token = iota((tokens, total), 0)
    mine = (iota((tokens, total), 1) - me * req) == (token >> SHIFT)
    place = jnp.sum(jnp.where(mine, jnp.broadcast_to(place_row, (tokens, total)), 0.0), axis=1, keepdims=True)
    place = place + (iota((tokens, 1), 0) & (DRAFT - 1)).astype(F32)
    return hot(iota((tokens, n_pool * cr), 1).astype(F32) == place)


def owner_matrix(orow, srow, me, n_pool, req, cr, slots):
    ocol = as_col(orow)
    rank_row, _ = ranks(orow, ocol, req)
    total, rows = orow.shape[1], slots * DRAFT
    block = (iota((1, total), 1) >> block_shift(req)).astype(F32)
    place_row = wrap(me.astype(F32) - block, n_pool) * cr + rank_row * DRAFT + FAR
    slot = (iota((rows, total), 0) >> SHIFT).astype(F32)
    match = (orow == me.astype(F32)) & (srow == slot)
    place = jnp.sum(jnp.where(match, jnp.broadcast_to(place_row, (rows, total)), 0.0), axis=1, keepdims=True)
    place = place - FAR + (iota((rows, 1), 0) & (DRAFT - 1)).astype(F32)
    return hot(iota((rows, n_pool * cr), 1).astype(F32) == place)


def return_matrix(orow, srow, me, n_pool, req, cr, slots):
    ocol, scol = as_col(orow), as_col(srow)
    _, rank_col = ranks(orow, ocol, req)
    total, rows = orow.shape[1], slots * DRAFT
    block = (iota((total, 1), 0) >> block_shift(req)).astype(F32)
    place_col = wrap(me.astype(F32) - block, n_pool) * cr + rank_col * DRAFT + FAR
    slot = (iota((total, rows), 1) >> SHIFT).astype(F32)
    match = (ocol == me.astype(F32)) & (scol == slot)
    place = jnp.sum(jnp.where(match, jnp.broadcast_to(place_col, (total, rows)), 0.0), axis=0, keepdims=True)
    place = place - FAR + (iota((1, rows), 1) & (DRAFT - 1)).astype(F32)
    return hot(iota((n_pool * cr, rows), 0).astype(F32) == place)


def slot_accepts(orow, srow, arow, me, slots):
    total, rows = orow.shape[1], slots * DRAFT
    slot = (iota((rows, total), 0) >> SHIFT).astype(F32)
    match = (orow == me.astype(F32)) & (srow == slot)
    return jnp.sum(jnp.where(match, jnp.broadcast_to(arow, (rows, total)), 0.0), axis=1, keepdims=True)


def conv_slots(raw, pool, weight, accepts):
    rows, width = raw.shape
    slots = rows // DRAFT
    window = pool.shape[1]
    old = jnp.concatenate(
        [pool.astype(F32), jnp.zeros((slots, DRAFT - window, width), F32)], axis=1
    ).reshape(rows, width)
    position = iota((rows, width), 0) & (DRAFT - 1)
    summed = weight[window] * raw
    for back in range(1, window + 1):
        new_part = pltpu.roll(raw, back, 0)
        old_part = pltpu.roll(old, (back - window) % rows, 0)
        summed = summed + weight[window - back] * jnp.where(position < back, old_part, new_part)
    sub, lane = iota((rows, rows), 0), iota((rows, rows), 1)
    here = (sub >> SHIFT) == (lane >> SHIFT)
    at = (sub & (DRAFT - 1)).astype(F32) + accepts
    source = (lane & (DRAFT - 1)).astype(F32)
    from_old = hot(here & (source == at) & (source < window))
    from_new = hot(here & (source + window == at))
    kept = dot(from_old, old.astype(BF16)) + dot(from_new, raw.astype(BF16))
    return summed, kept.astype(BF16).reshape(slots, DRAFT, width)[:, :window]


def silu(v):
    return v / (1.0 + jnp.exp(-v))


def spread_matrix(heads):
    shape = (heads, heads * HEAD_DIM)
    return hot(iota(shape, 0) == (iota(shape, 1) >> 6))


def spread(values, matrix):
    high = values.astype(BF16)
    low = (values - high.astype(F32)).astype(BF16)
    return dot(high, matrix) + dot(low, matrix)


def project_kernel(n_pool, req, cr, chunk, with_dt, *refs):
    me_ref, orow_ref, hidden, w = refs[:4]
    refs = refs[4:]
    if with_dt:
        w_dt, refs = refs[0], refs[1:]
    outs, refs = refs[:n_pool], refs[n_pool:]
    hbuf, wbuf, sems = refs[:3]
    steps = hidden.shape[1] // chunk
    copies = []
    for k in range(steps):
        part = pl.ds(k * chunk, chunk)
        copies.append(
            [
                pltpu.make_async_copy(hidden.at[:, part], hbuf.at[:, part], sems.at[0, k]),
                pltpu.make_async_copy(w.at[part], wbuf.at[part], sems.at[1, k]),
            ]
        )
        if with_dt:
            copies[-1].append(pltpu.make_async_copy(w_dt.at[part], refs[3].at[part], sems.at[2, k]))
        for copy in copies[-1]:
            copy.start()
    order = send_matrix(orow_ref[...].astype(F32), me_ref[0], n_pool, req, cr)
    total = jnp.zeros((hidden.shape[0], w.shape[1]), F32)
    if with_dt:
        total_dt = jnp.zeros((hidden.shape[0], w_dt.shape[1]), F32)
    for k in range(steps):
        for copy in copies[k]:
            copy.wait()
        rows = hbuf[:, k * chunk : (k + 1) * chunk]
        total = total + dot(rows, wbuf[k * chunk : (k + 1) * chunk])
        if with_dt:
            total_dt = total_dt + dot(rows, refs[3][k * chunk : (k + 1) * chunk])
    width = w.shape[1]
    placed = dot(order, total.astype(BF16)).astype(BF16)
    for s in range(n_pool):
        outs[s][:, :width] = placed[s * cr : (s + 1) * cr]
    if with_dt:
        heads = w_dt.shape[1]
        high = total_dt.astype(BF16)
        low = (total_dt - high.astype(F32)).astype(BF16)
        shape = (heads, 128)
        to_high = hot(iota(shape, 0) == iota(shape, 1))
        to_low = hot(iota(shape, 0) + heads == iota(shape, 1))
        pair = (dot(high, to_high) + dot(low, to_low)).astype(BF16)
        placed = dot(order, pair).astype(BF16)
        for s in range(n_pool):
            outs[s][:, width:] = placed[s * cr : (s + 1) * cr]


def project(me, orow, hidden, w, w_dt, n_pool, req, cr):
    tokens, depth = hidden.shape
    width = w.shape[1]
    chunk = min(512, depth)
    with_dt = w_dt is not None
    extra = 128 if with_dt else 0
    scratch = [
        pltpu.VMEM((tokens, depth), BF16),
        pltpu.VMEM((depth, width), BF16),
        pltpu.SemaphoreType.DMA((3, depth // chunk)),
    ]
    if with_dt:
        scratch.append(pltpu.VMEM((depth, w_dt.shape[1]), BF16))
    operands = [me, orow, hidden, w] + ([w_dt] if with_dt else [])
    return pl.pallas_call(
        functools.partial(project_kernel, n_pool, req, cr, chunk, with_dt),
        out_shape=[jax.ShapeDtypeStruct((cr, width + extra), BF16)] * n_pool,
        in_specs=[SMEM, VMEM, ANY, ANY] + ([ANY] if with_dt else []),
        out_specs=[VMEM] * n_pool,
        scratch_shapes=scratch,
        compiler_params=params(32),
        cost_estimate=cost(2 * tokens * depth * width, depth * (width + extra) * 2 + tokens * depth * 2),
    )(*operands)


def bc_kernel(n_pool, req, cr, me_ref, orow_ref, srow_ref, arow_ref, *refs):
    got, refs = refs[:n_pool], refs[n_pool:]
    pool_ref, weight_ref, act_ref, dt_ref, kept_ref = refs
    slots, _, width = pool_ref.shape
    me = me_ref[0]
    orow, srow, arow = (r[...].astype(F32) for r in (orow_ref, srow_ref, arow_ref))
    order = owner_matrix(orow, srow, me, n_pool, req, cr, slots)
    accepts = slot_accepts(orow, srow, arow, me, slots)
    raw = dot(order, jnp.concatenate([g[...] for g in got], axis=0))
    heads = dt_ref.shape[1]
    shape = (128, heads)
    lane = iota(shape, 0)
    head = iota(shape, 1)
    both = hot((lane == head) | (lane == head + heads))
    dt_ref[...] = dot(raw[:, width:].astype(BF16), both)
    summed, kept = conv_slots(raw[:, :width], pool_ref[...], weight_ref[...], accepts)
    kept_ref[...] = kept
    act_ref[...] = silu(summed).astype(BF16)


def bc_stage(me, orow, srow, arow, got, pool, weight, heads, n_pool, req, cr):
    slots, _, width = pool.shape
    rows = slots * DRAFT
    return pl.pallas_call(
        functools.partial(bc_kernel, n_pool, req, cr),
        out_shape=[
            jax.ShapeDtypeStruct((rows, width), BF16),
            jax.ShapeDtypeStruct((rows, heads), F32),
            jax.ShapeDtypeStruct(pool.shape, BF16),
        ],
        in_specs=[SMEM] + [VMEM] * (n_pool + 5),
        out_specs=[VMEM] * 3,
        compiler_params=params(24),
        cost_estimate=cost(2e6, 1e6),
    )(me, orow, srow, arow, *got, pool, weight)


def exchange_plan(n_tensor, width, span):
    piece = span * STATE
    per_group = HEADS // GROUPS
    head_local = HEADS // n_tensor
    edges, own = [], []
    for target in range(n_tensor):
        first = target * head_local // per_group
        for kind in range(2):
            column = (kind * GROUPS + first) * STATE
            source, part = column // width, column % width // piece
            (own if source == target else edges).append((source, target, kind, part))
    rounds = []
    for edge in edges:
        for one in rounds:
            if all(edge[0] != e[0] and edge[1] != e[1] for e in one):
                one.append(edge)
                break
        else:
            rounds.append([edge])
    return rounds, own


def exchange(act, n_tensor, span, rank):
    width = act.shape[1]
    piece = span * STATE
    rounds, own = exchange_plan(n_tensor, width, span)
    sides = [jnp.zeros((act.shape[0], piece), act.dtype)] * 2

    def part_of(table):
        offset = jnp.asarray(table, jnp.int32)[rank] * piece
        return lax.dynamic_slice_in_dim(act, offset, piece, axis=1)

    for kind in range(2):
        table, there = [0] * n_tensor, [False] * n_tensor
        for source, target, k, part in own:
            if k == kind:
                table[target], there[target] = part, True
        if any(there):
            sides[kind] = jnp.where(jnp.asarray(there)[rank], part_of(table), sides[kind])
    for one in rounds:
        table = [0] * n_tensor
        kinds = [-1] * n_tensor
        for source, target, kind, part in one:
            table[source], kinds[target] = part, kind
        moved = lax.ppermute(part_of(table), "tensor", [(e[0], e[1]) for e in one])
        got = jnp.asarray(kinds, jnp.int32)[rank]
        for kind in range(2):
            sides[kind] = jnp.where(got == kind, moved, sides[kind])
    return sides


def mix_kernel(
    me_ref, orow_ref, srow_ref, arow_ref, b_ref, c_ref, dt_ref, bias_ref, alog_ref, pool, y_ref, m_ref, w_ref, d_ref, buf, sems
):
    slots, heads = pool.shape[:2]
    rows = slots * DRAFT
    span = b_ref.shape[1] // STATE
    per = heads // span
    copies = [pltpu.make_async_copy(pool.at[j], buf.at[j], sems.at[j]) for j in range(slots)]
    for copy in copies:
        copy.start()
    orow, srow, arow = (r[...].astype(F32) for r in (orow_ref, srow_ref, arow_ref))
    accepts = slot_accepts(orow, srow, arow, me_ref[0], slots)
    x = dt_ref[...] + bias_ref[...]
    step = jnp.maximum(x, 0.0) + jnp.log1p(jnp.exp(-jnp.abs(x)))
    logs = -step * jnp.exp(alog_ref[...])
    position = iota((rows, heads), 0) & (DRAFT - 1)
    for back in (1, 2, 4):
        logs = logs + jnp.where(position >= back, pltpu.roll(logs, back, 0), 0.0)
    last = jnp.where(position.astype(F32) + 1 == accepts, logs, 0.0).reshape(slots, DRAFT, heads)
    last = jnp.broadcast_to(jnp.sum(last, axis=1, keepdims=True), (slots, DRAFT, heads))
    d_ref[...] = jnp.exp(last[:, 0, :])
    last = last.reshape(rows, heads)
    w_ref[...] = jnp.where(position.astype(F32) < accepts, jnp.exp(jnp.minimum(last - logs, 0.0)) * step, 0.0)
    eye = jnp.where(iota((rows, rows), 0) == iota((rows, rows), 1), 1.0, 0.0)

    def turned(v):
        return lax.dot_general(
            v, eye, (((0,), (0,)), ((), ())), preferred_element_type=F32, precision=lax.Precision.HIGHEST
        )

    logs_t, step_t = turned(logs), turned(step)
    sub, lane = iota((rows, rows), 0), iota((rows, rows), 1)
    causal = ((sub >> SHIFT) == (lane >> SHIFT)) & (lane <= sub)
    for g in range(span):
        part = slice(g * STATE, (g + 1) * STATE)
        pair = jnp.where(causal, dot_t(c_ref[:, part], b_ref[:, part]), 0.0)
        for h in range(g * per, (g + 1) * per):
            fade = jnp.exp(jnp.minimum(logs[:, h : h + 1] - logs_t[h : h + 1], 0.0))
            m_ref[h] = (pair * fade * step_t[h : h + 1]).astype(BF16)
    fade = spread(jnp.exp(logs), spread_matrix(heads))
    c = c_ref[...].astype(F32)
    for j in range(slots):
        copies[j].wait()
        here = slice(j * DRAFT, (j + 1) * DRAFT)
        for g in range(span):
            states = buf[j, g * per : (g + 1) * per].reshape(per * HEAD_DIM, STATE)
            columns = slice(g * per * HEAD_DIM, (g + 1) * per * HEAD_DIM)
            read = dot_t(c[here, g * STATE : (g + 1) * STATE].astype(BF16), states)
            y_ref[here, columns] = read * fade[here, columns]


def mix_stage(me, orow, srow, arow, b, c, dt, bias, a_log, pool):
    slots, heads = pool.shape[:2]
    rows = slots * DRAFT
    return pl.pallas_call(
        mix_kernel,
        out_shape=[
            jax.ShapeDtypeStruct((rows, heads * HEAD_DIM), F32),
            jax.ShapeDtypeStruct((heads, rows, rows), BF16),
            jax.ShapeDtypeStruct((rows, heads), F32),
            jax.ShapeDtypeStruct((slots, heads), F32),
        ],
        in_specs=[SMEM] + [VMEM] * 8 + [ANY],
        out_specs=[VMEM] * 4,
        scratch_shapes=[pltpu.VMEM(pool.shape, BF16), pltpu.SemaphoreType.DMA((slots,))],
        compiler_params=params(32),
        cost_estimate=cost(2 * rows * heads * HEAD_DIM * STATE, 2 * pool.size),
    )(me, orow, srow, arow, b, c, dt, bias, a_log, pool)


def x_kernel(n_pool, req, cr, me_ref, orow_ref, srow_ref, arow_ref, *refs):
    got, refs = refs[:n_pool], refs[n_pool:]
    pool_ref, weight_ref, y_ref, m_ref, skip_ref, gain_ref = refs[:6]
    outs, (x_ref, kept_ref) = refs[6 : 6 + n_pool], refs[6 + n_pool :]
    slots, _, width = pool_ref.shape
    heads = width // HEAD_DIM
    me = me_ref[0]
    orow, srow, arow = (r[...].astype(F32) for r in (orow_ref, srow_ref, arow_ref))
    order = owner_matrix(orow, srow, me, n_pool, req, cr, slots)
    accepts = slot_accepts(orow, srow, arow, me, slots)
    raw = dot(order, jnp.concatenate([g[...] for g in got], axis=0))
    summed, kept = conv_slots(raw, pool_ref[...], weight_ref[...], accepts)
    kept_ref[...] = kept
    x = silu(summed)
    x_ref[...] = x
    matrix = spread_matrix(heads)
    small = x.astype(BF16)
    parts = [dot(m_ref[h], small[:, h * HEAD_DIM : (h + 1) * HEAD_DIM]) for h in range(heads)]
    y = jnp.concatenate(parts, axis=1) + y_ref[...] + spread(skip_ref[...], matrix) * x
    square = (y * y).astype(BF16)
    scale = lax.rsqrt(dot_t(square, matrix) * (1.0 / HEAD_DIM) + EPS)
    normed = (y * spread(scale, matrix) * gain_ref[...]).astype(BF16)
    back = return_matrix(orow, srow, me, n_pool, req, cr, slots)
    placed = dot(back, normed).astype(BF16)
    for s in range(n_pool):
        outs[s][...] = placed[s * cr : (s + 1) * cr]


def x_stage(me, orow, srow, arow, got, pool, weight, y, m, skip, gain, n_pool, req, cr):
    slots, _, width = pool.shape
    rows = slots * DRAFT
    return pl.pallas_call(
        functools.partial(x_kernel, n_pool, req, cr),
        out_shape=[jax.ShapeDtypeStruct((cr, width), BF16)] * n_pool
        + [jax.ShapeDtypeStruct((rows, width), F32), jax.ShapeDtypeStruct(pool.shape, BF16)],
        in_specs=[SMEM] + [VMEM] * (n_pool + 9),
        out_specs=[VMEM] * (n_pool + 2),
        compiler_params=params(32),
        cost_estimate=cost(2 * rows * rows * width, 4e6),
    )(me, orow, srow, arow, *got, pool, weight, y, m, skip, gain)


def state_kernel(d_ref, x_ref, w_ref, b_ref, pool, new_pool, buf, sems, out_sems):
    slots, heads = pool.shape[:2]
    rows = slots * DRAFT
    span = b_ref.shape[1] // STATE
    per = heads // span
    copies = [pltpu.make_async_copy(pool.at[j], buf.at[j], sems.at[j]) for j in range(slots)]
    backs = [pltpu.make_async_copy(buf.at[j], new_pool.at[j], out_sems.at[j]) for j in range(slots)]
    for copy in copies:
        copy.start()
    weighted = x_ref[...] * spread(w_ref[...], spread_matrix(heads))
    turned = weighted.T
    high = turned.astype(BF16)
    b = b_ref[...]
    slot = iota((rows, STATE), 0) >> SHIFT
    for j in range(slots):
        copies[j].wait()
        for g in range(span):
            rhs = jnp.where(slot == j, b[:, g * STATE : (g + 1) * STATE].astype(F32), 0.0).astype(BF16)
            added = dot(high[g * per * HEAD_DIM : (g + 1) * per * HEAD_DIM], rhs)
            for i in range(per):
                h = g * per + i
                kept = buf[j, h].astype(F32) * d_ref[j, h] + added[i * HEAD_DIM : (i + 1) * HEAD_DIM]
                buf[j, h] = kept.astype(BF16)
        backs[j].start()
    for copy in backs:
        copy.wait()


def state_stage(d, x, w, b, pool):
    slots = pool.shape[0]
    return pl.pallas_call(
        state_kernel,
        out_shape=jax.ShapeDtypeStruct(pool.shape, BF16),
        in_specs=[SMEM] + [VMEM] * 3 + [ANY],
        out_specs=ANY,
        scratch_shapes=[
            pltpu.VMEM(pool.shape, BF16),
            pltpu.SemaphoreType.DMA((slots,)),
            pltpu.SemaphoreType.DMA((slots,)),
        ],
        compiler_params=params(32),
        cost_estimate=cost(4 * pool.size * DRAFT, 4 * pool.size),
    )(d, x, w, b, pool)


def out_kernel(n_line, other_core, n_pool, req, cr, me_ref, orow_ref, *refs):
    if other_core:
        got, refs = refs[:n_pool], refs[n_pool:]
    else:
        got, refs = refs[:1], refs[1:]
    w, outs = refs[0], refs[1 : 1 + n_line]
    refs = refs[1 + n_line :]
    if other_core:
        normed_ref, refs = refs[0], refs[1:]
    buf, sems = refs
    width = buf.shape[2]
    rank = me_ref[1]
    core, line = rank & 1, rank >> 1
    if other_core:
        core = 1 - core
    copies = []
    order = list(range(1, n_line)) + [0]
    for i in order:
        there = line + i
        there = jnp.where(there >= n_line, there - n_line, there)
        column = pl.multiple_of((2 * there + core) * width, 128)
        copies.append(pltpu.make_async_copy(w.at[:, pl.ds(column, width)], buf.at[i], sems.at[i]))
        copies[-1].start()
    if other_core:
        collect = collect_matrix(orow_ref[...].astype(F32), me_ref[0], n_pool, req, cr)
        rows = dot(collect, jnp.concatenate([g[...] for g in got], axis=0)).astype(BF16)
        normed_ref[...] = rows
    else:
        rows = got[0][...]
    for copy, i in zip(copies, order):
        copy.wait()
        outs[i][...] = dot(rows, buf[i]).astype(outs[i].dtype)


def out_stage(me, orow, got, w, n_line, other_core, n_pool, req, cr):
    depth, total = w.shape
    width = total // (2 * n_line)
    tokens = req * DRAFT
    kind = BF16 if other_core else F32
    shapes = [jax.ShapeDtypeStruct((tokens, width), kind)] * n_line
    if other_core:
        shapes = shapes + [jax.ShapeDtypeStruct((tokens, depth), BF16)]
    return pl.pallas_call(
        functools.partial(out_kernel, n_line, other_core, n_pool, req, cr),
        out_shape=shapes,
        in_specs=[SMEM, VMEM] + [VMEM] * len(got) + [ANY],
        out_specs=[VMEM] * len(shapes),
        scratch_shapes=[pltpu.VMEM((n_line, depth, width), BF16), pltpu.SemaphoreType.DMA((n_line,))],
        compiler_params=params(32),
        cost_estimate=cost(tokens * depth * total, depth * total),
    )(me, orow, *got, w)


def body(
    hidden,
    w_x,
    w_bc,
    w_dt,
    conv_x,
    conv_bc,
    dt_bias,
    a_log,
    d_skip,
    norm_gain,
    w_out,
    ssm_pool,
    conv_pool_x,
    conv_pool_bc,
    owners,
    slots,
    accepted,
):
    n_pool = lax.axis_size("pool")
    n_tensor = lax.axis_size("tensor")
    n_line = n_tensor // 2
    rank = lax.axis_index("tensor").astype(jnp.int32)
    me = jnp.stack([lax.axis_index("pool").astype(jnp.int32), rank])
    req = hidden.shape[0] // DRAFT
    share = req // n_pool
    capacity = share + share // 2
    cr = -(-capacity * DRAFT // 16) * 16
    head_local = w_dt.shape[1]
    span = max(1, head_local // (HEADS // GROUPS))
    orow, srow, arow = (v.reshape(1, -1) for v in (owners, slots, accepted))

    def row(v):
        return v.reshape(1, -1)

    def to_owner(parts):
        return [parts[0]] + [
            lax.ppermute(parts[s], "pool", [(i, (i + s) % n_pool) for i in range(n_pool)]) for s in range(1, n_pool)
        ]

    def to_requester(parts):
        return [parts[0]] + [
            lax.ppermute(parts[s], "pool", [((i + s) % n_pool, i) for i in range(n_pool)]) for s in range(1, n_pool)
        ]

    bc_sent = project(me, orow, hidden, w_bc, w_dt, n_pool, req, cr)
    bc_got = to_owner(bc_sent)
    x_sent = project(me, orow, hidden, w_x, None, n_pool, req, cr)
    x_got = to_owner(x_sent)
    act, dt, new_conv_bc = bc_stage(
        me, orow, srow, arow, bc_got, conv_pool_bc, conv_bc, head_local, n_pool, req, cr
    )
    b, c = exchange(act, n_tensor, span, rank)
    y, m, w, d = mix_stage(me, orow, srow, arow, b, c, dt, row(dt_bias), row(a_log), ssm_pool)
    stage = x_stage(
        me, orow, srow, arow, x_got, conv_pool_x, conv_x, y, m, row(d_skip), row(norm_gain), n_pool, req, cr
    )
    normed_sent, (x, new_conv_x) = stage[:n_pool], stage[n_pool:]
    normed_got = to_requester(normed_sent)
    new_pool = state_stage(d, x, w, b, ssm_pool)
    sends = out_stage(me, orow, normed_got, w_out, n_line, True, n_pool, req, cr)
    sends, normed = sends[:n_line], sends[n_line]
    swap = [(i, i ^ 1) for i in range(n_tensor)]
    order = list(range(1, n_line)) + [0]
    core_got = {i: lax.ppermute(sends[i], "tensor", swap) for i in order}
    keeps = out_stage(me, orow, [normed], w_out, n_line, False, n_pool, req, cr)
    mixed = None
    arrived = []
    for i in range(1, n_line):
        ahead = (keeps[i] + core_got[i].astype(F32)).astype(BF16)
        pairs = [(r, ((r // 2 + i) % n_line) * 2 + r % 2) for r in range(n_tensor)]
        arrived.append(lax.ppermute(ahead, "tensor", pairs))
    mixed = keeps[0] + core_got[0].astype(F32)
    for one in arrived:
        mixed = mixed + one.astype(F32)
    return (mixed.astype(BF16), new_pool, new_conv_x, new_conv_bc)


def solution(mesh):
    in_specs = (
        P(("groups", "pool"), None),
        P(None, "tensor"),
        P(None, "tensor"),
        P(None, "tensor"),
        P(None, "tensor"),
        P(None, "tensor"),
        P("tensor"),
        P("tensor"),
        P("tensor"),
        P("tensor"),
        P("tensor", None),
        P(("groups", "pool"), "tensor", None, None),
        P(("groups", "pool"), None, "tensor"),
        P(("groups", "pool"), None, "tensor"),
        P("groups"),
        P("groups"),
        P("groups"),
    )
    out_specs = (
        P(("groups", "pool"), "tensor"),
        P(("groups", "pool"), "tensor", None, None),
        P(("groups", "pool"), None, "tensor"),
        P(("groups", "pool"), None, "tensor"),
    )
    return jax.shard_map(body, mesh=mesh, in_specs=in_specs, out_specs=out_specs, check_vma=False)
```

time: 1130 us -> 89.4 us (0.08)
  local copies, waits for them, and re-layouts: 774 us -> 18.9 us
  matrix products: 186 us -> 0 us
  waiting for transfers between devices: 64 us -> 9.22 us
  other arithmetic: 49.8 us -> 2.62 us
  Pallas kernels: 0 us -> 31.5 us
    gather x15 -> x0, local copies, waits for them, and re-layouts: 741 us -> none  [the longest x6 717 us: conv_part(): kept_rows = jnp.take_along_axis(joined, picks, axis=1)]
    dot_general x12 -> x0, matrix products: 186 us -> none  [the longest x8 172 us: verify(): jnp.einsum('rhpn,rhn->rhp', carried, c_heads[:, position], precision=lax....]
    all_to_all x6 -> x0, waiting for transfers between devices: 36.7 us -> none  [the longest x1 29 us: body(): lax.all_to_all(going_home[0], 'pool', split_axis=0, concat_axis=0, tiled=...]
    all_to_all x6 -> x0, starting transfers between devices: 32 us -> none  [the longest x1 6.32 us: body(): lax.all_to_all(sent[2], 'pool', split_axis=0, concat_axis=0, tiled=True)]
    pallas_call x0 -> x8, Pallas kernels: none -> 31.5 us  [the longest x2 8.72 us: project(): pl.pallas_call(functools.partial(project_kernel, n_pool, req, cr, chunk,...]
    reduce_scatter x1 -> x0, waiting for transfers between devices: 27.4 us -> none  [verify(): lax.psum_scatter(partial_value, 'tensor', scatter_dimension=1, tiled=True)]
    convert_element_type x3 -> x2, other arithmetic: 26 us -> 0.85 us  [the longest x1 0.8 us: body(): return (mixed.astype(BF16), new_pool, new_conv_x, new_conv_bc)]
    ppermute x0 -> x14, starting transfers between devices: none -> 21.1 us  [the longest x6 10.9 us: to_owner(): lax.ppermute(parts[s], 'pool', [(i, (i + s) % n_pool) for i in range(n_po...]
  transfers between devices with their start and end apart: 7 -> 14, of which waited for: 4 -> 4; matrix products, arithmetic and copies ran while one was open for 87% -> 7% of each run, Pallas kernels for 0% -> 21%
where the time goes in v1:
time: 89.4 us; the launch traced here: 89 us
  Pallas kernels  31.5 us (35%)
  starting transfers between devices  21.1 us (24%)
  local copies, waits for them, and re-layouts  18.9 us (21%)
  waiting for transfers between devices  9.22 us (10%)
  between operations  5.63 us (6%)
  other arithmetic  2.62 us (3%)
    unnamed x59, local copies, waits for them, and re-layouts  14.7 us
    ppermute x6, starting transfers between devices, to_owner(): lax.ppermute(parts[s], 'pool', [(i, (i + s) % n_pool) for i in range(n_po...  10.9 us
    pallas_call x2, Pallas kernels, project(): pl.pallas_call(functools.partial(project_kernel, n_pool, req, cr, chunk,...  8.72 us
    ppermute x3, waiting for transfers between devices, to_requester(): lax.ppermute(parts[s], 'pool', [((i + s) % n_pool, i) for i in range(n_po...  8.48 us
    pallas_call x1, Pallas kernels, state_stage(): pl.pallas_call(state_kernel, out_shape=jax.ShapeDtypeStruct(pool.shape, B...  7.57 us
    pallas_call x1, Pallas kernels, mix_stage(): pl.pallas_call(mix_kernel, out_shape=[jax.ShapeDtypeStruct((rows, heads *...  5.3 us
    pallas_call x2, Pallas kernels, out_stage(): pl.pallas_call(functools.partial(out_kernel, n_line, other_core, n_pool,...  4.43 us
    ppermute x3, starting transfers between devices, to_requester(): lax.ppermute(parts[s], 'pool', [((i + s) % n_pool, i) for i in range(n_po...  4.05 us
  transfers between devices with their start and end apart: 14, of which 4 were waited for; matrix products, arithmetic and copies ran while one was open for 7% of the time, Pallas kernels for 21%

profile of v1, /device:TPU:0, one launch (start us, length us, event | category | flops | bytes accessed | tf_op | source)
XLA Modules:
  0.0 89.0 jit_solution(16715802396794114272)
XLA Ops:
  0.6 0.0 copy-start.24
  0.6 0.0 copy-start.23
  0.7 1.5 %copy.29.refs_4_ = bf16[4096,16]{1,0:T(8,128)(2,1)S(1)} copy(bf16[4096,16]{0,1:T(8,128)(2,1)} %param.28) | data formatting | bytes 262144 | tf_op args[3]
  2.2 0.1 pad_add_fusion.refs_0_.me_ref
  2.3 2.2 %copy-done.3 = bf16[4096,512]{1,0:T(8,128)(2,1)S(1)} copy-done((bf16[4096,512]{1,0:T(8,128)(2,1)S(1)}, bf16[4096,512]{1,0:T(8,128)(2,1)}, u32[]{:S(2)}) %copy-start.3) | copy-done | bytes 4194328
  4.5 1.2 %copy-done.4 = bf16[128,4096]{1,0:T(8,128)(2,1)S(1)} copy-done((bf16[128,4096]{1,0:T(8,128)(2,1)S(1)}, bf16[128,4096]{1,0:T(8,128)(2,1)}, u32[]{:S(2)}) %copy-start.4) | copy-done | bytes 1048600
  5.7 0.7 copy-done.8
  6.3 5.1 %shard_map.265 = (bf16[48,640]{1,0:T(8,128)(2,1)S(1)}, bf16[48,640]{1,0:T(8,128)(2,1)S(1)}, bf16[48,640]{1,0:T(8,128)(2,1)S(1)}, bf16[48,640]{1,0:T(8,128)(2,1)S(1)}) custom-call(s32[2]{0:T(128)S(1)} %pad_add_fusion.refs_0_.me_ref, s32[1,64]{1,0:T(1,128)S(1)} %bitcast.22, bf16[128,4096]{1,0:T(8,128)(2,1)S(1)} %copy-done.4, bf16[4096,512]{1,0:T(8,128)(2,1)S(1)} %copy-done.3, ...), custom_call_target="tpu_custom_call" | custom-call | flops 536870912 | bytes 6291456 | tf_op jit(solution)/shard_map/pallas_call | solution.py:232
  11.5 3.1 %collective-permute-start.3 = (bf16[48,640]{1,0:T(8,128)(2,1)S(1)}, bf16[48,640]{1,0:T(8,128)(2,1)S(1)}, u32[]{:S(2)}, u32[]{:S(2)}) collective-permute-start(bf16[48,640]{1,0:T(8,128)(2,1)S(1)} %get-tuple-element.35), channel_id=1, source_target_pairs={{0,4},{4,8},{8,12},{12,0},{1,5},{5,9},{9,13},{13,1},{2,6},{6,10},{... | collective-permute-start | bytes 184328 | tf_op jit(solution)/shard_map/ppermute | solution.py:578
  14.6 2.6 %collective-permute-start.4 = (bf16[48,640]{1,0:T(8,128)(2,1)S(1)}, bf16[48,640]{1,0:T(8,128)(2,1)S(1)}, u32[]{:S(2)}, u32[]{:S(2)}) collective-permute-start(bf16[48,640]{1,0:T(8,128)(2,1)S(1)} %get-tuple-element.36), channel_id=1, source_target_pairs={{0,8},{4,12},{8,0},{12,4},{1,9},{5,13},{9,1},{13,5},{2,10},{6,14},... | collective-permute-start | bytes 184328 | tf_op jit(solution)/shard_map/ppermute | solution.py:578
  17.2 1.3 %collective-permute-start.5 = (bf16[48,640]{1,0:T(8,128)(2,1)S(1)}, bf16[48,640]{1,0:T(8,128)(2,1)S(1)}, u32[]{:S(2)}, u32[]{:S(2)}) collective-permute-start(bf16[48,640]{1,0:T(8,128)(2,1)S(1)} %get-tuple-element.37), channel_id=1, source_target_pairs={{0,12},{4,0},{8,4},{12,8},{1,13},{5,1},{9,5},{13,9},{2,14},{6,2},{... | collective-permute-start | bytes 184328 | tf_op jit(solution)/shard_map/ppermute | solution.py:578
  18.5 0.6 dynamic_slice.37
  19.8 0.6 dynamic_slice.40
  21.0 0.4 collective-permute-done.4.refs_2_
  21.4 0.3 collective-permute-done.5.refs_3_
  21.8 2.0 %shard_map.266 = (bf16[144,512]{1,0:T(8,128)(2,1)S(1)}, f32[144,16]{1,0:T(8,128)S(1)}, bf16[18,3,512]{2,1,0:T(4,128)(2,1)}) custom-call(s32[2]{0:T(128)S(1)} %pad_add_fusion.refs_0_.me_ref, s32[1,64]{1,0:T(1,128)S(1)} %bitcast.23, s32[1,64]{1,0:T(1,128)S(1)} %bitcast.29, s32[1,64]{1,0:T(1,128)S(1)} %bitcast.32, ...), custom_call_target="tpu_custom_call" | custom-call | flops 2000000 | bytes 1000000 | tf_op jit(solution)/shard_map/pallas_call | solution.py:266
  23.8 1.9 %collective-permute-start.7 = (bf16[144,256]{1,0:T(8,128)(2,1)S(1)}, bf16[144,256]{1,0:T(8,128)(2,1)S(1)}, u32[]{:S(2)}, u32[]{:S(2)}) collective-permute-start(bf16[144,256]{1,0:T(8,128)(2,1)S(1)} %get-tuple-element.58), channel_id=1, source_target_pairs={{2,0},{0,1},{1,2},{6,4},{4,5},{5,6},{10,8},{8,9},{9,10},{14,12},{1... | collective-permute-start | bytes 221192 | tf_op jit(solution)/shard_map/ppermute | solution.py:324
  25.7 0.7 collective-permute-start.6
  26.4 3.4 %copy-done.2 = bf16[4096,1024]{1,0:T(8,128)(2,1)S(1)} copy-done((bf16[4096,1024]{1,0:T(8,128)(2,1)S(1)}, bf16[4096,1024]{1,0:T(8,128)(2,1)}, u32[]{:S(2)}) %copy-start.2) | copy-done | bytes 8388632
  29.8 0.0 copy-start.18
  29.8 0.0 copy-start.15
  29.9 3.6 %shard_map.264 = (bf16[48,1024]{1,0:T(8,128)(2,1)S(1)}, bf16[48,1024]{1,0:T(8,128)(2,1)S(1)}, bf16[48,1024]{1,0:T(8,128)(2,1)S(1)}, bf16[48,1024]{1,0:T(8,128)(2,1)S(1)}) custom-call(s32[2]{0:T(128)S(1)} %pad_add_fusion.refs_0_.me_ref, s32[1,64]{1,0:T(1,128)S(1)} %bitcast.24, bf16[128,4096]{1,0:T(8,128)(2,1)S(1)} %copy-done.5, bf16[4096,1024]{1,0:T(8,128)(2,1)S(1)} %copy-done.2), custom_call_target="tpu_custom_call" | custom-call | flops 1073741824 | bytes 9437184 | tf_op jit(solution)/shard_map/pallas_call | solution.py:232
  33.5 1.4 %collective-permute-start = (bf16[48,1024]{1,0:T(8,128)(2,1)S(1)}, bf16[48,1024]{1,0:T(8,128)(2,1)S(1)}, u32[]{:S(2)}, u32[]{:S(2)}) collective-permute-start(bf16[48,1024]{1,0:T(8,128)(2,1)S(1)} %get-tuple-element.31), channel_id=1, source_target_pairs={{0,4},{4,8},{8,12},{12,0},{1,5},{5,9},{9,13},{13,1},{2,6},{6,10},{... | collective-permute-start | bytes 294920 | tf_op jit(solution)/shard_map/ppermute | solution.py:578
  34.9 2.1 %collective-permute-start.1 = (bf16[48,1024]{1,0:T(8,128)(2,1)S(1)}, bf16[48,1024]{1,0:T(8,128)(2,1)S(1)}, u32[]{:S(2)}, u32[]{:S(2)}) collective-permute-start(bf16[48,1024]{1,0:T(8,128)(2,1)S(1)} %get-tuple-element.32), channel_id=1, source_target_pairs={{0,8},{4,12},{8,0},{12,4},{1,9},{5,13},{9,1},{13,5},{2,10},{6,14},... | collective-permute-start | bytes 294920 | tf_op jit(solution)/shard_map/ppermute | solution.py:578
  37.0 0.4 collective-permute-start.2
  37.4 0.6 dynamic_slice.36
  39.3 0.6 dynamic_slice.39
  41.2 0.6 dynamic_slice.46
  42.4 0.6 dynamic_slice.45
  43.0 0.6 dynamic_slice.42
  43.7 1.7 %select_select_fusion = (bf16[144,256]{1,0:T(8,128)(2,1)S(1)}, bf16[144,256]{1,0:T(8,128)(2,1)S(1)}) fusion(bf16[144,256]{1,0:T(8,128)(2,1)S(1)} %collective-permute-done.6, bf16[144,256]{1,0:T(8,128)(2,1)S(1)} %collective-permute-done.7, bf16[144,512]{1,0:T(8,128)(2,1)S(1)} %get-tuple-element.38, s32[]{:T(128)S(6)} %select_n.73, pred[]{:T(512)} %bitcast.12, ...), kind=kLoop, calls=%fused_computation.5 | loop fusion | flops 221184 | bytes 442378 | tf_op jit(solution)/shard_map/jit(_where)/select_n | solution.py:327
  45.4 2.3 %copy-done.1 = bf16[18,16,64,128]{3,2,1,0:T(8,128)(2,1)S(1)} copy-done((bf16[18,16,64,128]{3,2,1,0:T(8,128)(2,1)S(1)}, bf16[18,16,64,128]{3,2,1,0:T(8,128)(2,1)}, u32[]{:S(2)}) %copy-start.1) | copy-done | bytes 4718616
  47.7 5.3 %shard_map.267 = (f32[144,1024]{1,0:T(8,128)S(1)}, bf16[16,144,144]{2,1,0:T(8,128)(2,1)S(1)}, f32[144,16]{1,0:T(8,128)S(1)}, f32[18,16]{1,0:T(8,128)S(1)}) custom-call(s32[2]{0:T(128)S(1)} %pad_add_fusion.refs_0_.me_ref, s32[1,64]{1,0:T(1,128)S(1)} %bitcast.25, s32[1,64]{1,0:T(1,128)S(1)} %bitcast.30, s32[1,64]{1,0:T(1,128)S(1)} %bitcast.33, ...), custom_call_target="tpu_custom_call" | custom-call | flops 37748736 | bytes 4718592 | tf_op jit(solution)/shard_map/pallas_call | solution.py:385
  53.1 3.5 %shard_map.268 = (bf16[48,1024]{1,0:T(8,128)(2,1)S(1)}, bf16[48,1024]{1,0:T(8,128)(2,1)S(1)}, bf16[48,1024]{1,0:T(8,128)(2,1)S(1)}, bf16[48,1024]{1,0:T(8,128)(2...) custom-call(s32[2]{0:T(128)S(1)} %pad_add_fusion.refs_0_.me_ref, s32[1,64]{1,0:T(1,128)S(1)} %bitcast.26, ...), custom_call_target="tpu_custom_call" | custom-call | flops 42467328 | bytes 4000000 | tf_op jit(solution)/shard_map/pallas_call | solution.py:432
  56.6 1.9 %collective-permute-start.8 = (bf16[48,1024]{1,0:T(8,128)(2,1)S(1)}, bf16[48,1024]{1,0:T(8,128)(2,1)S(1)}, u32[]{:S(2)}, u32[]{:S(2)}) collective-permute-start(bf16[48,1024]{1,0:T(8,128)(2,1)S(1)} %get-tuple-element.43), channel_id=1, source_target_pairs={{4,0},{8,4},{12,8},{0,12},{5,1},{9,5},{13,9},{1,13},{6,2},{10,6},{... | collective-permute-start | bytes 294920 | tf_op jit(solution)/shard_map/ppermute | solution.py:583
  58.5 1.2 %collective-permute-start.9 = (bf16[48,1024]{1,0:T(8,128)(2,1)S(1)}, bf16[48,1024]{1,0:T(8,128)(2,1)S(1)}, u32[]{:S(2)}, u32[]{:S(2)}) collective-permute-start(bf16[48,1024]{1,0:T(8,128)(2,1)S(1)} %get-tuple-element.44), channel_id=1, source_target_pairs={{8,0},{12,4},{0,8},{4,12},{9,1},{13,5},{1,9},{5,13},{10,2},{14,6},... | collective-permute-start | bytes 294920 | tf_op jit(solution)/shard_map/ppermute | solution.py:583
  59.7 0.9 %collective-permute-start.10 = (bf16[48,1024]{1,0:T(8,128)(2,1)S(1)}, bf16[48,1024]{1,0:T(8,128)(2,1)S(1)}, u32[]{:S(2)}, u32[]{:S(2)}) collective-permute-start(bf16[48,1024]{1,0:T(8,128)(2,1)S(1)} %get-tuple-element.45), channel_id=1, source_target_pairs={{12,0},{0,4},{4,8},{8,12},{13,1},{1,5},{5,9},{9,13},{14,2},{2,6},{... | collective-permute-start | bytes 294920 | tf_op jit(solution)/shard_map/ppermute | solution.py:583
  60.6 0.6 collective-permute-done.8.refs_1_
  61.2 7.9 %collective-permute-done.9.refs_2_ = bf16[48,1024]{1,0:T(8,128)(2,1)S(1)} collective-permute-done((bf16[48,1024]{1,0:T(8,128)(2,1)S(1)}, bf16[48,1024]{1,0:T(8,128)(2,1)S(1)}, u32[]{:S(2)}, u32[]{:S(2)}) %collective-permute-start.9) | collective-permute-done | bytes 98336 | tf_op jit(solution)/shard_map/ppermute | solution.py:583
  69.1 3.4 %copy-done = bf16[1024,4096]{1,0:T(8,128)(2,1)S(1)} copy-done((bf16[1024,4096]{1,0:T(8,128)(2,1)S(1)}, bf16[1024,4096]{1,0:T(8,128)(2,1)}, u32[]{:S(2)}) %copy-start) | copy-done | bytes 8388632
  72.5 2.4 %shard_map.269 = (bf16[128,1024]{1,0:T(8,128)(2,1)S(1)}, bf16[128,1024]{1,0:T(8,128)(2,1)S(1)}, bf16[128,1024]{1,0:T(8,128)(2,1)S(1)}) custom-call(s32[2]{0:T(128)S(1)} %pad_add_fusion.refs_0_.me_ref, s32[1,64]{1,0:T(1,128)S(1)} %bitcast.27, bf16[48,1024]{1,0:T(8,128)(2,1)S(1)} %get-tuple-element.42.refs_0_, ...), custom_call_target="tpu_custom_call" | custom-call | flops 536870912 | bytes 4194304 | tf_op jit(solution)/shard_map/pallas_call | solution.py:530
  74.9 0.4 collective-permute-start.12
  75.3 0.2 collective-permute-start.11
  75.5 2.0 %shard_map.270 = (f32[128,1024]{1,0:T(8,128)S(1)}, f32[128,1024]{1,0:T(8,128)S(1)}) custom-call(s32[2]{0:T(128)S(1)} %pad_add_fusion.refs_0_.me_ref, s32[1,64]{1,0:T(1,128)S(1)} %bitcast.28, bf16[128,1024]{1,0:T(8,128)(2,1)S(1)} %get-tuple-element.46.refs_0_, bf16[1024,4096]{1,0:T(8,128)(2,1)S(1)} %bitcast.19), custom_call_target="tpu_custom_call" | custom-call | flops 536870912 | bytes 4194304 | tf_op jit(solution)/shard_map/pallas_call | solution.py:530
  77.5 0.1 add_convert_fusion.1
  77.6 3.0 %collective-permute-start.13 = (bf16[128,1024]{1,0:T(8,128)(2,1)S(1)}, bf16[128,1024]{1,0:T(8,128)(2,1)S(1)}, u32[]{:S(2)}, u32[]{:S(2)}) collective-permute-start(bf16[128,1024]{1,0:T(8,128)(2,1)S(1)} %add_convert_fusion.1), channel_id=1, source_target_pairs={{0,2},{1,3},{2,0},{3,1},{4,6},{5,7},{6,4},{7,5},{8,10},{9,11},{10,... | collective-permute-start | bytes 786440 | tf_op jit(solution)/shard_map/ppermute | solution.py:612
  80.6 7.6 %shard_map.271 = bf16[18,16,64,128]{3,2,1,0:T(8,128)(2,1)} custom-call(f32[18,16]{1,0:T(8,128)S(1)} %get-tuple-element.51.d_ref, f32[144,1024]{1,0:T(8,128)S(1)} %get-tuple-element.52.x_ref, f32[144,16]{1,0:T(8,128)S(1)} %get-tuple-element.53.w_ref, bf16[144,256]{1,0:T(8,128)(2,1)S(1)} %get-tuple-element.57.b_ref, bf16[18,16,64,128]{3,2,1,0:T(8,128)(2,1)S(1)} %bitcast.21), custom_call_target="tpu_custom_call" | custom-call | flops 75497472 | bytes 9437184 | tf_op jit(solution)/shard_map/pallas_call | solution.py:473
  88.2 0.8 add_convert_fusion
  (61 shorter events, 0.2 us)
Async XLA Ops:
  0.6 17.9 %copy-start.24 = (s32[4]{0:T(128)S(1)}, s32[4]{0:T(128)}, u32[]{:S(2)}) copy-start(s32[4]{0:T(128)} %constant.50.clone) | copy-start | bytes 52
  0.6 19.1 %copy-start.23 = (s32[4]{0:T(128)S(1)}, s32[4]{0:T(128)}, u32[]{:S(2)}) copy-start(s32[4]{0:T(128)} %constant.48.clone) | copy-start | bytes 52
  0.7 25.8 %copy-start.5 = (bf16[128,4096]{1,0:T(8,128)(2,1)S(1)}, bf16[128,4096]{1,0:T(8,128)(2,1)}, u32[]{:S(2)}) copy-start(bf16[128,4096]{1,0:T(8,128)(2,1)} %refs_2_.3) | copy-start | bytes 3145732
  0.7 21.1 %copy-start.9 = (s32[64]{0:T(128)S(1)}, s32[64]{0:T(128)}, u32[]{:S(2)}) copy-start(s32[64]{0:T(128)} %param.39) | copy-start | bytes 772
  0.7 21.1 %copy-start.13 = (s32[64]{0:T(128)S(1)}, s32[64]{0:T(128)}, u32[]{:S(2)}) copy-start(s32[64]{0:T(128)} %param.41) | copy-start | bytes 772
  0.7 21.1 %copy-start.12 = (s32[64]{0:T(128)S(1)}, s32[64]{0:T(128)}, u32[]{:S(2)}) copy-start(s32[64]{0:T(128)} %param.40) | copy-start | bytes 772
  0.7 21.0 %copy-start.7 = (bf16[18,3,512]{2,1,0:T(4,128)(2,1)S(1)}, bf16[18,3,512]{2,1,0:T(4,128)(2,1)}, u32[]{:S(2)}) copy-start(bf16[18,3,512]{2,1,0:T(4,128)(2,1)} %refs_4_.4) | copy-start | bytes 165892
  0.7 21.0 %copy-start.11 = (f32[4,512]{1,0:T(4,128)S(1)}, f32[4,512]{1,0:T(4,128)}, u32[]{:S(2)}) copy-start(f32[4,512]{1,0:T(4,128)} %refs_5_.2) | copy-start | bytes 24580
  2.3 2.2 %copy-start.3 = (bf16[4096,512]{1,0:T(8,128)(2,1)S(1)}, bf16[4096,512]{1,0:T(8,128)(2,1)}, u32[]{:S(2)}) copy-start(bf16[4096,512]{1,0:T(8,128)(2,1)} %refs_3_.3) | copy-start | bytes 12582916
  4.5 1.2 %copy-start.4 = (bf16[128,4096]{1,0:T(8,128)(2,1)S(1)}, bf16[128,4096]{1,0:T(8,128)(2,1)}, u32[]{:S(2)}) copy-start(bf16[128,4096]{1,0:T(8,128)(2,1)} %refs_2_.3) | copy-start | bytes 3145732
  5.7 0.7 copy-start.8
  11.5 9.5 %collective-permute-start.3 = (bf16[48,640]{1,0:T(8,128)(2,1)S(1)}, bf16[48,640]{1,0:T(8,128)(2,1)S(1)}, u32[]{:S(2)}, u32[]{:S(2)}) collective-permute-start(bf16[48,640]{1,0:T(8,128)(2,1)S(1)} %get-tuple-element.35), channel_id=1, source_target_pairs={{0,4},{4,8},{8,12},{12,0},{1,5},{5,9},{9,13},{13,1},{2,6},{6,10},{... | collective-permute-start | bytes 184328 | tf_op jit(solution)/shard_map/ppermute | solution.py:578
  14.6 6.9 %collective-permute-start.4 = (bf16[48,640]{1,0:T(8,128)(2,1)S(1)}, bf16[48,640]{1,0:T(8,128)(2,1)S(1)}, u32[]{:S(2)}, u32[]{:S(2)}) collective-permute-start(bf16[48,640]{1,0:T(8,128)(2,1)S(1)} %get-tuple-element.36), channel_id=1, source_target_pairs={{0,8},{4,12},{8,0},{12,4},{1,9},{5,13},{9,1},{13,5},{2,10},{6,14},... | collective-permute-start | bytes 184328 | tf_op jit(solution)/shard_map/ppermute | solution.py:578
  17.2 4.6 %collective-permute-start.5 = (bf16[48,640]{1,0:T(8,128)(2,1)S(1)}, bf16[48,640]{1,0:T(8,128)(2,1)S(1)}, u32[]{:S(2)}, u32[]{:S(2)}) collective-permute-start(bf16[48,640]{1,0:T(8,128)(2,1)S(1)} %get-tuple-element.37), channel_id=1, source_target_pairs={{0,12},{4,0},{8,4},{12,8},{1,13},{5,1},{9,5},{13,9},{2,14},{6,2},{... | collective-permute-start | bytes 184328 | tf_op jit(solution)/shard_map/ppermute | solution.py:578
  23.8 19.9 %collective-permute-start.7 = (bf16[144,256]{1,0:T(8,128)(2,1)S(1)}, bf16[144,256]{1,0:T(8,128)(2,1)S(1)}, u32[]{:S(2)}, u32[]{:S(2)}) collective-permute-start(bf16[144,256]{1,0:T(8,128)(2,1)S(1)} %get-tuple-element.58), channel_id=1, source_target_pairs={{2,0},{0,1},{1,2},{6,4},{4,5},{5,6},{10,8},{8,9},{9,10},{14,12},{1... | collective-permute-start | bytes 221192 | tf_op jit(solution)/shard_map/ppermute | solution.py:324
  25.7 17.9 %collective-permute-start.6 = (bf16[144,256]{1,0:T(8,128)(2,1)S(1)}, bf16[144,256]{1,0:T(8,128)(2,1)S(1)}, u32[]{:S(2)}, u32[]{:S(2)}) collective-permute-start(bf16[144,256]{1,0:T(8,128)(2,1)S(1)} %get-tuple-element.59), channel_id=1, source_target_pairs={{2,1},{3,2},{1,3},{6,5},{7,6},{5,7},{10,9},{11,10},{9,11},{14,13},... | collective-permute-start | bytes 221192 | tf_op jit(solution)/shard_map/ppermute | solution.py:324
  26.4 3.4 %copy-start.2 = (bf16[4096,1024]{1,0:T(8,128)(2,1)S(1)}, bf16[4096,1024]{1,0:T(8,128)(2,1)}, u32[]{:S(2)}) copy-start(bf16[4096,1024]{1,0:T(8,128)(2,1)} %refs_3_.2) | copy-start | bytes 25165828
  29.8 7.6 %copy-start.22 = (s32[4]{0:T(128)S(1)}, s32[4]{0:T(128)}, u32[]{:S(2)}) copy-start(s32[4]{0:T(128)} %constant.51.clone) | copy-start | bytes 52
  29.8 9.5 %copy-start.21 = (s32[4]{0:T(128)S(1)}, s32[4]{0:T(128)}, u32[]{:S(2)}) copy-start(s32[4]{0:T(128)} %constant.49.clone) | copy-start | bytes 52
  29.8 11.4 %copy-start.20 = (s32[4]{0:T(128)S(1)}, s32[4]{0:T(128)}, u32[]{:S(2)}) copy-start(s32[4]{0:T(128)} %constant.47.clone) | copy-start | bytes 52
  29.8 12.6 %copy-start.19 = (pred[4]{0:T(512)(128)(4,1)S(1)}, pred[4]{0:T(512)(128)(4,1)}, u32[]{:S(2)}) copy-start(pred[4]{0:T(512)(128)(4,1)} %constant.46.clone) | copy-start | bytes 16
  29.8 13.2 %copy-start.18 = (pred[4]{0:T(512)(128)(4,1)S(1)}, pred[4]{0:T(512)(128)(4,1)}, u32[]{:S(2)}) copy-start(pred[4]{0:T(512)(128)(4,1)} %constant.44.clone) | copy-start | bytes 16
  29.8 15.5 %copy-start.15 = (f32[16]{0:T(128)S(1)}, f32[16]{0:T(128)}, u32[]{:S(2)}) copy-start(f32[16]{0:T(128)} %param.31) | copy-start | bytes 196
  29.8 15.5 %copy-start.16 = (f32[16]{0:T(128)S(1)}, f32[16]{0:T(128)}, u32[]{:S(2)}) copy-start(f32[16]{0:T(128)} %param.32) | copy-start | bytes 196
  29.9 23.2 %copy-start.6 = (bf16[18,3,1024]{2,1,0:T(4,128)(2,1)S(1)}, bf16[18,3,1024]{2,1,0:T(4,128)(2,1)}, u32[]{:S(2)}) copy-start(bf16[18,3,1024]{2,1,0:T(4,128)(2,1)} %refs_4_.5) | copy-start | bytes 331780
  33.5 19.6 %copy-start.10 = (f32[4,1024]{1,0:T(4,128)S(1)}, f32[4,1024]{1,0:T(4,128)}, u32[]{:S(2)}) copy-start(f32[4,1024]{1,0:T(4,128)} %refs_5_.3) | copy-start | bytes 49156
  33.5 19.6 %copy-start.14 = (f32[1024]{0:T(1024)S(1)}, f32[1024]{0:T(1024)}, u32[]{:S(2)}) copy-start(f32[1024]{0:T(1024)} %param.34) | copy-start | bytes 12292
  33.5 19.6 %copy-start.17 = (f32[16]{0:T(128)S(1)}, f32[16]{0:T(128)}, u32[]{:S(2)}) copy-start(f32[16]{0:T(128)} %param.33) | copy-start | bytes 196
  33.5 19.6 %collective-permute-start = (bf16[48,1024]{1,0:T(8,128)(2,1)S(1)}, bf16[48,1024]{1,0:T(8,128)(2,1)S(1)}, u32[]{:S(2)}, u32[]{:S(2)}) collective-permute-start(bf16[48,1024]{1,0:T(8,128)(2,1)S(1)} %get-tuple-element.31), channel_id=1, source_target_pairs={{0,4},{4,8},{8,12},{12,0},{1,5},{5,9},{9,13},{13,1},{2,6},{6,10},{... | collective-permute-start | bytes 294920 | tf_op jit(solution)/shard_map/ppermute | solution.py:578
  34.9 18.1 %collective-permute-start.1 = (bf16[48,1024]{1,0:T(8,128)(2,1)S(1)}, bf16[48,1024]{1,0:T(8,128)(2,1)S(1)}, u32[]{:S(2)}, u32[]{:S(2)}) collective-permute-start(bf16[48,1024]{1,0:T(8,128)(2,1)S(1)} %get-tuple-element.32), channel_id=1, source_target_pairs={{0,8},{4,12},{8,0},{12,4},{1,9},{5,13},{9,1},{13,5},{2,10},{6,14},... | collective-permute-start | bytes 294920 | tf_op jit(solution)/shard_map/ppermute | solution.py:578
  37.0 16.1 %collective-permute-start.2 = (bf16[48,1024]{1,0:T(8,128)(2,1)S(1)}, bf16[48,1024]{1,0:T(8,128)(2,1)S(1)}, u32[]{:S(2)}, u32[]{:S(2)}) collective-permute-start(bf16[48,1024]{1,0:T(8,128)(2,1)S(1)} %get-tuple-element.33), channel_id=1, source_target_pairs={{0,12},{4,0},{8,4},{12,8},{1,13},{5,1},{9,5},{13,9},{2,14},{6,2},{... | collective-permute-start | bytes 294920 | tf_op jit(solution)/shard_map/ppermute | solution.py:578
  43.7 31.8 %slice-start = ((s8[8388608]{0:T(1024)(128)(4,1)}), s8[4194304]{0:T(1024)(128)(4,1)S(1)}, s32[]{:S(2)}) async-start(s8[8388608]{0:T(1024)(128)(4,1)} %bitcast.18), calls=%async_computation | async-start | bytes 8388608
  45.4 2.3 %copy-start.1 = (bf16[18,16,64,128]{3,2,1,0:T(8,128)(2,1)S(1)}, bf16[18,16,64,128]{3,2,1,0:T(8,128)(2,1)}, u32[]{:S(2)}) copy-start(bf16[18,16,64,128]{3,2,1,0:T(8,128)(2,1)} %pool.3) | copy-start | bytes 14155780
  56.6 4.6 %collective-permute-start.8 = (bf16[48,1024]{1,0:T(8,128)(2,1)S(1)}, bf16[48,1024]{1,0:T(8,128)(2,1)S(1)}, u32[]{:S(2)}, u32[]{:S(2)}) collective-permute-start(bf16[48,1024]{1,0:T(8,128)(2,1)S(1)} %get-tuple-element.43), channel_id=1, source_target_pairs={{4,0},{8,4},{12,8},{0,12},{5,1},{9,5},{13,9},{1,13},{6,2},{10,6},{... | collective-permute-start | bytes 294920 | tf_op jit(solution)/shard_map/ppermute | solution.py:583
  58.5 10.6 %collective-permute-start.9 = (bf16[48,1024]{1,0:T(8,128)(2,1)S(1)}, bf16[48,1024]{1,0:T(8,128)(2,1)S(1)}, u32[]{:S(2)}, u32[]{:S(2)}) collective-permute-start(bf16[48,1024]{1,0:T(8,128)(2,1)S(1)} %get-tuple-element.44), channel_id=1, source_target_pairs={{8,0},{12,4},{0,8},{4,12},{9,1},{13,5},{1,9},{5,13},{10,2},{14,6},... | collective-permute-start | bytes 294920 | tf_op jit(solution)/shard_map/ppermute | solution.py:583
  59.7 9.4 %collective-permute-start.10 = (bf16[48,1024]{1,0:T(8,128)(2,1)S(1)}, bf16[48,1024]{1,0:T(8,128)(2,1)S(1)}, u32[]{:S(2)}, u32[]{:S(2)}) collective-permute-start(bf16[48,1024]{1,0:T(8,128)(2,1)S(1)} %get-tuple-element.45), channel_id=1, source_target_pairs={{12,0},{0,4},{4,8},{8,12},{13,1},{1,5},{5,9},{9,13},{14,2},{2,6},{... | collective-permute-start | bytes 294920 | tf_op jit(solution)/shard_map/ppermute | solution.py:583
  69.1 3.4 %copy-start = (bf16[1024,4096]{1,0:T(8,128)(2,1)S(1)}, bf16[1024,4096]{1,0:T(8,128)(2,1)}, u32[]{:S(2)}) copy-start(bf16[1024,4096]{1,0:T(8,128)(2,1)} %refs_1_.1) | copy-start | bytes 25165828
  72.5 3.0 %slice-start.1 = ((s8[8388608]{0:T(1024)(128)(4,1)}), s8[4194304]{0:T(1024)(128)(4,1)S(1)}, s32[]{:S(2)}) async-start(s8[8388608]{0:T(1024)(128)(4,1)} %bitcast.18), calls=%async_computation.1 | async-start | bytes 8388608
  72.5 8.1 %slice-start.2 = ((s8[4718592]{0:T(1024)(128)(4,1)}), s8[4194304]{0:T(1024)(128)(4,1)S(1)}, s32[]{:S(2)}) async-start(s8[4718592]{0:T(1024)(128)(4,1)} %bitcast.20), calls=%async_computation.2 | async-start | bytes 8388608
  74.9 2.6 %collective-permute-start.12 = (bf16[128,1024]{1,0:T(8,128)(2,1)S(1)}, bf16[128,1024]{1,0:T(8,128)(2,1)S(1)}, u32[]{:S(2)}, u32[]{:S(2)}) collective-permute-start(bf16[128,1024]{1,0:T(8,128)(2,1)S(1)} %get-tuple-element.50), channel_id=1, source_target_pairs={{0,1},{1,0},{2,3},{3,2},{4,5},{5,4},{6,7},{7,6},{8,9},{9,8},{10,11... | collective-permute-start | bytes 786440 | tf_op jit(solution)/shard_map/ppermute | solution.py:605
  75.3 12.8 %collective-permute-start.11 = (bf16[128,1024]{1,0:T(8,128)(2,1)S(1)}, bf16[128,1024]{1,0:T(8,128)(2,1)S(1)}, u32[]{:S(2)}, u32[]{:S(2)}) collective-permute-start(bf16[128,1024]{1,0:T(8,128)(2,1)S(1)} %get-tuple-element.48), channel_id=1, source_target_pairs={{0,1},{1,0},{2,3},{3,2},{4,5},{5,4},{6,7},{7,6},{8,9},{9,8},{10,11... | collective-permute-start | bytes 786440 | tf_op jit(solution)/shard_map/ppermute | solution.py:605
  75.5 5.1 %slice-start.3 = ((s8[4718592]{0:T(1024)(128)(4,1)}), s8[524288]{0:T(1024)(128)(4,1)S(1)}, s32[]{:S(2)}) async-start(s8[4718592]{0:T(1024)(128)(4,1)} %bitcast.20), calls=%async_computation.3 | async-start | bytes 1048576
  77.6 10.6 %collective-permute-start.13 = (bf16[128,1024]{1,0:T(8,128)(2,1)S(1)}, bf16[128,1024]{1,0:T(8,128)(2,1)S(1)}, u32[]{:S(2)}, u32[]{:S(2)}) collective-permute-start(bf16[128,1024]{1,0:T(8,128)(2,1)S(1)} %add_convert_fusion.1), channel_id=1, source_target_pairs={{0,2},{1,3},{2,0},{3,1},{4,6},{5,7},{6,4},{7,5},{8,10},{9,11},{10,... | collective-permute-start | bytes 786440 | tf_op jit(solution)/shard_map/ppermute | solution.py:612

commit v2 on v1

--- a/solution.py
+++ b/solution.py
@@ -19,6 +19,7 @@
 F32 = jnp.float32
 BF16 = jnp.bfloat16
 ANY = pl.BlockSpec(memory_space=pl.ANY)
+HBM = pl.BlockSpec(memory_space=pltpu.HBM)
 VMEM = pl.BlockSpec(memory_space=pltpu.VMEM)
 SMEM = pl.BlockSpec(memory_space=pltpu.SMEM)
 
@@ -184,26 +185,26 @@
             ]
         )
         if with_dt:
-            copies[-1].append(pltpu.make_async_copy(w_dt.at[part], refs[3].at[part], sems.at[2, k]))
+            copies[-1].append(pltpu.make_async_copy(w_dt.at[:, part], refs[3].at[:, part], sems.at[2, k]))
         for copy in copies[-1]:
             copy.start()
     order = send_matrix(orow_ref[...].astype(F32), me_ref[0], n_pool, req, cr)
     total = jnp.zeros((hidden.shape[0], w.shape[1]), F32)
     if with_dt:
-        total_dt = jnp.zeros((hidden.shape[0], w_dt.shape[1]), F32)
+        total_dt = jnp.zeros((hidden.shape[0], w_dt.shape[0]), F32)
     for k in range(steps):
         for copy in copies[k]:
             copy.wait()
         rows = hbuf[:, k * chunk : (k + 1) * chunk]
         total = total + dot(rows, wbuf[k * chunk : (k + 1) * chunk])
         if with_dt:
-            total_dt = total_dt + dot(rows, refs[3][k * chunk : (k + 1) * chunk])
+            total_dt = total_dt + dot_t(rows, refs[3][:, k * chunk : (k + 1) * chunk])
     width = w.shape[1]
     placed = dot(order, total.astype(BF16)).astype(BF16)
     for s in range(n_pool):
         outs[s][:, :width] = placed[s * cr : (s + 1) * cr]
     if with_dt:
-        heads = w_dt.shape[1]
+        heads = w_dt.shape[0]
         high = total_dt.astype(BF16)
         low = (total_dt - high.astype(F32)).astype(BF16)
         shape = (heads, 128)
@@ -227,54 +228,25 @@
         pltpu.SemaphoreType.DMA((3, depth // chunk)),
     ]
     if with_dt:
-        scratch.append(pltpu.VMEM((depth, w_dt.shape[1]), BF16))
-    operands = [me, orow, hidden, w] + ([w_dt] if with_dt else [])
+        scratch.append(pltpu.VMEM((w_dt.shape[0], depth), BF16))
+    streamed = [hidden, w] + ([w_dt] if with_dt else [])
+    streamed = [pltpu.with_memory_space_constraint(v, pltpu.HBM) for v in streamed]
     return pl.pallas_call(
         functools.partial(project_kernel, n_pool, req, cr, chunk, with_dt),
         out_shape=[jax.ShapeDtypeStruct((cr, width + extra), BF16)] * n_pool,
-        in_specs=[SMEM, VMEM, ANY, ANY] + ([ANY] if with_dt else []),
+        in_specs=[SMEM, VMEM] + [HBM] * len(streamed),
         out_specs=[VMEM] * n_pool,
         scratch_shapes=scratch,
-        compiler_params=params(32),
+        compiler_params=params(16),
         cost_estimate=cost(2 * tokens * depth * width, depth * (width + extra) * 2 + tokens * depth * 2),
-    )(*operands)
-
-
-def bc_kernel(n_pool, req, cr, me_ref, orow_ref, srow_ref, arow_ref, *refs):
-    got, refs = refs[:n_pool], refs[n_pool:]
-    pool_ref, weight_ref, act_ref, dt_ref, kept_ref = refs
-    slots, _, width = pool_ref.shape
-    me = me_ref[0]
-    orow, srow, arow = (r[...].astype(F32) for r in (orow_ref, srow_ref, arow_ref))
-    order = owner_matrix(orow, srow, me, n_pool, req, cr, slots)
-    accepts = slot_accepts(orow, srow, arow, me, slots)
-    raw = dot(order, jnp.concatenate([g[...] for g in got], axis=0))
-    heads = dt_ref.shape[1]
-    shape = (128, heads)
-    lane = iota(shape, 0)
-    head = iota(shape, 1)
-    both = hot((lane == head) | (lane == head + heads))
-    dt_ref[...] = dot(raw[:, width:].astype(BF16), both)
-    summed, kept = conv_slots(raw[:, :width], pool_ref[...], weight_ref[...], accepts)
-    kept_ref[...] = kept
-    act_ref[...] = silu(summed).astype(BF16)
-
-
-def bc_stage(me, orow, srow, arow, got, pool, weight, heads, n_pool, req, cr):
-    slots, _, width = pool.shape
-    rows = slots * DRAFT
-    return pl.pallas_call(
-        functools.partial(bc_kernel, n_pool, req, cr),
-        out_shape=[
-            jax.ShapeDtypeStruct((rows, width), BF16),
-            jax.ShapeDtypeStruct((rows, heads), F32),
-            jax.ShapeDtypeStruct(pool.shape, BF16),
-        ],
-        in_specs=[SMEM] + [VMEM] * (n_pool + 5),
-        out_specs=[VMEM] * 3,
-        compiler_params=params(24),
-        cost_estimate=cost(2e6, 1e6),
-    )(me, orow, srow, arow, *got, pool, weight)
+    )(me, orow, *streamed)
+
+
+def pick(rank, table):
+    value = jnp.int32(table[0])
+    for i in range(1, len(table)):
+        value = jnp.where(rank == i, jnp.int32(table[i]), value)
+    return value
 
 
 def exchange_plan(n_tensor, width, span):
@@ -296,48 +268,76 @@
                 break
         else:
             rounds.append([edge])
-    return rounds, own
-
-
-def exchange(act, n_tensor, span, rank):
-    width = act.shape[1]
+    return [own] + rounds
+
+
+def bc_kernel(n_pool, req, cr, parts, me_ref, orow_ref, srow_ref, arow_ref, *refs):
+    got, refs = refs[:n_pool], refs[n_pool:]
+    pool_ref, weight_ref, dt_ref, kept_ref = refs[:4]
+    outs, act_ref = refs[4:-1], refs[-1]
+    slots, _, width = pool_ref.shape
+    me, rank = me_ref[0], me_ref[1]
+    orow, srow, arow = (r[...].astype(F32) for r in (orow_ref, srow_ref, arow_ref))
+    order = owner_matrix(orow, srow, me, n_pool, req, cr, slots)
+    accepts = slot_accepts(orow, srow, arow, me, slots)
+    raw = dot(order, jnp.concatenate([g[...] for g in got], axis=0))
+    summed, kept = conv_slots(raw[:, :width], pool_ref[...], weight_ref[...], accepts)
+    act_ref[...] = silu(summed).astype(BF16)
+    for table, out in zip(parts, outs):
+        piece = out.shape[1]
+        out[...] = act_ref[:, pl.ds(pl.multiple_of(pick(rank, table) * piece, 128), piece)]
+    heads = dt_ref.shape[1]
+    shape = (128, heads)
+    lane = iota(shape, 0)
+    head = iota(shape, 1)
+    both = hot((lane == head) | (lane == head + heads))
+    dt_ref[...] = dot(raw[:, width:].astype(BF16), both)
+    kept_ref[...] = kept
+
+
+def bc_stage(me, orow, srow, arow, got, pool, weight, heads, plan, span, n_pool, req, cr):
+    slots, _, width = pool.shape
+    rows = slots * DRAFT
     piece = span * STATE
-    rounds, own = exchange_plan(n_tensor, width, span)
-    sides = [jnp.zeros((act.shape[0], piece), act.dtype)] * 2
-
-    def part_of(table):
-        offset = jnp.asarray(table, jnp.int32)[rank] * piece
-        return lax.dynamic_slice_in_dim(act, offset, piece, axis=1)
-
-    for kind in range(2):
-        table, there = [0] * n_tensor, [False] * n_tensor
-        for source, target, k, part in own:
-            if k == kind:
-                table[target], there[target] = part, True
-        if any(there):
-            sides[kind] = jnp.where(jnp.asarray(there)[rank], part_of(table), sides[kind])
-    for one in rounds:
+    n_tensor = HEADS // heads
+    parts = []
+    for one in plan:
         table = [0] * n_tensor
-        kinds = [-1] * n_tensor
-        for source, target, kind, part in one:
-            table[source], kinds[target] = part, kind
-        moved = lax.ppermute(part_of(table), "tensor", [(e[0], e[1]) for e in one])
-        got = jnp.asarray(kinds, jnp.int32)[rank]
-        for kind in range(2):
-            sides[kind] = jnp.where(got == kind, moved, sides[kind])
-    return sides
-
-
-def mix_kernel(
-    me_ref, orow_ref, srow_ref, arow_ref, b_ref, c_ref, dt_ref, bias_ref, alog_ref, pool, y_ref, m_ref, w_ref, d_ref, buf, sems
-):
+        for source, _, _, part in one:
+            table[source] = part
+        parts.append(table)
+    return pl.pallas_call(
+        functools.partial(bc_kernel, n_pool, req, cr, parts),
+        out_shape=[
+            jax.ShapeDtypeStruct((rows, heads), F32),
+            jax.ShapeDtypeStruct(pool.shape, BF16),
+        ]
+        + [jax.ShapeDtypeStruct((rows, piece), BF16)] * len(plan),
+        in_specs=[SMEM] + [VMEM] * (n_pool + 5),
+        out_specs=[VMEM] * (2 + len(plan)),
+        scratch_shapes=[pltpu.VMEM((rows, width), BF16)],
+        compiler_params=params(16),
+        cost_estimate=cost(2e6, 1e6),
+    )(me, orow, srow, arow, *got, pool, weight)
+
+
+def mix_kernel(kinds, me_ref, orow_ref, srow_ref, arow_ref, *refs):
+    pieces, refs = refs[: len(kinds)], refs[len(kinds) :]
+    dt_ref, bias_ref, alog_ref, pool, y_ref, m_ref, w_ref, d_ref, b_ref, c_ref = refs
     slots, heads = pool.shape[:2]
     rows = slots * DRAFT
     span = b_ref.shape[1] // STATE
     per = heads // span
-    copies = [pltpu.make_async_copy(pool.at[j], buf.at[j], sems.at[j]) for j in range(slots)]
-    for copy in copies:
-        copy.start()
+    for side, ref in enumerate((b_ref, c_ref)):
+        ref[...] = pieces[0][...]
+        for table, piece in zip(kinds, pieces):
+            mine = [int(kind == side) for kind in table]
+            if any(mine):
+
+                @pl.when(pick(me_ref[1], mine) == 1)
+                def _(ref=ref, piece=piece):
+                    ref[...] = piece[...]
+
     orow, srow, arow = (r[...].astype(F32) for r in (orow_ref, srow_ref, arow_ref))
     accepts = slot_accepts(orow, srow, arow, me_ref[0], slots)
     x = dt_ref[...] + bias_ref[...]
@@ -370,32 +370,39 @@
     fade = spread(jnp.exp(logs), spread_matrix(heads))
     c = c_ref[...].astype(F32)
     for j in range(slots):
-        copies[j].wait()
         here = slice(j * DRAFT, (j + 1) * DRAFT)
         for g in range(span):
-            states = buf[j, g * per : (g + 1) * per].reshape(per * HEAD_DIM, STATE)
+            states = pool[j, g * per : (g + 1) * per].reshape(per * HEAD_DIM, STATE)
             columns = slice(g * per * HEAD_DIM, (g + 1) * per * HEAD_DIM)
             read = dot_t(c[here, g * STATE : (g + 1) * STATE].astype(BF16), states)
             y_ref[here, columns] = read * fade[here, columns]
 
 
-def mix_stage(me, orow, srow, arow, b, c, dt, bias, a_log, pool):
+def mix_stage(me, orow, srow, arow, pieces, dt, bias, a_log, pool, plan):
     slots, heads = pool.shape[:2]
     rows = slots * DRAFT
+    n_tensor = HEADS // heads
+    kinds = []
+    for one in plan:
+        table = [-1] * n_tensor
+        for _, target, kind, _ in one:
+            table[target] = kind
+        kinds.append(table)
     return pl.pallas_call(
-        mix_kernel,
+        functools.partial(mix_kernel, kinds),
         out_shape=[
             jax.ShapeDtypeStruct((rows, heads * HEAD_DIM), F32),
             jax.ShapeDtypeStruct((heads, rows, rows), BF16),
             jax.ShapeDtypeStruct((rows, heads), F32),
             jax.ShapeDtypeStruct((slots, heads), F32),
+            jax.ShapeDtypeStruct(pieces[0].shape, BF16),
         ],
-        in_specs=[SMEM] + [VMEM] * 8 + [ANY],
-        out_specs=[VMEM] * 4,
-        scratch_shapes=[pltpu.VMEM(pool.shape, BF16), pltpu.SemaphoreType.DMA((slots,))],
-        compiler_params=params(32),
+        in_specs=[SMEM] + [VMEM] * (7 + len(plan)),
+        out_specs=[VMEM] * 5,
+        scratch_shapes=[pltpu.VMEM(pieces[0].shape, BF16)],
+        compiler_params=params(16),
         cost_estimate=cost(2 * rows * heads * HEAD_DIM * STATE, 2 * pool.size),
-    )(me, orow, srow, arow, b, c, dt, bias, a_log, pool)
+    )(me, orow, srow, arow, *pieces, dt, bias, a_log, pool)
 
 
 def x_kernel(n_pool, req, cr, me_ref, orow_ref, srow_ref, arow_ref, *refs):
@@ -440,28 +447,24 @@
     )(me, orow, srow, arow, *got, pool, weight, y, m, skip, gain)
 
 
-def state_kernel(d_ref, x_ref, w_ref, b_ref, pool, new_pool, buf, sems, out_sems):
+def state_kernel(d_ref, x_ref, w_ref, b_ref, pool, new_pool, buf, out_sems):
     slots, heads = pool.shape[:2]
     rows = slots * DRAFT
     span = b_ref.shape[1] // STATE
     per = heads // span
-    copies = [pltpu.make_async_copy(pool.at[j], buf.at[j], sems.at[j]) for j in range(slots)]
     backs = [pltpu.make_async_copy(buf.at[j], new_pool.at[j], out_sems.at[j]) for j in range(slots)]
-    for copy in copies:
-        copy.start()
     weighted = x_ref[...] * spread(w_ref[...], spread_matrix(heads))
     turned = weighted.T
     high = turned.astype(BF16)
     b = b_ref[...]
     slot = iota((rows, STATE), 0) >> SHIFT
     for j in range(slots):
-        copies[j].wait()
         for g in range(span):
             rhs = jnp.where(slot == j, b[:, g * STATE : (g + 1) * STATE].astype(F32), 0.0).astype(BF16)
             added = dot(high[g * per * HEAD_DIM : (g + 1) * per * HEAD_DIM], rhs)
             for i in range(per):
                 h = g * per + i
-                kept = buf[j, h].astype(F32) * d_ref[j, h] + added[i * HEAD_DIM : (i + 1) * HEAD_DIM]
+                kept = pool[j, h].astype(F32) * d_ref[j, h] + added[i * HEAD_DIM : (i + 1) * HEAD_DIM]
                 buf[j, h] = kept.astype(BF16)
         backs[j].start()
     for copy in backs:
@@ -473,50 +476,36 @@
     return pl.pallas_call(
         state_kernel,
         out_shape=jax.ShapeDtypeStruct(pool.shape, BF16),
-        in_specs=[SMEM] + [VMEM] * 3 + [ANY],
-        out_specs=ANY,
+        in_specs=[SMEM] + [VMEM] * 4,
+        out_specs=HBM,
         scratch_shapes=[
             pltpu.VMEM(pool.shape, BF16),
             pltpu.SemaphoreType.DMA((slots,)),
-            pltpu.SemaphoreType.DMA((slots,)),
         ],
-        compiler_params=params(32),
+        compiler_params=params(16),
         cost_estimate=cost(4 * pool.size * DRAFT, 4 * pool.size),
     )(d, x, w, b, pool)
 
 
 def out_kernel(n_line, other_core, n_pool, req, cr, me_ref, orow_ref, *refs):
-    if other_core:
-        got, refs = refs[:n_pool], refs[n_pool:]
-    else:
-        got, refs = refs[:1], refs[1:]
-    w, outs = refs[0], refs[1 : 1 + n_line]
-    refs = refs[1 + n_line :]
-    if other_core:
-        normed_ref, refs = refs[0], refs[1:]
-    buf, sems = refs
-    width = buf.shape[2]
+    n_got = n_pool if other_core else 1
+    got, w, refs = refs[:n_got], refs[n_got], refs[n_got + 1 :]
+    outs = refs[:n_line]
+    width = outs[0].shape[1]
     rank = me_ref[1]
     core, line = rank & 1, rank >> 1
     if other_core:
         core = 1 - core
-    copies = []
-    order = list(range(1, n_line)) + [0]
-    for i in order:
+        collect = collect_matrix(orow_ref[...].astype(F32), me_ref[0], n_pool, req, cr)
+        rows = dot(collect, jnp.concatenate([g[...] for g in got], axis=0)).astype(BF16)
+        refs[n_line][...] = rows
+    else:
+        rows = got[0][...]
+    for i in list(range(1, n_line)) + [0]:
         there = line + i
         there = jnp.where(there >= n_line, there - n_line, there)
         column = pl.multiple_of((2 * there + core) * width, 128)
-        copies.append(pltpu.make_async_copy(w.at[:, pl.ds(column, width)], buf.at[i], sems.at[i]))
-        copies[-1].start()
-    if other_core:
-        collect = collect_matrix(orow_ref[...].astype(F32), me_ref[0], n_pool, req, cr)
-        rows = dot(collect, jnp.concatenate([g[...] for g in got], axis=0)).astype(BF16)
-        normed_ref[...] = rows
-    else:
-        rows = got[0][...]
-    for copy, i in zip(copies, order):
-        copy.wait()
-        outs[i][...] = dot(rows, buf[i]).astype(outs[i].dtype)
+        outs[i][...] = dot(rows, w[:, pl.ds(column, width)]).astype(outs[i].dtype)
 
 
 def out_stage(me, orow, got, w, n_line, other_core, n_pool, req, cr):
@@ -530,10 +519,9 @@
     return pl.pallas_call(
         functools.partial(out_kernel, n_line, other_core, n_pool, req, cr),
         out_shape=shapes,
-        in_specs=[SMEM, VMEM] + [VMEM] * len(got) + [ANY],
+        in_specs=[SMEM] + [VMEM] * (len(got) + 2),
         out_specs=[VMEM] * len(shapes),
-        scratch_shapes=[pltpu.VMEM((n_line, depth, width), BF16), pltpu.SemaphoreType.DMA((n_line,))],
-        compiler_params=params(32),
+        compiler_params=params(16),
         cost_estimate=cost(tokens * depth * total, depth * total),
     )(me, orow, *got, w)
 
@@ -560,8 +548,7 @@
     n_pool = lax.axis_size("pool")
     n_tensor = lax.axis_size("tensor")
     n_line = n_tensor // 2
-    rank = lax.axis_index("tensor").astype(jnp.int32)
-    me = jnp.stack([lax.axis_index("pool").astype(jnp.int32), rank])
+    me = jnp.stack([lax.axis_index(axis).astype(jnp.int32) for axis in ("pool", "tensor")])
     req = hidden.shape[0] // DRAFT
     share = req // n_pool
     capacity = share + share // 2
@@ -583,21 +570,26 @@
             lax.ppermute(parts[s], "pool", [((i + s) % n_pool, i) for i in range(n_pool)]) for s in range(1, n_pool)
         ]
 
-    bc_sent = project(me, orow, hidden, w_bc, w_dt, n_pool, req, cr)
+    bc_sent = project(me, orow, hidden, w_bc, w_dt.T, n_pool, req, cr)
     bc_got = to_owner(bc_sent)
     x_sent = project(me, orow, hidden, w_x, None, n_pool, req, cr)
     x_got = to_owner(x_sent)
-    act, dt, new_conv_bc = bc_stage(
-        me, orow, srow, arow, bc_got, conv_pool_bc, conv_bc, head_local, n_pool, req, cr
+    bc_got, _ = lax.optimization_barrier((bc_got, x_sent))
+    plan = exchange_plan(n_tensor, w_bc.shape[1], span)
+    stage = bc_stage(
+        me, orow, srow, arow, bc_got, conv_pool_bc, conv_bc, head_local, plan, span, n_pool, req, cr
     )
-    b, c = exchange(act, n_tensor, span, rank)
-    y, m, w, d = mix_stage(me, orow, srow, arow, b, c, dt, row(dt_bias), row(a_log), ssm_pool)
+    dt, new_conv_bc, pieces = stage[0], stage[1], list(stage[2:])
+    for i in range(1, len(plan)):
+        pieces[i] = lax.ppermute(pieces[i], "tensor", [(e[0], e[1]) for e in plan[i]])
+    y, m, w, d, b = mix_stage(me, orow, srow, arow, pieces, dt, row(dt_bias), row(a_log), ssm_pool, plan)
     stage = x_stage(
         me, orow, srow, arow, x_got, conv_pool_x, conv_x, y, m, row(d_skip), row(norm_gain), n_pool, req, cr
     )
     normed_sent, (x, new_conv_x) = stage[:n_pool], stage[n_pool:]
     normed_got = to_requester(normed_sent)
     new_pool = state_stage(d, x, w, b, ssm_pool)
+    normed_got, _ = lax.optimization_barrier((normed_got, new_pool))
     sends = out_stage(me, orow, normed_got, w_out, n_line, True, n_pool, req, cr)
     sends, normed = sends[:n_line], sends[n_line]
     swap = [(i, i ^ 1) for i in range(n_tensor)]

time: 89.4 us -> 61.9 us (0.69)
  local copies, waits for them, and re-layouts: 18.9 us -> 0.74 us
  Pallas kernels: 31.5 us -> 24.8 us
  waiting for transfers between devices: 9.22 us -> 14 us
  between operations: 5.63 us -> 0.95 us
  other arithmetic: 2.62 us -> 0.93 us
  starting transfers between devices: 21.1 us -> 20.2 us
    unnamed x59 -> x32, local copies, waits for them, and re-layouts: 14.7 us -> 0.74 us
    ppermute x1, waiting for transfers between devices: 0.01 us -> 7.17 us  [body(): arrived.append(lax.ppermute(ahead, 'tensor', pairs))]
    ppermute x3, waiting for transfers between devices: 8.48 us -> 3.2 us  [to_requester(): lax.ppermute(parts[s], 'pool', [((i + s) % n_pool, i) for i in range(n_po...]
    dynamic_slice x8 -> x0, local copies, waits for them, and re-layouts: 4.18 us -> none  [the longest x3 1.76 us: part_of(): offset = jnp.asarray(table, jnp.int32)[rank] * piece]
    ppermute x2, waiting for transfers between devices: 0.01 us -> 3.65 us  [body(): lax.ppermute(pieces[i], 'tensor', [(e[0], e[1]) for e in plan[i]])]
    pallas_call x1, Pallas kernels: 7.57 us -> 4.65 us  [state_stage(): pl.pallas_call(state_kernel, out_shape=jax.ShapeDtypeStruct(pool.shape, B...]
    pallas_call x2, Pallas kernels: 7.32 us -> 4.78 us  [the longest x1 2.75 us: mix_stage(): pl.pallas_call(functools.partial(mix_kernel, kinds), out_shape=[jax.Shape...]
    select_n x1 -> x0, other arithmetic: 1.69 us -> none  [exchange(): sides[kind] = jnp.where(got == kind, moved, sides[kind])]
  transfers between devices with their start and end apart: 14 -> 14, of which waited for: 4 -> 3; matrix products, arithmetic and copies ran while one was open for 7% -> 0% of each run, Pallas kernels for 21% -> 25%
where the time goes in v2:
time: 61.9 us; the launch traced here: 61.7 us
  Pallas kernels  24.8 us (40%)
  starting transfers between devices  20.2 us (33%)
  waiting for transfers between devices  14 us (23%)
  between operations  0.95 us (2%)
  other arithmetic  0.93 us (2%)
  local copies, waits for them, and re-layouts  0.74 us (1%)
    ppermute x6, starting transfers between devices, to_owner(): lax.ppermute(parts[s], 'pool', [(i, (i + s) % n_pool) for i in range(n_po...  10.9 us
    pallas_call x2, Pallas kernels, project(): pl.pallas_call(functools.partial(project_kernel, n_pool, req, cr, chunk,...  9.07 us
    ppermute x1, waiting for transfers between devices, body(): arrived.append(lax.ppermute(ahead, 'tensor', pairs))  7.17 us
    pallas_call x1, Pallas kernels, state_stage(): pl.pallas_call(state_kernel, out_shape=jax.ShapeDtypeStruct(pool.shape, B...  4.65 us
    ppermute x3, starting transfers between devices, to_requester(): lax.ppermute(parts[s], 'pool', [((i + s) % n_pool, i) for i in range(n_po...  4.05 us
    ppermute x2, waiting for transfers between devices, body(): lax.ppermute(pieces[i], 'tensor', [(e[0], e[1]) for e in plan[i]])  3.65 us
    pallas_call x1, Pallas kernels, x_stage(): pl.pallas_call(functools.partial(x_kernel, n_pool, req, cr), out_shape=[j...  3.47 us
    ppermute x3, waiting for transfers between devices, to_requester(): lax.ppermute(parts[s], 'pool', [((i + s) % n_pool, i) for i in range(n_po...  3.2 us
  transfers between devices with their start and end apart: 14, of which 3 were waited for; matrix products, arithmetic and copies ran while one was open for 0% of the time, Pallas kernels for 25%

profile of v2, /device:TPU:0, one launch (start us, length us, event | category | flops | bytes accessed | tf_op | source)
XLA Modules:
  0.0 61.7 jit_solution(7924863295448110666)
XLA Ops:
  0.6 0.1 pad_add_fusion.refs_0_.me_ref
  0.7 0.7 %copy-done.2 = s32[64]{0:T(128)S(1)} copy-done((s32[64]{0:T(128)S(1)}, s32[64]{0:T(128)}, u32[]{:S(2)}) %copy-start.2) | copy-done | bytes 280
  1.4 4.1 %shard_map.193 = (bf16[48,640]{1,0:T(8,128)(2,1)S(1)}, bf16[48,640]{1,0:T(8,128)(2,1)S(1)}, bf16[48,640]{1,0:T(8,128)(2,1)S(1)}, bf16[48,640]{1,0:T(8,128)(2,1)S(1)}) custom-call(s32[2]{0:T(128)S(1)} %pad_add_fusion.refs_0_.me_ref, s32[1,64]{1,0:T(1,128)S(1)} %bitcast.14, bf16[128,4096]{1,0:T(8,128)(2,1)} %refs_2_.3, bf16[4096,512]{1,0:T(8,128)(2,1)} %refs_3_.3, ...), custom_call_target="tpu_custom_call" | custom-call | flops 536870912 | bytes 6291456 | tf_op jit(solution)/shard_map/pallas_call | solution.py:234
  5.4 3.1 %collective-permute-start.3 = (bf16[48,640]{1,0:T(8,128)(2,1)S(1)}, bf16[48,640]{1,0:T(8,128)(2,1)S(1)}, u32[]{:S(2)}, u32[]{:S(2)}) collective-permute-start(bf16[48,640]{1,0:T(8,128)(2,1)S(1)} %get-tuple-element.46), channel_id=1, source_target_pairs={{0,4},{4,8},{8,12},{12,0},{1,5},{5,9},{9,13},{13,1},{2,6},{6,10},{... | collective-permute-start | bytes 184328 | tf_op jit(solution)/shard_map/ppermute | solution.py:565
  8.5 2.6 %collective-permute-start.4 = (bf16[48,640]{1,0:T(8,128)(2,1)S(1)}, bf16[48,640]{1,0:T(8,128)(2,1)S(1)}, u32[]{:S(2)}, u32[]{:S(2)}) collective-permute-start(bf16[48,640]{1,0:T(8,128)(2,1)S(1)} %get-tuple-element.47), channel_id=1, source_target_pairs={{0,8},{4,12},{8,0},{12,4},{1,9},{5,13},{9,1},{13,5},{2,10},{6,14},... | collective-permute-start | bytes 184328 | tf_op jit(solution)/shard_map/ppermute | solution.py:565
  11.1 0.0 copy-start.7
  11.1 0.0 slice-start.3
  11.1 0.0 copy-start.9
  11.2 0.0 copy-start.10
  11.2 1.4 %collective-permute-start.5 = (bf16[48,640]{1,0:T(8,128)(2,1)S(1)}, bf16[48,640]{1,0:T(8,128)(2,1)S(1)}, u32[]{:S(2)}, u32[]{:S(2)}) collective-permute-start(bf16[48,640]{1,0:T(8,128)(2,1)S(1)} %get-tuple-element.48), channel_id=1, source_target_pairs={{0,12},{4,0},{8,4},{12,8},{1,13},{5,1},{9,5},{13,9},{2,14},{6,2},{... | collective-permute-start | bytes 184328 | tf_op jit(solution)/shard_map/ppermute | solution.py:565
  12.6 5.0 %shard_map.192 = (bf16[48,1024]{1,0:T(8,128)(2,1)S(1)}, bf16[48,1024]{1,0:T(8,128)(2,1)S(1)}, bf16[48,1024]{1,0:T(8,128)(2,1)S(1)}, bf16[48,1024]{1,0:T(8,128)(2,1)S(1)}) custom-call(s32[2]{0:T(128)S(1)} %pad_add_fusion.refs_0_.me_ref, s32[1,64]{1,0:T(1,128)S(1)} %bitcast.15, bf16[128,4096]{1,0:T(8,128)(2,1)} %refs_2_.3, bf16[4096,1024]{1,0:T(8,128)(2,1)} %refs_3_.2), custom_call_target="tpu_custom_call" | custom-call | flops 1073741824 | bytes 9437184 | tf_op jit(solution)/shard_map/pallas_call | solution.py:234
  17.6 0.0 copy-start
  17.6 0.0 copy-start.3
  17.6 0.0 copy-start.4
  17.6 0.0 copy-start.8
  17.6 0.0 copy-start.11
  17.6 0.7 %collective-permute-start = (bf16[48,1024]{1,0:T(8,128)(2,1)S(1)}, bf16[48,1024]{1,0:T(8,128)(2,1)S(1)}, u32[]{:S(2)}, u32[]{:S(2)}) collective-permute-start(bf16[48,1024]{1,0:T(8,128)(2,1)S(1)} %get-tuple-element.42), channel_id=1, source_target_pairs={{0,4},{4,8},{8,12},{12,0},{1,5},{5,9},{9,13},{13,1},{2,6},{6,10},{... | collective-permute-start | bytes 294920 | tf_op jit(solution)/shard_map/ppermute | solution.py:565
  18.4 0.8 %collective-permute-start.1 = (bf16[48,1024]{1,0:T(8,128)(2,1)S(1)}, bf16[48,1024]{1,0:T(8,128)(2,1)S(1)}, u32[]{:S(2)}, u32[]{:S(2)}) collective-permute-start(bf16[48,1024]{1,0:T(8,128)(2,1)S(1)} %get-tuple-element.43), channel_id=1, source_target_pairs={{0,8},{4,12},{8,0},{12,4},{1,9},{5,13},{9,1},{13,5},{2,10},{6,14},... | collective-permute-start | bytes 294920 | tf_op jit(solution)/shard_map/ppermute | solution.py:565
  19.1 0.0 collective-permute-done.3.refs_1_
  19.1 2.4 %collective-permute-start.2 = (bf16[48,1024]{1,0:T(8,128)(2,1)S(1)}, bf16[48,1024]{1,0:T(8,128)(2,1)S(1)}, u32[]{:S(2)}, u32[]{:S(2)}) collective-permute-start(bf16[48,1024]{1,0:T(8,128)(2,1)S(1)} %get-tuple-element.44), channel_id=1, source_target_pairs={{0,12},{4,0},{8,4},{12,8},{1,13},{5,1},{9,5},{13,9},{2,14},{6,2},{... | collective-permute-start | bytes 294920 | tf_op jit(solution)/shard_map/ppermute | solution.py:565
  21.5 0.0 collective-permute-done.4.refs_2_
  21.5 0.0 collective-permute-done.5.refs_3_
  21.6 2.0 %shard_map.194 = (f32[144,16]{1,0:T(8,128)S(1)}, bf16[18,3,512]{2,1,0:T(4,128)(2,1)}, bf16[144,256]{1,0:T(8,128)(2,1)S(1)}, bf16[144,256]{1,0:T(8,128)(2,1)S(1)}, bf16[144,256]{1,0:T(8,128)(2,1)S(1)}) custom-call(s32[2]{0:T(128)S(1)} %pad_add_fusion.refs_0_.me_ref, s32[1,64]{1,0:T(1,128)S(1)} %bitcast.16, s32[1,64]{1,0:T(1,128)S(1)} %bitcast.21, ...), custom_call_target="tpu_custom_call" | custom-call | flops 2000000 | bytes 1000000 | tf_op jit(solution)/shard_map/pallas_call | solution.py:309
  23.6 1.9 %collective-permute-start.6 = (bf16[144,256]{1,0:T(8,128)(2,1)S(1)}, bf16[144,256]{1,0:T(8,128)(2,1)S(1)}, u32[]{:S(2)}, u32[]{:S(2)}) collective-permute-start(bf16[144,256]{1,0:T(8,128)(2,1)S(1)} %get-tuple-element.54), channel_id=1, source_target_pairs={{2,0},{0,1},{1,2},{6,4},{4,5},{5,6},{10,8},{8,9},{9,10},{14,12},{1... | collective-permute-start | bytes 221192 | tf_op jit(solution)/shard_map/ppermute | solution.py:584
  25.5 0.7 %collective-permute-start.7 = (bf16[144,256]{1,0:T(8,128)(2,1)S(1)}, bf16[144,256]{1,0:T(8,128)(2,1)S(1)}, u32[]{:S(2)}, u32[]{:S(2)}) collective-permute-start(bf16[144,256]{1,0:T(8,128)(2,1)S(1)} %get-tuple-element.55), channel_id=1, source_target_pairs={{2,1},{3,2},{1,3},{6,5},{7,6},{5,7},{10,9},{11,10},{9,11},{14,13},... | collective-permute-start | bytes 221192 | tf_op jit(solution)/shard_map/ppermute | solution.py:584
  26.2 3.6 %collective-permute-done.6.refs_1_ = bf16[144,256]{1,0:T(8,128)(2,1)S(1)} collective-permute-done((bf16[144,256]{1,0:T(8,128)(2,1)S(1)}, bf16[144,256]{1,0:T(8,128)(2,1)S(1)}, u32[]{:S(2)}, u32[]{:S(2)}) %collective-permute-start.6) | collective-permute-done | bytes 73760 | tf_op jit(solution)/shard_map/ppermute | solution.py:584
  29.8 0.0 collective-permute-done.7.refs_2_
  29.9 0.0 slice-start
  29.9 2.7 %shard_map.195 = (f32[144,1024]{1,0:T(8,128)S(1)}, bf16[16,144,144]{2,1,0:T(8,128)(2,1)S(1)}, f32[144,16]{1,0:T(8,128)S(1)}, f32[18,16]{1,0:T(8,128)S(1)}, bf16[144,256]{1,0:T(8,128)(2,1)S(1)}) custom-call(s32[2]{0:T(128)S(1)} %pad_add_fusion.refs_0_.me_ref, s32[1,64]{1,0:T(1,128)S(1)} %bitcast.17, s32[1,64]{1,0:T(1,128)S(1)} %bitcast.22, ...), custom_call_target="tpu_custom_call" | custom-call | flops 37748736 | bytes 4718592 | tf_op jit(solution)/shard_map/pallas_call | solution.py:391
  32.6 0.0 collective-permute-done.refs_1_
  32.6 0.0 collective-permute-done.1.refs_2_
  32.7 0.0 collective-permute-done.2.refs_3_
  32.7 3.5 %shard_map.196 = (bf16[48,1024]{1,0:T(8,128)(2,1)S(1)}, bf16[48,1024]{1,0:T(8,128)(2,1)S(1)}, bf16[48,1024]{1,0:T(8,128)(2,1)S(1)}, bf16[48,1024]{1,0:T(8,128)(2...) custom-call(s32[2]{0:T(128)S(1)} %pad_add_fusion.refs_0_.me_ref, s32[1,64]{1,0:T(1,128)S(1)} %bitcast.18, ...), custom_call_target="tpu_custom_call" | custom-call | flops 42467328 | bytes 4000000 | tf_op jit(solution)/shard_map/pallas_call | solution.py:439
  36.2 1.2 %collective-permute-start.8 = (bf16[48,1024]{1,0:T(8,128)(2,1)S(1)}, bf16[48,1024]{1,0:T(8,128)(2,1)S(1)}, u32[]{:S(2)}, u32[]{:S(2)}) collective-permute-start(bf16[48,1024]{1,0:T(8,128)(2,1)S(1)} %get-tuple-element.60), channel_id=1, source_target_pairs={{4,0},{8,4},{12,8},{0,12},{5,1},{9,5},{13,9},{1,13},{6,2},{10,6},{... | collective-permute-start | bytes 294920 | tf_op jit(solution)/shard_map/ppermute | solution.py:570
  37.4 0.8 %collective-permute-start.9 = (bf16[48,1024]{1,0:T(8,128)(2,1)S(1)}, bf16[48,1024]{1,0:T(8,128)(2,1)S(1)}, u32[]{:S(2)}, u32[]{:S(2)}) collective-permute-start(bf16[48,1024]{1,0:T(8,128)(2,1)S(1)} %get-tuple-element.61), channel_id=1, source_target_pairs={{8,0},{12,4},{0,8},{4,12},{9,1},{13,5},{1,9},{5,13},{10,2},{14,6},... | collective-permute-start | bytes 294920 | tf_op jit(solution)/shard_map/ppermute | solution.py:570
  38.2 2.0 %collective-permute-start.10 = (bf16[48,1024]{1,0:T(8,128)(2,1)S(1)}, bf16[48,1024]{1,0:T(8,128)(2,1)S(1)}, u32[]{:S(2)}, u32[]{:S(2)}) collective-permute-start(bf16[48,1024]{1,0:T(8,128)(2,1)S(1)} %get-tuple-element.62), channel_id=1, source_target_pairs={{12,0},{0,4},{4,8},{8,12},{13,1},{1,5},{5,9},{9,13},{14,2},{2,6},{... | collective-permute-start | bytes 294920 | tf_op jit(solution)/shard_map/ppermute | solution.py:570
  40.3 4.7 %shard_map.197 = bf16[18,16,64,128]{3,2,1,0:T(8,128)(2,1)} custom-call(f32[18,16]{1,0:T(8,128)S(1)} %get-tuple-element.63.d_ref, f32[144,1024]{1,0:T(8,128)S(1)} %get-tuple-element.64.x_ref, f32[144,16]{1,0:T(8,128)S(1)} %get-tuple-element.65.w_ref, bf16[144,256]{1,0:T(8,128)(2,1)S(1)} %get-tuple-element.66.b_ref, bf16[18,16,64,128]{3,2,1,0:T(8,128)(2,1)S(1)} %bitcast.13), custom_call_target="tpu_custom_call" | custom-call | flops 75497472 | bytes 9437184 | tf_op jit(solution)/shard_map/pallas_call | solution.py:476
  44.9 0.0 collective-permute-done.8.refs_1_
  44.9 3.2 %collective-permute-done.9.refs_2_ = bf16[48,1024]{1,0:T(8,128)(2,1)S(1)} collective-permute-done((bf16[48,1024]{1,0:T(8,128)(2,1)S(1)}, bf16[48,1024]{1,0:T(8,128)(2,1)S(1)}, u32[]{:S(2)}, u32[]{:S(2)}) %collective-permute-start.9) | collective-permute-done | bytes 98336 | tf_op jit(solution)/shard_map/ppermute | solution.py:570
  48.1 0.0 collective-permute-done.10.refs_3_
  48.1 1.5 %shard_map.198 = (bf16[128,1024]{1,0:T(8,128)(2,1)S(1)}, bf16[128,1024]{1,0:T(8,128)(2,1)S(1)}, bf16[128,1024]{1,0:T(8,128)(2,1)S(1)}) custom-call(s32[2]{0:T(128)S(1)} %pad_add_fusion.refs_0_.me_ref, s32[1,64]{1,0:T(1,128)S(1)} %bitcast.19, bf16[48,1024]{1,0:T(8,128)(2,1)S(1)} %get-tuple-element.67.refs_0_, ...), custom_call_target="tpu_custom_call" | custom-call | flops 536870912 | bytes 4194304 | tf_op jit(solution)/shard_map/pallas_call | solution.py:519
  49.7 1.0 %collective-permute-start.12 = (bf16[128,1024]{1,0:T(8,128)(2,1)S(1)}, bf16[128,1024]{1,0:T(8,128)(2,1)S(1)}, u32[]{:S(2)}, u32[]{:S(2)}) collective-permute-start(bf16[128,1024]{1,0:T(8,128)(2,1)S(1)} %get-tuple-element.75), channel_id=1, source_target_pairs={{0,1},{1,0},{2,3},{3,2},{4,5},{5,4},{6,7},{7,6},{8,9},{9,8},{10,11... | collective-permute-start | bytes 786440 | tf_op jit(solution)/shard_map/ppermute | solution.py:597
  50.7 0.1 collective-permute-start.11
  50.8 1.3 %shard_map.199 = (f32[128,1024]{1,0:T(8,128)S(1)}, f32[128,1024]{1,0:T(8,128)S(1)}) custom-call(s32[2]{0:T(128)S(1)} %pad_add_fusion.refs_0_.me_ref, s32[1,64]{1,0:T(1,128)S(1)} %bitcast.20, bf16[128,1024]{1,0:T(8,128)(2,1)S(1)} %get-tuple-element.71.refs_0_, bf16[1024,4096]{1,0:T(8,128)(2,1)S(1)} %bitcast.11), custom_call_target="tpu_custom_call" | custom-call | flops 536870912 | bytes 4194304 | tf_op jit(solution)/shard_map/pallas_call | solution.py:519
  52.1 0.1 add_convert_fusion.1
  52.2 1.5 %collective-permute-start.13 = (bf16[128,1024]{1,0:T(8,128)(2,1)S(1)}, bf16[128,1024]{1,0:T(8,128)(2,1)S(1)}, u32[]{:S(2)}, u32[]{:S(2)}) collective-permute-start(bf16[128,1024]{1,0:T(8,128)(2,1)S(1)} %add_convert_fusion.1), channel_id=1, source_target_pairs={{0,2},{1,3},{2,0},{3,1},{4,6},{5,7},{6,4},{7,5},{8,10},{9,11},{10,... | collective-permute-start | bytes 786440 | tf_op jit(solution)/shard_map/ppermute | solution.py:604
  53.7 7.2 %collective-permute-done.13 = bf16[128,1024]{1,0:T(8,128)(2,1)S(1)} collective-permute-done((bf16[128,1024]{1,0:T(8,128)(2,1)S(1)}, bf16[128,1024]{1,0:T(8,128)(2,1)S(1)}, u32[]{:S(2)}, u32[]{:S(2)}) %collective-permute-start.13) | collective-permute-done | bytes 262176 | tf_op jit(solution)/shard_map/ppermute | solution.py:604
  60.9 0.8 %add_convert_fusion = bf16[128,1024]{1,0:T(8,128)(2,1)} fusion(bf16[128,1024]{1,0:T(8,128)(2,1)S(1)} %collective-permute-done.13, f32[128,1024]{1,0:T(8,128)S(1)} %get-tuple-element.72, bf16[128,1024]{1,0:T(8,128)(2,1)S(1)} %collective-permute-done.11), kind=kLoop, calls=%fused_computation | loop fusion | flops 655360 | bytes 1310720 | tf_op jit(solution)/shard_map/convert_element_type | solution.py:608
  (25 shorter events, 0.0 us)
Async XLA Ops:
  0.7 0.7 %copy-start.2 = (s32[64]{0:T(128)S(1)}, s32[64]{0:T(128)}, u32[]{:S(2)}) copy-start(s32[64]{0:T(128)} %param.31) | copy-start | bytes 772
  5.4 13.7 %collective-permute-start.3 = (bf16[48,640]{1,0:T(8,128)(2,1)S(1)}, bf16[48,640]{1,0:T(8,128)(2,1)S(1)}, u32[]{:S(2)}, u32[]{:S(2)}) collective-permute-start(bf16[48,640]{1,0:T(8,128)(2,1)S(1)} %get-tuple-element.46), channel_id=1, source_target_pairs={{0,4},{4,8},{8,12},{12,0},{1,5},{5,9},{9,13},{13,1},{2,6},{6,10},{... | collective-permute-start | bytes 184328 | tf_op jit(solution)/shard_map/ppermute | solution.py:565
  8.5 13.0 %collective-permute-start.4 = (bf16[48,640]{1,0:T(8,128)(2,1)S(1)}, bf16[48,640]{1,0:T(8,128)(2,1)S(1)}, u32[]{:S(2)}, u32[]{:S(2)}) collective-permute-start(bf16[48,640]{1,0:T(8,128)(2,1)S(1)} %get-tuple-element.47), channel_id=1, source_target_pairs={{0,8},{4,12},{8,0},{12,4},{1,9},{5,13},{9,1},{13,5},{2,10},{6,14},... | collective-permute-start | bytes 184328 | tf_op jit(solution)/shard_map/ppermute | solution.py:565
  11.1 18.7 %slice-start.2 = ((s8[4718592]{0:T(1024)(128)(4,1)}), s8[4194304]{0:T(1024)(128)(4,1)S(1)}, s32[]{:S(2)}) async-start(s8[4718592]{0:T(1024)(128)(4,1)} %bitcast.12), calls=%async_computation.2 | async-start | bytes 8388608
  11.1 10.4 %copy-start.1 = (bf16[18,3,512]{2,1,0:T(4,128)(2,1)S(1)}, bf16[18,3,512]{2,1,0:T(4,128)(2,1)}, u32[]{:S(2)}) copy-start(bf16[18,3,512]{2,1,0:T(4,128)(2,1)} %refs_4_.3) | copy-start | bytes 165892
  11.1 10.4 %copy-start.5 = (f32[4,512]{1,0:T(4,128)S(1)}, f32[4,512]{1,0:T(4,128)}, u32[]{:S(2)}) copy-start(f32[4,512]{1,0:T(4,128)} %refs_5_.2) | copy-start | bytes 24580
  11.1 10.4 %copy-start.6 = (s32[64]{0:T(128)S(1)}, s32[64]{0:T(128)}, u32[]{:S(2)}) copy-start(s32[64]{0:T(128)} %param.32) | copy-start | bytes 772
  11.1 10.4 %copy-start.7 = (s32[64]{0:T(128)S(1)}, s32[64]{0:T(128)}, u32[]{:S(2)}) copy-start(s32[64]{0:T(128)} %param.33) | copy-start | bytes 772
  11.1 18.7 %slice-start.3 = ((s8[4718592]{0:T(1024)(128)(4,1)}), s8[524288]{0:T(1024)(128)(4,1)S(1)}, s32[]{:S(2)}) async-start(s8[4718592]{0:T(1024)(128)(4,1)} %bitcast.12), calls=%async_computation.3 | async-start | bytes 1048576
  11.1 18.7 %copy-start.9 = (f32[16]{0:T(128)S(1)}, f32[16]{0:T(128)}, u32[]{:S(2)}) copy-start(f32[16]{0:T(128)} %param.23) | copy-start | bytes 196
  11.2 18.7 %copy-start.10 = (f32[16]{0:T(128)S(1)}, f32[16]{0:T(128)}, u32[]{:S(2)}) copy-start(f32[16]{0:T(128)} %param.24) | copy-start | bytes 196
  11.2 10.4 %collective-permute-start.5 = (bf16[48,640]{1,0:T(8,128)(2,1)S(1)}, bf16[48,640]{1,0:T(8,128)(2,1)S(1)}, u32[]{:S(2)}, u32[]{:S(2)}) collective-permute-start(bf16[48,640]{1,0:T(8,128)(2,1)S(1)} %get-tuple-element.48), channel_id=1, source_target_pairs={{0,12},{4,0},{8,4},{12,8},{1,13},{5,1},{9,5},{13,9},{2,14},{6,2},{... | collective-permute-start | bytes 184328 | tf_op jit(solution)/shard_map/ppermute | solution.py:565
  17.6 15.1 %copy-start = (bf16[18,3,1024]{2,1,0:T(4,128)(2,1)S(1)}, bf16[18,3,1024]{2,1,0:T(4,128)(2,1)}, u32[]{:S(2)}) copy-start(bf16[18,3,1024]{2,1,0:T(4,128)(2,1)} %refs_4_.4) | copy-start | bytes 331780
  17.6 15.1 %copy-start.3 = (s32[64]{0:T(128)S(1)}, s32[64]{0:T(128)}, u32[]{:S(2)}) copy-start(s32[64]{0:T(128)} %param.31) | copy-start | bytes 772
  17.6 15.1 %copy-start.4 = (f32[4,1024]{1,0:T(4,128)S(1)}, f32[4,1024]{1,0:T(4,128)}, u32[]{:S(2)}) copy-start(f32[4,1024]{1,0:T(4,128)} %refs_5_.3) | copy-start | bytes 49156
  17.6 15.1 %copy-start.8 = (f32[1024]{0:T(1024)S(1)}, f32[1024]{0:T(1024)}, u32[]{:S(2)}) copy-start(f32[1024]{0:T(1024)} %param.26) | copy-start | bytes 12292
  17.6 15.1 %copy-start.11 = (f32[16]{0:T(128)S(1)}, f32[16]{0:T(128)}, u32[]{:S(2)}) copy-start(f32[16]{0:T(128)} %param.25) | copy-start | bytes 196
  17.6 15.0 %collective-permute-start = (bf16[48,1024]{1,0:T(8,128)(2,1)S(1)}, bf16[48,1024]{1,0:T(8,128)(2,1)S(1)}, u32[]{:S(2)}, u32[]{:S(2)}) collective-permute-start(bf16[48,1024]{1,0:T(8,128)(2,1)S(1)} %get-tuple-element.42), channel_id=1, source_target_pairs={{0,4},{4,8},{8,12},{12,0},{1,5},{5,9},{9,13},{13,1},{2,6},{6,10},{... | collective-permute-start | bytes 294920 | tf_op jit(solution)/shard_map/ppermute | solution.py:565
  18.4 14.3 %collective-permute-start.1 = (bf16[48,1024]{1,0:T(8,128)(2,1)S(1)}, bf16[48,1024]{1,0:T(8,128)(2,1)S(1)}, u32[]{:S(2)}, u32[]{:S(2)}) collective-permute-start(bf16[48,1024]{1,0:T(8,128)(2,1)S(1)} %get-tuple-element.43), channel_id=1, source_target_pairs={{0,8},{4,12},{8,0},{12,4},{1,9},{5,13},{9,1},{13,5},{2,10},{6,14},... | collective-permute-start | bytes 294920 | tf_op jit(solution)/shard_map/ppermute | solution.py:565
  19.1 13.5 %collective-permute-start.2 = (bf16[48,1024]{1,0:T(8,128)(2,1)S(1)}, bf16[48,1024]{1,0:T(8,128)(2,1)S(1)}, u32[]{:S(2)}, u32[]{:S(2)}) collective-permute-start(bf16[48,1024]{1,0:T(8,128)(2,1)S(1)} %get-tuple-element.44), channel_id=1, source_target_pairs={{0,12},{4,0},{8,4},{12,8},{1,13},{5,1},{9,5},{13,9},{2,14},{6,2},{... | collective-permute-start | bytes 294920 | tf_op jit(solution)/shard_map/ppermute | solution.py:565
  23.6 6.2 %collective-permute-start.6 = (bf16[144,256]{1,0:T(8,128)(2,1)S(1)}, bf16[144,256]{1,0:T(8,128)(2,1)S(1)}, u32[]{:S(2)}, u32[]{:S(2)}) collective-permute-start(bf16[144,256]{1,0:T(8,128)(2,1)S(1)} %get-tuple-element.54), channel_id=1, source_target_pairs={{2,0},{0,1},{1,2},{6,4},{4,5},{5,6},{10,8},{8,9},{9,10},{14,12},{1... | collective-permute-start | bytes 221192 | tf_op jit(solution)/shard_map/ppermute | solution.py:584
  25.5 4.3 %collective-permute-start.7 = (bf16[144,256]{1,0:T(8,128)(2,1)S(1)}, bf16[144,256]{1,0:T(8,128)(2,1)S(1)}, u32[]{:S(2)}, u32[]{:S(2)}) collective-permute-start(bf16[144,256]{1,0:T(8,128)(2,1)S(1)} %get-tuple-element.55), channel_id=1, source_target_pairs={{2,1},{3,2},{1,3},{6,5},{7,6},{5,7},{10,9},{11,10},{9,11},{14,13},... | collective-permute-start | bytes 221192 | tf_op jit(solution)/shard_map/ppermute | solution.py:584
  29.9 18.2 %slice-start = ((s8[8388608]{0:T(1024)(128)(4,1)}), s8[4194304]{0:T(1024)(128)(4,1)S(1)}, s32[]{:S(2)}) async-start(s8[8388608]{0:T(1024)(128)(4,1)} %bitcast.10), calls=%async_computation | async-start | bytes 8388608
  36.2 8.7 %collective-permute-start.8 = (bf16[48,1024]{1,0:T(8,128)(2,1)S(1)}, bf16[48,1024]{1,0:T(8,128)(2,1)S(1)}, u32[]{:S(2)}, u32[]{:S(2)}) collective-permute-start(bf16[48,1024]{1,0:T(8,128)(2,1)S(1)} %get-tuple-element.60), channel_id=1, source_target_pairs={{4,0},{8,4},{12,8},{0,12},{5,1},{9,5},{13,9},{1,13},{6,2},{10,6},{... | collective-permute-start | bytes 294920 | tf_op jit(solution)/shard_map/ppermute | solution.py:570
  37.4 10.7 %collective-permute-start.9 = (bf16[48,1024]{1,0:T(8,128)(2,1)S(1)}, bf16[48,1024]{1,0:T(8,128)(2,1)S(1)}, u32[]{:S(2)}, u32[]{:S(2)}) collective-permute-start(bf16[48,1024]{1,0:T(8,128)(2,1)S(1)} %get-tuple-element.61), channel_id=1, source_target_pairs={{8,0},{12,4},{0,8},{4,12},{9,1},{13,5},{1,9},{5,13},{10,2},{14,6},... | collective-permute-start | bytes 294920 | tf_op jit(solution)/shard_map/ppermute | solution.py:570
  38.2 9.9 %collective-permute-start.10 = (bf16[48,1024]{1,0:T(8,128)(2,1)S(1)}, bf16[48,1024]{1,0:T(8,128)(2,1)S(1)}, u32[]{:S(2)}, u32[]{:S(2)}) collective-permute-start(bf16[48,1024]{1,0:T(8,128)(2,1)S(1)} %get-tuple-element.62), channel_id=1, source_target_pairs={{12,0},{0,4},{4,8},{8,12},{13,1},{1,5},{5,9},{9,13},{14,2},{2,6},{... | collective-permute-start | bytes 294920 | tf_op jit(solution)/shard_map/ppermute | solution.py:570
  40.3 7.9 %slice-start.1 = ((s8[8388608]{0:T(1024)(128)(4,1)}), s8[4194304]{0:T(1024)(128)(4,1)S(1)}, s32[]{:S(2)}) async-start(s8[8388608]{0:T(1024)(128)(4,1)} %bitcast.10), calls=%async_computation.1 | async-start | bytes 8388608
  49.7 2.4 %collective-permute-start.12 = (bf16[128,1024]{1,0:T(8,128)(2,1)S(1)}, bf16[128,1024]{1,0:T(8,128)(2,1)S(1)}, u32[]{:S(2)}, u32[]{:S(2)}) collective-permute-start(bf16[128,1024]{1,0:T(8,128)(2,1)S(1)} %get-tuple-element.75), channel_id=1, source_target_pairs={{0,1},{1,0},{2,3},{3,2},{4,5},{5,4},{6,7},{7,6},{8,9},{9,8},{10,11... | collective-permute-start | bytes 786440 | tf_op jit(solution)/shard_map/ppermute | solution.py:597
  50.7 3.0 %collective-permute-start.11 = (bf16[128,1024]{1,0:T(8,128)(2,1)S(1)}, bf16[128,1024]{1,0:T(8,128)(2,1)S(1)}, u32[]{:S(2)}, u32[]{:S(2)}) collective-permute-start(bf16[128,1024]{1,0:T(8,128)(2,1)S(1)} %get-tuple-element.73), channel_id=1, source_target_pairs={{0,1},{1,0},{2,3},{3,2},{4,5},{5,4},{6,7},{7,6},{8,9},{9,8},{10,11... | collective-permute-start | bytes 786440 | tf_op jit(solution)/shard_map/ppermute | solution.py:597
  52.2 8.7 %collective-permute-start.13 = (bf16[128,1024]{1,0:T(8,128)(2,1)S(1)}, bf16[128,1024]{1,0:T(8,128)(2,1)S(1)}, u32[]{:S(2)}, u32[]{:S(2)}) collective-permute-start(bf16[128,1024]{1,0:T(8,128)(2,1)S(1)} %add_convert_fusion.1), channel_id=1, source_target_pairs={{0,2},{1,3},{2,0},{3,1},{4,6},{5,7},{6,4},{7,5},{8,10},{9,11},{10,... | collective-permute-start | bytes 786440 | tf_op jit(solution)/shard_map/ppermute | solution.py:604

commit v3 on v2

v3 whole, which is shorter than its diff:
```python
import functools

import jax
import jax.numpy as jnp
from jax import lax
from jax.experimental import pallas as pl
from jax.experimental.pallas import tpu as pltpu
from jax.sharding import PartitionSpec as P

HEADS = 64
HEAD_DIM = 64
STATE = 128
GROUPS = 8
DRAFT = 8
SHIFT = 3
EPS = 1e-05
FAR = 4096.0

F32 = jnp.float32
BF16 = jnp.bfloat16
ANY = pl.BlockSpec(memory_space=pl.ANY)
HBM = pl.BlockSpec(memory_space=pltpu.HBM)
VMEM = pl.BlockSpec(memory_space=pltpu.VMEM)
SMEM = pl.BlockSpec(memory_space=pltpu.SMEM)


def params(mib, **more):
    return pltpu.CompilerParams(vmem_limit_bytes=mib * 2**20, **more)


def cost(flops, moved):
    return pl.CostEstimate(flops=int(flops), bytes_accessed=int(moved), transcendentals=0)


def iota(shape, dim):
    return lax.broadcasted_iota(jnp.int32, shape, dim)


def dot(a, b):
    return jnp.dot(a, b, preferred_element_type=F32)


def dot_t(a, b):
    return lax.dot_general(a, b, (((1,), (1,)), ((), ())), preferred_element_type=F32)


def as_col(row):
    n = row.shape[1]
    eye = iota((n, n), 0) == iota((n, n), 1)
    return jnp.sum(jnp.where(eye, jnp.broadcast_to(row, (n, n)), 0.0), axis=1, keepdims=True)


def wrap(value, n):
    return jnp.where(value < 0, value + n, value)


def block_shift(req):
    return req.bit_length() - 1


def ranks(orow, ocol, req):
    n = orow.shape[1]
    sub, lane = iota((n, n), 0), iota((n, n), 1)
    sh = block_shift(req)
    same = (ocol == orow) & ((sub >> sh) == (lane >> sh))
    row = jnp.sum(jnp.where(same & (sub < lane), 1.0, 0.0), axis=0, keepdims=True)
    col = jnp.sum(jnp.where(same & (lane < sub), 1.0, 0.0), axis=1, keepdims=True)
    return row, col


def hot(mask):
    return jnp.where(mask, 1.0, 0.0).astype(BF16)


def send_matrix(orow, me, n_pool, req, cr):
    ocol = as_col(orow)
    _, rank_col = ranks(orow, ocol, req)
    total, tokens = orow.shape[1], req * DRAFT
    place_col = wrap(ocol - me.astype(F32), n_pool) * cr + rank_col * DRAFT
    token = iota((total, tokens), 1)
    mine = (iota((total, tokens), 0) - me * req) == (token >> SHIFT)
    place = jnp.sum(jnp.where(mine, jnp.broadcast_to(place_col, (total, tokens)), 0.0), axis=0, keepdims=True)
    place = place + (iota((1, tokens), 1) & (DRAFT - 1)).astype(F32)
    return hot(iota((n_pool * cr, tokens), 0).astype(F32) == place)


def collect_matrix(orow, me, n_pool, req, cr):
    ocol = as_col(orow)
    rank_row, _ = ranks(orow, ocol, req)
    total, tokens = orow.shape[1], req * DRAFT
    place_row = wrap(orow - me.astype(F32), n_pool) * cr + rank_row * DRAFT
    token = iota((tokens, total), 0)
    mine = (iota((tokens, total), 1) - me * req) == (token >> SHIFT)
    place = jnp.sum(jnp.where(mine, jnp.broadcast_to(place_row, (tokens, total)), 0.0), axis=1, keepdims=True)
    place = place + (iota((tokens, 1), 0) & (DRAFT - 1)).astype(F32)
    return hot(iota((tokens, n_pool * cr), 1).astype(F32) == place)


def owner_matrix(orow, srow, me, n_pool, req, cr, slots):
    ocol = as_col(orow)
    rank_row, _ = ranks(orow, ocol, req)
    total, rows = orow.shape[1], slots * DRAFT
    block = (iota((1, total), 1) >> block_shift(req)).astype(F32)
    place_row = wrap(me.astype(F32) - block, n_pool) * cr + rank_row * DRAFT + FAR
    slot = (iota((rows, total), 0) >> SHIFT).astype(F32)
    match = (orow == me.astype(F32)) & (srow == slot)
    place = jnp.sum(jnp.where(match, jnp.broadcast_to(place_row, (rows, total)), 0.0), axis=1, keepdims=True)
    place = place - FAR + (iota((rows, 1), 0) & (DRAFT - 1)).astype(F32)
    return hot(iota((rows, n_pool * cr), 1).astype(F32) == place)


def pack_matrices(orow, srow, me, n_pool, req, cr, slots):
    ocol, scol = as_col(orow), as_col(srow)
    _, rank_col = ranks(orow, ocol, req)
    total, rows, tokens = orow.shape[1], slots * DRAFT, req * DRAFT
    mine = me.astype(F32)
    sub, lane = iota((total, total), 0), iota((total, total), 1)
    index = jnp.sum(jnp.where((orow == mine) & (lane < sub), 1.0, 0.0), axis=1, keepdims=True)
    slot = (iota((total, rows), 1) >> SHIFT).astype(F32)
    match = (ocol == mine) & (scol == slot)
    value = jnp.broadcast_to(index * DRAFT + FAR, (total, rows))
    at = jnp.sum(jnp.where(match, value, 0.0), axis=0, keepdims=True) - FAR
    at = at + (iota((1, rows), 1) & (DRAFT - 1)).astype(F32)
    pack = hot(iota((tokens, rows), 0).astype(F32) == at)
    block = (iota((total, 1), 0) >> block_shift(req)).astype(F32)
    place_col = wrap(mine - block, n_pool) * cr + rank_col * DRAFT + FAR
    match = (ocol == mine) & (index == (iota((total, tokens), 1) >> SHIFT).astype(F32))
    at = jnp.sum(jnp.where(match, jnp.broadcast_to(place_col, (total, tokens)), 0.0), axis=0, keepdims=True) - FAR
    at = at + (iota((1, tokens), 1) & (DRAFT - 1)).astype(F32)
    return pack, hot(iota((n_pool * cr, tokens), 0).astype(F32) == at)


def slot_accepts(orow, srow, arow, me, slots):
    total, rows = orow.shape[1], slots * DRAFT
    slot = (iota((rows, total), 0) >> SHIFT).astype(F32)
    match = (orow == me.astype(F32)) & (srow == slot)
    return jnp.sum(jnp.where(match, jnp.broadcast_to(arow, (rows, total)), 0.0), axis=1, keepdims=True)


def padded_pool(pool, width):
    slots, window, _ = pool.shape
    old = jnp.concatenate([pool.astype(F32), jnp.zeros((slots, DRAFT - window, width), F32)], axis=1)
    return old.reshape(slots * DRAFT, width)


def conv_slots(raw, pool, weight):
    rows, width = raw.shape
    window = pool.shape[1]
    old = padded_pool(pool, width)
    position = iota((rows, width), 0) & (DRAFT - 1)
    summed = weight[window] * raw
    for back in range(1, window + 1):
        new_part = pltpu.roll(raw, back, 0)
        old_part = pltpu.roll(old, (back - window) % rows, 0)
        summed = summed + weight[window - back] * jnp.where(position < back, old_part, new_part)
    return summed


def kept_rows(raw, pool, accepts):
    rows, width = raw.shape
    slots, window, _ = pool.shape
    old = padded_pool(pool, width)
    sub, lane = iota((rows, rows), 0), iota((rows, rows), 1)
    here = (sub >> SHIFT) == (lane >> SHIFT)
    at = (sub & (DRAFT - 1)).astype(F32) + accepts
    source = (lane & (DRAFT - 1)).astype(F32)
    from_old = hot(here & (source == at) & (source < window))
    from_new = hot(here & (source + window == at))
    kept = dot(from_old, old.astype(BF16)) + dot(from_new, raw.astype(BF16))
    return kept.astype(BF16).reshape(slots, DRAFT, width)[:, :window]


def silu(v):
    return v / (1.0 + jnp.exp(-v))


def spread_matrix(heads):
    shape = (heads, heads * HEAD_DIM)
    return hot(iota(shape, 0) == (iota(shape, 1) >> 6))


def spread(values, matrix):
    high = values.astype(BF16)
    low = (values - high.astype(F32)).astype(BF16)
    return dot(high, matrix) + dot(low, matrix)


def dma(pairs, sems, row):
    return [pltpu.make_async_copy(src, dst, sems.at[row, k]) for k, (src, dst) in enumerate(pairs)]


def project_bc_kernel(n_pool, req, cr, chunk, slots, owners, places, takes, hidden, w, w_dt, *refs):
    outs, refs = refs[:n_pool], refs[n_pool:]
    hbuf, send_ref, owner_ref, pack_ref, return_ref, collect_ref, accepts_ref = refs[:7]
    meta_buf, wbuf, dt_buf, sems = refs[7:]
    steps = hidden.shape[1] // chunk
    parts = [pl.ds(k * chunk, chunk) for k in range(steps)]
    copies = list(
        zip(
            dma([(hidden.at[:, p], hbuf.at[:, p]) for p in parts], sems, 0),
            dma([(w.at[p], wbuf.at[p]) for p in parts], sems, 1),
            dma([(w_dt.at[:, p], dt_buf.at[:, p]) for p in parts], sems, 2),
        )
    )
    tables = dma([(v, meta_buf.at[i]) for i, v in enumerate((owners, places, takes))], sems, 3)
    for copy in tables:
        copy.start()
    for group in copies:
        for copy in group:
            copy.start()
    for copy in tables:
        copy.wait()
    me = lax.axis_index("pool").astype(jnp.int32)
    orow, srow, arow = (meta_buf[i].astype(F32) for i in range(3))
    order = send_matrix(orow, me, n_pool, req, cr)
    send_ref[...] = order
    owner_ref[...] = owner_matrix(orow, srow, me, n_pool, req, cr, slots)
    pack_ref[...], return_ref[...] = pack_matrices(orow, srow, me, n_pool, req, cr, slots)
    collect_ref[...] = collect_matrix(orow, me, n_pool, req, cr)
    accepts_ref[...] = slot_accepts(orow, srow, arow, me, slots)
    heads = w_dt.shape[0]
    total, total_dt = None, None
    for k in range(steps):
        for copy in copies[k]:
            copy.wait()
        here = slice(k * chunk, (k + 1) * chunk)
        added, added_dt = dot(hbuf[:, here], wbuf[here]), dot_t(hbuf[:, here], dt_buf[:, here])
        total = added if total is None else total + added
        total_dt = added_dt if total_dt is None else total_dt + added_dt
    width = w.shape[1]
    placed = dot(order, total.astype(BF16)).astype(BF16)
    high = total_dt.astype(BF16)
    low = (total_dt - high.astype(F32)).astype(BF16)
    shape = (heads, 128)
    to_high = hot(iota(shape, 0) == iota(shape, 1))
    to_low = hot(iota(shape, 0) + heads == iota(shape, 1))
    pair = (dot(high, to_high) + dot(low, to_low)).astype(BF16)
    placed_dt = dot(order, pair).astype(BF16)
    for s in range(n_pool):
        outs[s][:, :width] = placed[s * cr : (s + 1) * cr]
        outs[s][:, width:] = placed_dt[s * cr : (s + 1) * cr]


def in_hbm(*arrays):
    return [pltpu.with_memory_space_constraint(v, pltpu.HBM) for v in arrays]


def project_bc(tables, hidden, w, w_dt, slots, n_pool, req, cr):
    tokens, depth = hidden.shape
    chunk = min(512, depth)
    width, rows = w.shape[1], slots * DRAFT
    outs = pl.pallas_call(
        functools.partial(project_bc_kernel, n_pool, req, cr, chunk, slots),
        out_shape=[jax.ShapeDtypeStruct((cr, width + 128), BF16)] * n_pool
        + [
            jax.ShapeDtypeStruct((tokens, depth), BF16),
            jax.ShapeDtypeStruct((n_pool * cr, tokens), BF16),
            jax.ShapeDtypeStruct((rows, n_pool * cr), BF16),
            jax.ShapeDtypeStruct((tokens, rows), BF16),
            jax.ShapeDtypeStruct((n_pool * cr, tokens), BF16),
            jax.ShapeDtypeStruct((tokens, n_pool * cr), BF16),
            jax.ShapeDtypeStruct((rows, 1), F32),
        ],
        in_specs=[HBM] * 6,
        out_specs=[VMEM] * (n_pool + 7),
        scratch_shapes=[
            pltpu.VMEM((3,) + tables[0].shape, jnp.int32),
            pltpu.VMEM((depth, width), BF16),
            pltpu.VMEM(w_dt.shape, BF16),
            pltpu.SemaphoreType.DMA((4, max(3, depth // chunk))),
        ],
        compiler_params=params(12),
        cost_estimate=cost(2 * tokens * depth * width, depth * (width + 128 + tokens) * 2),
    )(*in_hbm(*tables, hidden, w, w_dt))
    return outs[:n_pool], outs[n_pool:]


def project_x_kernel(n_pool, cr, chunk, hbuf, w, send_ref, *refs):
    outs, (wbuf, sems) = refs[:n_pool], refs[n_pool:]
    steps = w.shape[0] // chunk
    parts = [pl.ds(k * chunk, chunk) for k in range(steps)]
    copies = dma([(w.at[p], wbuf.at[p]) for p in parts], sems, 0)
    for copy in copies:
        copy.start()
    total = None
    for k in range(steps):
        copies[k].wait()
        here = slice(k * chunk, (k + 1) * chunk)
        added = dot(hbuf[:, here], wbuf[here])
        total = added if total is None else total + added
    placed = dot(send_ref[...], total.astype(BF16)).astype(BF16)
    for s in range(n_pool):
        outs[s][...] = placed[s * cr : (s + 1) * cr]


def project_x(hidden, w, send, n_pool, cr):
    tokens, depth = hidden.shape
    chunk = min(512, depth)
    width = w.shape[1]
    return pl.pallas_call(
        functools.partial(project_x_kernel, n_pool, cr, chunk),
        out_shape=[jax.ShapeDtypeStruct((cr, width), BF16)] * n_pool,
        in_specs=[VMEM, HBM, VMEM],
        out_specs=[VMEM] * n_pool,
        scratch_shapes=[
            pltpu.VMEM((depth, width), BF16),
            pltpu.SemaphoreType.DMA((1, depth // chunk)),
        ],
        compiler_params=params(14),
        cost_estimate=cost(2 * tokens * depth * width, depth * (width + tokens) * 2),
    )(hidden, *in_hbm(w), send)


def pick(rank, table):
    value = jnp.int32(table[0])
    for i in range(1, len(table)):
        value = jnp.where(rank == i, jnp.int32(table[i]), value)
    return value


def exchange_plan(n_tensor, width, span):
    piece = span * STATE
    per_group = HEADS // GROUPS
    head_local = HEADS // n_tensor
    edges, own = [], []
    for target in range(n_tensor):
        first = target * head_local // per_group
        for kind in range(2):
            column = (kind * GROUPS + first) * STATE
            source, part = column // width, column % width // piece
            (own if source == target else edges).append((source, target, kind, part))
    rounds = []
    while edges:
        best = matching(edges, n_tensor)
        rounds.append(best)
        edges = [e for e in edges if e not in best]
    return [own] + rounds


def completed(edges, n):
    pairs = [(e[0], e[1]) for e in edges]
    sources = [i for i in range(n) if i not in [p[0] for p in pairs]]
    targets = [i for i in reversed(range(n)) if i not in [p[1] for p in pairs]]
    return pairs + list(zip(sources, targets))


def matching(edges, n):
    held = {}

    def place(source, seen):
        for edge in edges:
            if edge[0] == source and edge[1] not in seen:
                seen.add(edge[1])
                if edge[1] not in held or place(held[edge[1]][0], seen):
                    held[edge[1]] = edge
                    return True
        return False

    for source in range(n):
        place(source, set())
    return [held[target] for target in sorted(held)]


def bc_kernel(n_pool, parts, owner_ref, *refs):
    got, refs = refs[:n_pool], refs[n_pool:]
    pool_ref, weight_ref, raw_ref = refs[:3]
    outs, act_ref = refs[3:-1], refs[-1]
    width = pool_ref.shape[2]
    rank = lax.axis_index("tensor").astype(jnp.int32)
    raw = dot(owner_ref[...], jnp.concatenate([g[...] for g in got], axis=0))
    raw_ref[...] = raw
    act_ref[...] = silu(conv_slots(raw[:, :width], pool_ref[...], weight_ref[...])).astype(BF16)
    for table, out in zip(parts, outs):
        piece = out.shape[1]
        out[...] = act_ref[:, pl.ds(pl.multiple_of(pick(rank, table) * piece, 128), piece)]


def bc_stage(owner, got, pool, weight, plan, span, n_pool, n_tensor):
    slots, _, width = pool.shape
    rows = slots * DRAFT
    piece = span * STATE
    parts = []
    for one in plan:
        table = [0] * n_tensor
        for source, _, _, part in one:
            table[source] = part
        parts.append(table)
    return pl.pallas_call(
        functools.partial(bc_kernel, n_pool, parts),
        out_shape=[jax.ShapeDtypeStruct((rows, width + 128), F32)]
        + [jax.ShapeDtypeStruct((rows, piece), BF16)] * len(plan),
        in_specs=[VMEM] * (n_pool + 3),
        out_specs=[VMEM] * (1 + len(plan)),
        scratch_shapes=[pltpu.VMEM((rows, width), BF16)],
        compiler_params=params(8),
        cost_estimate=cost(2e6, 1e6),
    )(owner, *got, pool, weight)


def pre_kernel(accepts_ref, raw_ref, bias_ref, alog_ref, pool, m_ref, fade_ref, w_ref, d_ref, states, sems):
    slots, heads = pool.shape[:2]
    rows = slots * DRAFT
    copies = [pltpu.make_async_copy(pool.at[j], states.at[j], sems.at[j]) for j in range(slots)]
    for copy in copies:
        copy.start()
    accepts = accepts_ref[...]
    width = raw_ref.shape[1] - 128
    shape = (128, heads)
    lane, head = iota(shape, 0), iota(shape, 1)
    both = hot((lane == head) | (lane == head + heads))
    x = dot(raw_ref[:, width:].astype(BF16), both) + bias_ref[...]
    step = jnp.maximum(x, 0.0) + jnp.log1p(jnp.exp(-jnp.abs(x)))
    logs = -step * jnp.exp(alog_ref[...])
    position = iota((rows, heads), 0) & (DRAFT - 1)
    for back in (1, 2, 4):
        logs = logs + jnp.where(position >= back, pltpu.roll(logs, back, 0), 0.0)
    last = jnp.where(position.astype(F32) + 1 == accepts, logs, 0.0).reshape(slots, DRAFT, heads)
    last = jnp.broadcast_to(jnp.sum(last, axis=1, keepdims=True), (slots, DRAFT, heads))
    d_ref[...] = jnp.exp(last[:, 0, :])
    last = last.reshape(rows, heads)
    w_ref[...] = jnp.where(position.astype(F32) < accepts, jnp.exp(jnp.minimum(last - logs, 0.0)) * step, 0.0)
    lanes = heads * DRAFT
    shape = (heads, lanes)
    repeat = jnp.where(iota(shape, 0) == (iota(shape, 1) >> SHIFT), 1.0, 0.0)

    def wide(v):
        return jnp.dot(v, repeat, preferred_element_type=F32, precision=lax.Precision.HIGHEST)

    t, u = iota((rows, lanes), 0) & (DRAFT - 1), iota((rows, lanes), 1) & (DRAFT - 1)

    def at_u(v):
        v = jnp.where(t == u, v, 0.0).reshape(slots, DRAFT, lanes)
        return jnp.broadcast_to(jnp.sum(v, axis=1, keepdims=True), (slots, DRAFT, lanes)).reshape(rows, lanes)

    wide_logs = wide(logs)
    fade = jnp.where(u <= t, jnp.exp(jnp.minimum(wide_logs - at_u(wide_logs), 0.0)) * at_u(wide(step)), 0.0)
    fade = fade.astype(BF16)
    shape = (lanes, rows)
    same = (iota(shape, 0) & (DRAFT - 1)) == (iota(shape, 1) & (DRAFT - 1))
    head = iota(shape, 0) >> SHIFT
    for h in range(heads):
        m_ref[h] = dot(fade, hot(same & (head == h))).astype(BF16)
    fade_ref[...] = spread(jnp.exp(logs), spread_matrix(heads))
    for copy in copies:
        copy.wait()


def pre_stage(accepts, raw, bias, a_log, pool):
    slots, heads = pool.shape[:2]
    rows = slots * DRAFT
    return pl.pallas_call(
        pre_kernel,
        out_shape=[
            jax.ShapeDtypeStruct((heads, rows, rows), BF16),
            jax.ShapeDtypeStruct((rows, heads * HEAD_DIM), F32),
            jax.ShapeDtypeStruct((rows, heads), F32),
            jax.ShapeDtypeStruct((slots, heads), F32),
            jax.ShapeDtypeStruct(pool.shape, BF16),
        ],
        in_specs=[VMEM] * 4 + [HBM],
        out_specs=[VMEM] * 5,
        scratch_shapes=[pltpu.SemaphoreType.DMA((slots,))],
        compiler_params=params(20),
        cost_estimate=cost(1e6, 2 * pool.size),
    )(accepts, raw, bias, a_log, *in_hbm(pool))


def mix_kernel(kinds, fade_m_ref, fade_ref, states, *refs):
    pieces, (y_ref, m_ref, b_ref, c_ref) = refs[: len(kinds)], refs[len(kinds) :]
    slots, heads = states.shape[:2]
    span = b_ref.shape[1] // STATE
    per = heads // span
    rank = lax.axis_index("tensor").astype(jnp.int32)
    for side, ref in enumerate((b_ref, c_ref)):
        ref[...] = pieces[0][...]
        for table, piece in zip(kinds, pieces):
            mine = [int(kind == side) for kind in table]
            if any(mine):

                @pl.when(pick(rank, mine) == 1)
                def _(ref=ref, piece=piece):
                    ref[...] = piece[...]

    rows = slots * DRAFT
    here = (iota((rows, rows), 0) >> SHIFT) == (iota((rows, rows), 1) >> SHIFT)
    for g in range(span):
        part = slice(g * STATE, (g + 1) * STATE)
        pair = jnp.where(here, dot_t(c_ref[:, part], b_ref[:, part]), 0.0)
        for h in range(g * per, (g + 1) * per):
            m_ref[h] = (pair * fade_m_ref[h].astype(F32)).astype(BF16)
    c = c_ref[...].astype(F32)
    for j in range(slots):
        here = slice(j * DRAFT, (j + 1) * DRAFT)
        for g in range(span):
            old = states[j, g * per : (g + 1) * per].reshape(per * HEAD_DIM, STATE)
            columns = slice(g * per * HEAD_DIM, (g + 1) * per * HEAD_DIM)
            read = dot_t(c[here, g * STATE : (g + 1) * STATE].astype(BF16), old)
            y_ref[here, columns] = read * fade_ref[here, columns]


def mix_stage(fade_m, fade, states, pieces, plan, n_tensor):
    slots, heads = states.shape[:2]
    rows = slots * DRAFT
    kinds = []
    for one in plan:
        table = [-1] * n_tensor
        for _, target, kind, _ in one:
            table[target] = kind
        kinds.append(table)
    return pl.pallas_call(
        functools.partial(mix_kernel, kinds),
        out_shape=[
            jax.ShapeDtypeStruct((rows, heads * HEAD_DIM), F32),
            jax.ShapeDtypeStruct((heads, rows, rows), BF16),
            jax.ShapeDtypeStruct(pieces[0].shape, BF16),
        ],
        in_specs=[VMEM] * (3 + len(plan)),
        out_specs=[VMEM] * 3,
        scratch_shapes=[pltpu.VMEM(pieces[0].shape, BF16)],
        compiler_params=params(8),
        cost_estimate=cost(2 * rows * heads * HEAD_DIM * STATE, 2 * states.size),
    )(fade_m, fade, states, *pieces)


def x_kernel(n_pool, owner_ref, pack_ref, *refs):
    got, refs = refs[:n_pool], refs[n_pool:]
    pool_ref, weight_ref, y_ref, m_ref, skip_ref, gain_ref = refs[:6]
    normed_ref, x_ref, raw_ref = refs[6:]
    heads = pool_ref.shape[2] // HEAD_DIM
    raw = dot(owner_ref[...], jnp.concatenate([g[...] for g in got], axis=0))
    raw_ref[...] = raw
    x = silu(conv_slots(raw, pool_ref[...], weight_ref[...]))
    x_ref[...] = x
    matrix = spread_matrix(heads)
    small = x.astype(BF16)
    parts = [dot(m_ref[h], small[:, h * HEAD_DIM : (h + 1) * HEAD_DIM]) for h in range(heads)]
    y = jnp.concatenate(parts, axis=1) + y_ref[...] + spread(skip_ref[...], matrix) * x
    square = (y * y).astype(BF16)
    scale = lax.rsqrt(dot_t(square, matrix) * (1.0 / HEAD_DIM) + EPS)
    normed = (y * spread(scale, matrix) * gain_ref[...]).astype(BF16)
    normed_ref[...] = dot(pack_ref[...], normed).astype(BF16)


def x_stage(owner, pack, got, pool, weight, y, m, skip, gain, n_pool):
    slots, _, width = pool.shape
    rows = slots * DRAFT
    return pl.pallas_call(
        functools.partial(x_kernel, n_pool),
        out_shape=[jax.ShapeDtypeStruct((pack.shape[0], width), BF16)] + [jax.ShapeDtypeStruct((rows, width), F32)] * 2,
        in_specs=[VMEM] * (n_pool + 8),
        out_specs=[VMEM] * 3,
        compiler_params=params(16),
        cost_estimate=cost(2 * rows * rows * width, 4e6),
    )(owner, pack, *got, pool, weight, y, m, skip, gain)


def state_kernel(span_of, again, d_ref, x_ref, w_ref, b_ref, pool, accepts_ref, raws, convs, *refs):
    new_pool, kepts, buf, out_sems = refs[1:] if again else refs
    slots, heads = pool.shape[:2]
    rows = slots * DRAFT
    span = b_ref.shape[1] // STATE
    per = heads // span
    backs = {j: pltpu.make_async_copy(buf.at[j], new_pool.at[j], out_sems.at[j]) for j in span_of}
    weighted = x_ref[...] * spread(w_ref[...], spread_matrix(heads))
    high = weighted.T.astype(BF16)
    b = b_ref[...]
    slot = iota((rows, STATE), 0) >> SHIFT
    for j in span_of:
        for g in range(span):
            rhs = jnp.where(slot == j, b[:, g * STATE : (g + 1) * STATE].astype(F32), 0.0).astype(BF16)
            added = dot(high[g * per * HEAD_DIM : (g + 1) * per * HEAD_DIM], rhs)
            for i in range(per):
                h = g * per + i
                kept = pool[j, h].astype(F32) * d_ref[j, h] + added[i * HEAD_DIM : (i + 1) * HEAD_DIM]
                buf[j, h] = kept.astype(BF16)
        backs[j].start()
    for raw, conv, kept in zip(raws, convs, kepts):
        kept[...] = kept_rows(raw[:, : conv.shape[2]], conv[...], accepts_ref[...])
    for copy in backs.values():
        copy.wait()


def state_stage(span_of, d, x, w, b, pool, accepts, raws, convs, begun):
    slots = pool.shape[0]
    again = begun is not None
    operands = [d, x, w, b, pool, accepts, raws, convs] + ([begun] if again else [])
    at = 6 + len(raws) + len(convs)
    return pl.pallas_call(
        functools.partial(state_kernel, span_of, again),
        out_shape=[jax.ShapeDtypeStruct(pool.shape, BF16), [jax.ShapeDtypeStruct(v.shape, BF16) for v in convs]],
        in_specs=[SMEM] + [VMEM] * 5 + [[VMEM] * len(raws), [VMEM] * len(convs)] + ([HBM] if again else []),
        out_specs=[HBM, [VMEM] * len(convs)],
        scratch_shapes=[
            pltpu.VMEM(pool.shape, BF16),
            pltpu.SemaphoreType.DMA((slots,)),
        ],
        input_output_aliases={at: 0} if again else {},
        compiler_params=params(16),
        cost_estimate=cost(2 * pool.size * DRAFT, 2 * pool.size),
    )(*operands)


def out_kernel(chunks, n_line, other_core, rows, w, *outs):
    width = outs[0].shape[1]
    rank = lax.axis_index("tensor").astype(jnp.int32)
    core, line = rank & 1, rank >> 1
    if other_core:
        core = 1 - core
    for i, out in zip(chunks, outs):
        there = line + i
        there = jnp.where(there >= n_line, there - n_line, there)
        column = pl.multiple_of((2 * there + core) * width, 128)
        out[...] = dot(rows[...], w[:, pl.ds(column, width)]).astype(out.dtype)


def out_stage(rows, w, chunks, n_line, other_core):
    depth, total = w.shape
    width = total // (2 * n_line)
    tokens = rows.shape[0]
    return pl.pallas_call(
        functools.partial(out_kernel, chunks, n_line, other_core),
        out_shape=[jax.ShapeDtypeStruct((tokens, width), BF16 if other_core else F32)] * len(chunks),
        in_specs=[VMEM] * 2,
        out_specs=[VMEM] * len(chunks),
        compiler_params=params(8),
        cost_estimate=cost(2 * tokens * depth * width * len(chunks), 2 * depth * width * len(chunks)),
    )(rows, w)


def place_kernel(part, n_pool, cr, keep, core, return_ref, *refs):
    arrived, outs = refs[:-n_pool], refs[-n_pool:]
    total = keep[:, part] + core[:, part].astype(F32)
    for one in arrived:
        total = total + one[...].astype(F32)
    placed = dot(return_ref[...], total.astype(BF16)).astype(BF16)
    for s in range(n_pool):
        outs[s][...] = placed[s * cr : (s + 1) * cr]


def place_stage(part, keep, core, back, arrived, n_pool, cr):
    width = part.stop - part.start
    return pl.pallas_call(
        functools.partial(place_kernel, part, n_pool, cr),
        out_shape=[jax.ShapeDtypeStruct((cr, width), BF16)] * n_pool,
        in_specs=[VMEM] * (3 + len(arrived)),
        out_specs=[VMEM] * n_pool,
        compiler_params=params(8),
        cost_estimate=cost(1e6, 1e6),
    )(keep, core, back, *arrived)


def collect_kernel(collect_ref, parts, out):
    at = 0
    for got in parts:
        width = got[0].shape[1]
        rows = jnp.concatenate([g[...] for g in got], axis=0)
        out[:, at : at + width] = dot(collect_ref[...], rows).astype(BF16)
        at += width


def collect_stage(collect, parts):
    width = sum(got[0].shape[1] for got in parts)
    return pl.pallas_call(
        collect_kernel,
        out_shape=jax.ShapeDtypeStruct((collect.shape[0], width), BF16),
        in_specs=[VMEM, [[VMEM] * len(got) for got in parts]],
        out_specs=VMEM,
        compiler_params=params(8),
        cost_estimate=cost(1e6, 1e6),
    )(collect, parts)


def body(
    hidden,
    w_x,
    w_bc,
    w_dt,
    conv_x,
    conv_bc,
    dt_bias,
    a_log,
    d_skip,
    norm_gain,
    w_out,
    ssm_pool,
    conv_pool_x,
    conv_pool_bc,
    owners,
    slots,
    accepted,
):
    n_pool = lax.axis_size("pool")
    n_tensor = lax.axis_size("tensor")
    n_line = n_tensor // 2
    req = hidden.shape[0] // DRAFT
    share = req // n_pool
    capacity = share + share // 2
    cr = -(-capacity * DRAFT // 16) * 16
    head_local = w_dt.shape[1]
    span = max(1, head_local // (HEADS // GROUPS))

    def row(v):
        return v.reshape(1, -1)

    def to_owner(parts):
        return [parts[0]] + [
            lax.ppermute(parts[s], "pool", [(i, (i + s) % n_pool) for i in range(n_pool)]) for s in range(1, n_pool)
        ]

    def to_requester(parts):
        return [parts[0]] + [
            lax.ppermute(parts[s], "pool", [((i + s) % n_pool, i) for i in range(n_pool)]) for s in range(1, n_pool)
        ]

    bc_sent, routes = project_bc([row(owners), row(slots), row(accepted)], hidden, w_bc, w_dt.T, ssm_pool.shape[0], n_pool, req, cr)
    hidden_kept, send, owner, pack, back, collect, accepts = routes
    bc_got = to_owner(bc_sent)
    x_sent = project_x(hidden_kept, w_x, send, n_pool, cr)
    x_got = to_owner(x_sent)
    bc_got, _ = lax.optimization_barrier((bc_got, x_sent))
    plan = exchange_plan(n_tensor, w_bc.shape[1], span)
    raw_bc, *pieces = bc_stage(owner, bc_got, conv_pool_bc, conv_bc, plan, span, n_pool, n_tensor)
    for i in range(1, len(plan)):
        pieces[i] = lax.ppermute(pieces[i], "tensor", completed(plan[i], n_tensor))
    fade_m, fade, w, d, states = pre_stage(accepts, raw_bc, row(dt_bias), row(a_log), ssm_pool)
    pieces, _ = lax.optimization_barrier((pieces, fade))
    y, m, b = mix_stage(fade_m, fade, states, pieces, plan, n_tensor)
    normed, x, raw_x = x_stage(owner, pack, x_got, conv_pool_x, conv_x, y, m, row(d_skip), row(norm_gain), n_pool)
    ahead = list(range(1, n_line))
    swap = [(i, i ^ 1) for i in range(n_tensor)]
    sends = out_stage(normed, w_out, ahead, n_line, True)
    core_got = [lax.ppermute(v, "tensor", swap) for v in sends]
    keeps = out_stage(normed, w_out, ahead, n_line, False)
    summed = [(k + g.astype(F32)).astype(BF16) for k, g in zip(keeps, core_got)]
    width = w_out.shape[1] // n_tensor
    parts = [slice(0, width // 2), slice(width // 2, width)]
    arrived = [
        [
            lax.ppermute(v[:, part], "tensor", [(r, ((r // 2 + i) % n_line) * 2 + r % 2) for r in range(n_tensor)])
            for i, v in zip(ahead, summed)
        ]
        for part in parts
    ]
    normed, _ = lax.optimization_barrier((normed, summed))
    (send_0,) = out_stage(normed, w_out, [0], n_line, True)
    core_0 = lax.ppermute(send_0, "tensor", swap)
    (keep_0,) = out_stage(normed, w_out, [0], n_line, False)
    half = states.shape[0] // 2
    x, _ = lax.optimization_barrier((x, keep_0))
    begun, _ = state_stage(range(half), d, x, w, b, states, accepts, [], [], None)
    keep_0, _ = lax.optimization_barrier((keep_0, begun))
    placed = [place_stage(part, keep_0, core_0, back, one, n_pool, cr) for part, one in zip(parts, arrived)]
    returned = [to_requester(one) for one in placed]
    x, _ = lax.optimization_barrier((x, placed[-1]))
    new_pool, (new_conv_x, new_conv_bc) = state_stage(
        range(half, states.shape[0]), d, x, w, b, states, accepts, [raw_x, raw_bc], [conv_pool_x, conv_pool_bc], begun
    )
    returned, _ = lax.optimization_barrier((returned, new_conv_x))
    mixed = collect_stage(collect, returned)
    return (mixed, new_pool, new_conv_x, new_conv_bc)


def solution(mesh):
    in_specs = (
        P(("groups", "pool"), None),
        P(None, "tensor"),
        P(None, "tensor"),
        P(None, "tensor"),
        P(None, "tensor"),
        P(None, "tensor"),
        P("tensor"),
        P("tensor"),
        P("tensor"),
        P("tensor"),
        P("tensor", None),
        P(("groups", "pool"), "tensor", None, None),
        P(("groups", "pool"), None, "tensor"),
        P(("groups", "pool"), None, "tensor"),
        P("groups"),
        P("groups"),
        P("groups"),
    )
    out_specs = (
        P(("groups", "pool"), "tensor"),
        P(("groups", "pool"), "tensor", None, None),
        P(("groups", "pool"), None, "tensor"),
        P(("groups", "pool"), None, "tensor"),
    )
    return jax.shard_map(body, mesh=mesh, in_specs=in_specs, out_specs=out_specs, check_vma=False)
```

time: 61.9 us -> 51.9 us (0.84)
  waiting for transfers between devices: 14 us -> 2.2 us
  starting transfers between devices: 20.2 us -> 23.1 us
  other arithmetic: 0.93 us -> 0.07 us
  local copies, waits for them, and re-layouts: 0.74 us -> 0.07 us
    ppermute x5 -> x6, waiting for transfers between devices: 10.8 us -> 1.2 us  [the longest x1 0.71 us: body(): core_got = [lax.ppermute(v, 'tensor', swap) for v in sends]]
    ppermute x3 -> x6, starting transfers between devices: 4.05 us -> 7.08 us  [to_requester(): lax.ppermute(parts[s], 'pool', [((i + s) % n_pool, i) for i in range(n_po...]
    ppermute x3 -> x6, waiting for transfers between devices: 3.2 us -> 0.95 us  [to_requester(): lax.ppermute(parts[s], 'pool', [((i + s) % n_pool, i) for i in range(n_po...]
    pallas_call x7 -> x14, Pallas kernels: 22.1 us -> 23.8 us  [the longest x2 7.5 us: state_stage(): pl.pallas_call(functools.partial(state_kernel, span_of, again), out_shape...]
    pallas_call x1, Pallas kernels: 2.75 us -> 1.57 us  [mix_stage(): pl.pallas_call(functools.partial(mix_kernel, kinds), out_shape=[jax.Shape...]
    convert_element_type x2 -> x1, other arithmetic: 0.85 us -> 0.07 us  [body(): summed = [(k + g.astype(F32)).astype(BF16) for k, g in zip(keeps, core_got)]]
    unnamed x32 -> x20, local copies, waits for them, and re-layouts: 0.74 us -> 0.05 us
    ppermute x5 -> x6, starting transfers between devices: 5.22 us -> 5.1 us  [the longest x2 2.09 us: body(): lax.ppermute(v[:, part], 'tensor', [(r, (r // 2 + i) % n_line * 2 + r % 2...]
  transfers between devices with their start and end apart: 14 -> 18, of which waited for: 3 -> 3; matrix products, arithmetic and copies ran while one was open for 0% -> 0% of each run, Pallas kernels for 25% -> 35%
where the time goes in v3:
time: 51.9 us; the launch traced here: 51.7 us
  Pallas kernels  25.4 us (49%)
  starting transfers between devices  23.1 us (45%)
  waiting for transfers between devices  2.2 us (4%)
  between operations  0.91 us (2%)
    ppermute x6, starting transfers between devices, to_owner(): lax.ppermute(parts[s], 'pool', [(i, (i + s) % n_pool) for i in range(n_po...  10.9 us
    pallas_call x2, Pallas kernels, state_stage(): pl.pallas_call(functools.partial(state_kernel, span_of, again), out_shape...  7.5 us
    ppermute x6, starting transfers between devices, to_requester(): lax.ppermute(parts[s], 'pool', [((i + s) % n_pool, i) for i in range(n_po...  7.08 us
    pallas_call x1, Pallas kernels, project_x(): pl.pallas_call(functools.partial(project_x_kernel, n_pool, cr, chunk), ou...  4.13 us
    pallas_call x1, Pallas kernels, project_bc(): pl.pallas_call(functools.partial(project_bc_kernel, n_pool, req, cr, chun...  3.6 us
    pallas_call x1, Pallas kernels, pre_stage(): pl.pallas_call(pre_kernel, out_shape=[jax.ShapeDtypeStruct((heads, rows,...  2.95 us
    ppermute x2, starting transfers between devices, body(): lax.ppermute(v[:, part], 'tensor', [(r, (r // 2 + i) % n_line * 2 + r % 2...  2.09 us
    pallas_call x1, Pallas kernels, x_stage(): pl.pallas_call(functools.partial(x_kernel, n_pool), out_shape=[jax.ShapeD...  1.96 us
  transfers between devices with their start and end apart: 18, of which 3 were waited for; matrix products, arithmetic and copies ran while one was open for 0% of the time, Pallas kernels for 35%

profile of v3, /device:TPU:0, one launch (start us, length us, event | category | flops | bytes accessed | tf_op | source)
XLA Modules:
  0.0 51.7 jit_solution(3953627816201433996)
XLA Ops:
  0.6 3.6 %shard_map.192 = (bf16[48,640]{1,0:T(8,128)(2,1)S(1)}, bf16[48,640]{1,0:T(8,128)(2,1)S(1)}, bf16[48,640]{1,0:T(8,128)(2,1)S(1)}, bf16[48,640]{1,0:T(8,128)(2,1)S...) custom-call(s32[1,64]{1,0:T(1,128)} %bitcast.15, ...), custom_call_target="tpu_custom_call" | custom-call | flops 536870912 | bytes 6291456 | tf_op jit(solution)/shard_map/pallas_call | solution.py:252
  4.2 3.1 %collective-permute-start.3 = (bf16[48,640]{1,0:T(8,128)(2,1)S(1)}, bf16[48,640]{1,0:T(8,128)(2,1)S(1)}, u32[]{:S(2)}, u32[]{:S(2)}) collective-permute-start(bf16[48,640]{1,0:T(8,128)(2,1)S(1)} %get-tuple-element.75), channel_id=1, source_target_pairs={{0,4},{4,8},{8,12},{12,0},{1,5},{5,9},{9,13},{13,1},{2,6},{6,10},{... | collective-permute-start | bytes 184328 | tf_op jit(solution)/shard_map/ppermute | solution.py:707
  7.3 2.6 %collective-permute-start.4 = (bf16[48,640]{1,0:T(8,128)(2,1)S(1)}, bf16[48,640]{1,0:T(8,128)(2,1)S(1)}, u32[]{:S(2)}, u32[]{:S(2)}) collective-permute-start(bf16[48,640]{1,0:T(8,128)(2,1)S(1)} %get-tuple-element.76), channel_id=1, source_target_pairs={{0,8},{4,12},{8,0},{12,4},{1,9},{5,13},{9,1},{13,5},{2,10},{6,14},... | collective-permute-start | bytes 184328 | tf_op jit(solution)/shard_map/ppermute | solution.py:707
  9.9 1.3 %collective-permute-start.5 = (bf16[48,640]{1,0:T(8,128)(2,1)S(1)}, bf16[48,640]{1,0:T(8,128)(2,1)S(1)}, u32[]{:S(2)}, u32[]{:S(2)}) collective-permute-start(bf16[48,640]{1,0:T(8,128)(2,1)S(1)} %get-tuple-element.77), channel_id=1, source_target_pairs={{0,12},{4,0},{8,4},{12,8},{1,13},{5,1},{9,5},{13,9},{2,14},{6,2},{... | collective-permute-start | bytes 184328 | tf_op jit(solution)/shard_map/ppermute | solution.py:707
  11.3 0.0 slice-start
  11.3 4.1 %shard_map.193 = (bf16[48,1024]{1,0:T(8,128)(2,1)S(1)}, bf16[48,1024]{1,0:T(8,128)(2,1)S(1)}, bf16[48,1024]{1,0:T(8,128)(2,1)S(1)}, bf16[48,1024]{1,0:T(8,128)(2,1)S(1)}) custom-call(bf16[128,4096]{1,0:T(8,128)(2,1)S(1)} %get-tuple-element.67.hbuf, bf16[4096,1024]{1,0:T(8,128)(2,1)} %w.7, bf16[192,128]{1,0:T(8,128)(2,1)S(1)} %get-tuple-element.68.send_ref), custom_call_target="tpu_custom_call" | custom-call | flops 1073741824 | bytes 9437184 | tf_op jit(solution)/shard_map/pallas_call | solution.py:300
  15.4 0.7 %collective-permute-start = (bf16[48,1024]{1,0:T(8,128)(2,1)S(1)}, bf16[48,1024]{1,0:T(8,128)(2,1)S(1)}, u32[]{:S(2)}, u32[]{:S(2)}) collective-permute-start(bf16[48,1024]{1,0:T(8,128)(2,1)S(1)} %get-tuple-element.70), channel_id=1, source_target_pairs={{0,4},{4,8},{8,12},{12,0},{1,5},{5,9},{9,13},{13,1},{2,6},{6,10},{... | collective-permute-start | bytes 294920 | tf_op jit(solution)/shard_map/ppermute | solution.py:707
  16.1 0.3 collective-permute-start.1
  16.5 2.8 %collective-permute-start.2 = (bf16[48,1024]{1,0:T(8,128)(2,1)S(1)}, bf16[48,1024]{1,0:T(8,128)(2,1)S(1)}, u32[]{:S(2)}, u32[]{:S(2)}) collective-permute-start(bf16[48,1024]{1,0:T(8,128)(2,1)S(1)} %get-tuple-element.72), channel_id=1, source_target_pairs={{0,12},{4,0},{8,4},{12,8},{1,13},{5,1},{9,5},{13,9},{2,14},{6,2},{... | collective-permute-start | bytes 294920 | tf_op jit(solution)/shard_map/ppermute | solution.py:707
  19.3 0.0 collective-permute-done.4.refs_2_
  19.3 0.0 collective-permute-done.5.refs_3_
  19.3 0.5 shard_map.194
  19.8 0.0 collective-permute-start.6
  19.8 1.6 %collective-permute-start.7 = (bf16[144,256]{1,0:T(8,128)(2,1)S(1)}, bf16[144,256]{1,0:T(8,128)(2,1)S(1)}, u32[]{:S(2)}, u32[]{:S(2)}) collective-permute-start(bf16[144,256]{1,0:T(8,128)(2,1)S(1)} %get-tuple-element.88), channel_id=1, source_target_pairs={{2,1},{1,2},{0,3},{3,0},{6,5},{5,6},{4,7},{7,4},{10,9},{9,10},{8,1... | collective-permute-start | bytes 221192 | tf_op jit(solution)/shard_map/ppermute | solution.py:724
  21.4 0.0 copy-start.4
  21.4 0.0 copy-start.7
  21.4 0.0 slice-start.1
  21.5 3.0 %shard_map.195 = (bf16[16,144,144]{2,1,0:T(8,128)(2,1)S(1)}, f32[144,1024]{1,0:T(8,128)S(1)}, f32[144,16]{1,0:T(8,128)S(1)}, f32[18,16]{1,0:T(8,128)S(1)}, bf16[18,16,64,128]{3,2,1,0:T(8,128)(2,1)S(1)}) custom-call(f32[144,1]{1,0:T(8,128)S(1)} %get-tuple-element.73.accepts_ref, f32[144,640]{1,0:T(8,128)S(1)} %get-tuple-element.82.raw_ref.raws_1_, ...), custom_call_target="tpu_custom_call" | custom-call | flops 1000000 | bytes 4718592 | tf_op jit(solution)/shard_map/pallas_call | solution.py:451
  24.4 0.0 collective-permute-done.6.refs_1_
  24.5 0.0 collective-permute-done.7.refs_2_
  24.5 1.6 %shard_map.196 = (f32[144,1024]{1,0:T(8,128)S(1)}, bf16[16,144,144]{2,1,0:T(8,128)(2,1)S(1)}, bf16[144,256]{1,0:T(8,128)(2,1)S(1)}) custom-call(bf16[16,144,144]{2,1,0:T(8,128)(2,1)S(1)} %get-tuple-element.83.fade_m_ref, f32[144,1024]{1,0:T(8,128)S(1)} %get-tuple-element.84.fade_ref, bf16[18,16,64,128]{3,2,1,0:T(8,128)(2,1)S(1)} %get-tuple-element.85.states.pool, ...), custom_call_target="tpu_custom_call" | custom-call | flops 37748736 | bytes 4718592 | tf_op jit(solution)/shard_map/pallas_call | solution.py:510
  26.0 0.0 collective-permute-done.2.refs_3_
  26.1 2.0 %shard_map.197 = (bf16[128,1024]{1,0:T(8,128)(2,1)S(1)}, f32[144,1024]{1,0:T(8,128)S(1)}, f32[144,1024]{1,0:T(8,128)S(1)}) custom-call(bf16[144,192]{1,0:T(8,128)(2,1)S(1)} %get-tuple-element.65.owner_ref, bf16[128,144]{1,0:T(8,128)(2,1)S(1)} %get-tuple-element.66.pack_ref, bf16[48,1024]{1,0:T(8,128)(2,1)S(1)} %get-tuple-element.69.refs_0_, ...), custom_call_target="tpu_custom_call" | custom-call | flops 42467328 | bytes 4000000 | tf_op jit(solution)/shard_map/pallas_call | solution.py:547
  28.1 0.5 shard_map.199
  28.6 1.0 %collective-permute-start.8 = (bf16[128,1024]{1,0:T(8,128)(2,1)S(1)}, bf16[128,1024]{1,0:T(8,128)(2,1)S(1)}, u32[]{:S(2)}, u32[]{:S(2)}) collective-permute-start(bf16[128,1024]{1,0:T(8,128)(2,1)S(1)} %shard_map.199), channel_id=1, source_target_pairs={{0,1},{1,0},{2,3},{3,2},{4,5},{5,4},{6,7},{7,6},{8,9},{9,8},{10,11... | collective-permute-start | bytes 786440 | tf_op jit(solution)/shard_map/ppermute | solution.py:732
  29.5 0.4 shard_map.198
  30.0 0.7 %collective-permute-done.8 = bf16[128,1024]{1,0:T(8,128)(2,1)S(1)} collective-permute-done((bf16[128,1024]{1,0:T(8,128)(2,1)S(1)}, bf16[128,1024]{1,0:T(8,128)(2,1)S(1)}, u32[]{:S(2)}, u32[]{:S(2)}) %collective-permute-start.8) | collective-permute-done | bytes 262176 | tf_op jit(solution)/shard_map/ppermute | solution.py:732
  30.7 0.1 add_convert_fusion
  30.8 0.5 shard_map.202
  31.2 0.4 collective-permute-start.9
  31.7 1.2 %collective-permute-start.10 = (bf16[128,512]{1,0:T(8,128)(2,1)S(1)}, bf16[128,512]{1,0:T(8,128)(2,1)S(1)}, u32[]{:S(2)}, u32[]{:S(2)}) collective-permute-start(bf16[128,512]{1,0:T(8,128)(2,1)S(1)} %get-tuple-element.125), channel_id=1, source_target_pairs={{0,2},{1,3},{2,0},{3,1},{4,6},{5,7},{6,4},{7,5},{8,10},{9,11},{10,... | collective-permute-start | bytes 393224 | tf_op jit(solution)/shard_map/ppermute | solution.py:739
  32.9 0.9 %collective-permute-start.14 = (bf16[128,512]{1,0:T(8,128)(2,1)S(1)}, bf16[128,512]{1,0:T(8,128)(2,1)S(1)}, u32[]{:S(2)}, u32[]{:S(2)}) collective-permute-start(bf16[128,512]{1,0:T(8,128)(2,1)S(1)} %get-tuple-element.124), channel_id=1, source_target_pairs={{0,2},{1,3},{2,0},{3,1},{4,6},{5,7},{6,4},{7,5},{8,10},{9,11},{10,... | collective-permute-start | bytes 393224 | tf_op jit(solution)/shard_map/ppermute | solution.py:739
  33.8 0.5 shard_map.200.keep
  34.3 3.4 %shard_map.201.refs_0_ = bf16[18,16,64,128]{3,2,1,0:T(8,128)(2,1)} custom-call(f32[18,16]{1,0:T(8,128)S(1)} %get-tuple-element.96.d_ref, f32[144,1024]{1,0:T(8,128)S(1)} %get-tuple-element.111.x_ref, f32[144,16]{1,0:T(8,128)S(1)} %get-tuple-element.99.w_ref, bf16[144,256]{1,0:T(8,128)(2,1)S(1)} %get-tuple-element.100.b_ref, ...), custom_call_target="tpu_custom_call" | custom-call | flops 37748736 | bytes 4718592 | tf_op jit(solution)/shard_map/pallas_call | solution.py:588
  37.7 0.5 collective-permute-done.10.refs_0_
  38.1 0.0 collective-permute-done.9.core
  38.1 0.2 shard_map.203
  38.4 1.3 %collective-permute-start.11 = (bf16[48,512]{1,0:T(8,128)(2,1)S(1)}, bf16[48,512]{1,0:T(8,128)(2,1)S(1)}, u32[]{:S(2)}, u32[]{:S(2)}) collective-permute-start(bf16[48,512]{1,0:T(8,128)(2,1)S(1)} %get-tuple-element.104), channel_id=1, source_target_pairs={{4,0},{8,4},{12,8},{0,12},{5,1},{9,5},{13,9},{1,13},{6,2},{10,6},{... | collective-permute-start | bytes 147464 | tf_op jit(solution)/shard_map/ppermute | solution.py:712
  39.6 0.7 %collective-permute-start.12 = (bf16[48,512]{1,0:T(8,128)(2,1)S(1)}, bf16[48,512]{1,0:T(8,128)(2,1)S(1)}, u32[]{:S(2)}, u32[]{:S(2)}) collective-permute-start(bf16[48,512]{1,0:T(8,128)(2,1)S(1)} %get-tuple-element.105), channel_id=1, source_target_pairs={{8,0},{12,4},{0,8},{4,12},{9,1},{13,5},{1,9},{5,13},{10,2},{14,6},... | collective-permute-start | bytes 147464 | tf_op jit(solution)/shard_map/ppermute | solution.py:712
  40.3 1.8 %collective-permute-start.13 = (bf16[48,512]{1,0:T(8,128)(2,1)S(1)}, bf16[48,512]{1,0:T(8,128)(2,1)S(1)}, u32[]{:S(2)}, u32[]{:S(2)}) collective-permute-start(bf16[48,512]{1,0:T(8,128)(2,1)S(1)} %get-tuple-element.106), channel_id=1, source_target_pairs={{12,0},{0,4},{4,8},{8,12},{13,1},{1,5},{5,9},{9,13},{14,2},{2,6},{... | collective-permute-start | bytes 147464 | tf_op jit(solution)/shard_map/ppermute | solution.py:712
  42.2 0.2 shard_map.204
  42.4 2.1 %collective-permute-start.15 = (bf16[48,512]{1,0:T(8,128)(2,1)S(1)}, bf16[48,512]{1,0:T(8,128)(2,1)S(1)}, u32[]{:S(2)}, u32[]{:S(2)}) collective-permute-start(bf16[48,512]{1,0:T(8,128)(2,1)S(1)} %get-tuple-element.108), channel_id=1, source_target_pairs={{4,0},{8,4},{12,8},{0,12},{5,1},{9,5},{13,9},{1,13},{6,2},{10,6},{... | collective-permute-start | bytes 147464 | tf_op jit(solution)/shard_map/ppermute | solution.py:712
  44.5 0.4 collective-permute-start.16
  44.9 0.0 collective-permute-done.11.parts_0__1_
  44.9 0.8 %collective-permute-start.17 = (bf16[48,512]{1,0:T(8,128)(2,1)S(1)}, bf16[48,512]{1,0:T(8,128)(2,1)S(1)}, u32[]{:S(2)}, u32[]{:S(2)}) collective-permute-start(bf16[48,512]{1,0:T(8,128)(2,1)S(1)} %get-tuple-element.110), channel_id=1, source_target_pairs={{12,0},{0,4},{4,8},{8,12},{13,1},{1,5},{5,9},{9,13},{14,2},{2,6},{... | collective-permute-start | bytes 147464 | tf_op jit(solution)/shard_map/ppermute | solution.py:712
  45.7 4.1 %shard_map.205 = (bf16[18,16,64,128]{3,2,1,0:T(8,128)(2,1)}, bf16[18,3,1024]{2,1,0:T(4,128)(2,1)}, bf16[18,3,512]{2,1,0:T(4,128)(2,1)}) custom-call(f32[18,16]{1,0:T(8,128)S(1)} %get-tuple-element.96.d_ref, f32[144,1024]{1,0:T(8,128)S(1)} %get-tuple-element.111.x_ref, f32[144,16]{1,0:T(8,128)S(1)} %get-tuple-element.99.w_ref, ...), custom_call_target="tpu_custom_call", output_to_operand_aliasing={{0}: (10, {})} | custom-call | flops 37748736 | bytes 4718592 | tf_op jit(solution)/shard_map/pallas_call | solution.py:588
  49.8 0.9 %collective-permute-done.17.parts_1__3_ = bf16[48,512]{1,0:T(8,128)(2,1)S(1)} collective-permute-done((bf16[48,512]{1,0:T(8,128)(2,1)S(1)}, bf16[48,512]{1,0:T(8,128)(2,1)S(1)}, u32[]{:S(2)}, u32[]{:S(2)}) %collective-permute-start.17) | collective-permute-done | bytes 49184 | tf_op jit(solution)/shard_map/ppermute | solution.py:712
  50.8 0.9 %shard_map.206 = bf16[128,1024]{1,0:T(8,128)(2,1)} custom-call(bf16[128,192]{1,0:T(8,128)(2,1)S(1)} %get-tuple-element.64.collect_ref, bf16[48,512]{1,0:T(8,128)(2,1)S(1)} %get-tuple-element.114.parts_0__0_, bf16[48,512]{1,0:T(8,128)(2,1)S(1)} %collective-permute-done.11.parts_0__1_, bf16[48,512]{1,0:T(8,128)(2,1)S(1)} %collective-permute-done.12.parts_0__2_, ...), custom_call_target="tpu_custom_call" | custom-call | flops 1000000 | bytes 1000000 | tf_op jit(solution)/shard_map/pallas_call | solution.py:663
  (26 shorter events, 0.1 us)
Async XLA Ops:
  4.2 12.2 %collective-permute-start.3 = (bf16[48,640]{1,0:T(8,128)(2,1)S(1)}, bf16[48,640]{1,0:T(8,128)(2,1)S(1)}, u32[]{:S(2)}, u32[]{:S(2)}) collective-permute-start(bf16[48,640]{1,0:T(8,128)(2,1)S(1)} %get-tuple-element.75), channel_id=1, source_target_pairs={{0,4},{4,8},{8,12},{12,0},{1,5},{5,9},{9,13},{13,1},{2,6},{6,10},{... | collective-permute-start | bytes 184328 | tf_op jit(solution)/shard_map/ppermute | solution.py:707
  7.3 12.0 %collective-permute-start.4 = (bf16[48,640]{1,0:T(8,128)(2,1)S(1)}, bf16[48,640]{1,0:T(8,128)(2,1)S(1)}, u32[]{:S(2)}, u32[]{:S(2)}) collective-permute-start(bf16[48,640]{1,0:T(8,128)(2,1)S(1)} %get-tuple-element.76), channel_id=1, source_target_pairs={{0,8},{4,12},{8,0},{12,4},{1,9},{5,13},{9,1},{13,5},{2,10},{6,14},... | collective-permute-start | bytes 184328 | tf_op jit(solution)/shard_map/ppermute | solution.py:707
  9.9 9.4 %collective-permute-start.5 = (bf16[48,640]{1,0:T(8,128)(2,1)S(1)}, bf16[48,640]{1,0:T(8,128)(2,1)S(1)}, u32[]{:S(2)}, u32[]{:S(2)}) collective-permute-start(bf16[48,640]{1,0:T(8,128)(2,1)S(1)} %get-tuple-element.77), channel_id=1, source_target_pairs={{0,12},{4,0},{8,4},{12,8},{1,13},{5,1},{9,5},{13,9},{2,14},{6,2},{... | collective-permute-start | bytes 184328 | tf_op jit(solution)/shard_map/ppermute | solution.py:707
  11.3 8.1 %copy-start.1 = (bf16[18,3,512]{2,1,0:T(4,128)(2,1)S(1)}, bf16[18,3,512]{2,1,0:T(4,128)(2,1)}, u32[]{:S(2)}) copy-start(bf16[18,3,512]{2,1,0:T(4,128)(2,1)} %convs_1_.1) | copy-start | bytes 165892
  11.3 8.1 %copy-start.3 = (f32[4,512]{1,0:T(4,128)S(1)}, f32[4,512]{1,0:T(4,128)}, u32[]{:S(2)}) copy-start(f32[4,512]{1,0:T(4,128)} %refs_5_.2) | copy-start | bytes 24580
  11.3 10.1 %copy-start.5 = (f32[16]{0:T(128)S(1)}, f32[16]{0:T(128)}, u32[]{:S(2)}) copy-start(f32[16]{0:T(128)} %param.23) | copy-start | bytes 196
  11.3 10.2 %copy-start.6 = (f32[16]{0:T(128)S(1)}, f32[16]{0:T(128)}, u32[]{:S(2)}) copy-start(f32[16]{0:T(128)} %param.24) | copy-start | bytes 196
  11.3 16.8 %slice-start = ((s8[8388608]{0:T(1024)(128)(4,1)}), s8[4194304]{0:T(1024)(128)(4,1)S(1)}, s32[]{:S(2)}) async-start(s8[8388608]{0:T(1024)(128)(4,1)} %bitcast.8), calls=%async_computation | async-start | bytes 8388608
  15.4 10.6 %collective-permute-start = (bf16[48,1024]{1,0:T(8,128)(2,1)S(1)}, bf16[48,1024]{1,0:T(8,128)(2,1)S(1)}, u32[]{:S(2)}, u32[]{:S(2)}) collective-permute-start(bf16[48,1024]{1,0:T(8,128)(2,1)S(1)} %get-tuple-element.70), channel_id=1, source_target_pairs={{0,4},{4,8},{8,12},{12,0},{1,5},{5,9},{9,13},{13,1},{2,6},{6,10},{... | collective-permute-start | bytes 294920 | tf_op jit(solution)/shard_map/ppermute | solution.py:707
  16.1 9.9 %collective-permute-start.1 = (bf16[48,1024]{1,0:T(8,128)(2,1)S(1)}, bf16[48,1024]{1,0:T(8,128)(2,1)S(1)}, u32[]{:S(2)}, u32[]{:S(2)}) collective-permute-start(bf16[48,1024]{1,0:T(8,128)(2,1)S(1)} %get-tuple-element.71), channel_id=1, source_target_pairs={{0,8},{4,12},{8,0},{12,4},{1,9},{5,13},{9,1},{13,5},{2,10},{6,14},... | collective-permute-start | bytes 294920 | tf_op jit(solution)/shard_map/ppermute | solution.py:707
  16.5 9.6 %collective-permute-start.2 = (bf16[48,1024]{1,0:T(8,128)(2,1)S(1)}, bf16[48,1024]{1,0:T(8,128)(2,1)S(1)}, u32[]{:S(2)}, u32[]{:S(2)}) collective-permute-start(bf16[48,1024]{1,0:T(8,128)(2,1)S(1)} %get-tuple-element.72), channel_id=1, source_target_pairs={{0,12},{4,0},{8,4},{12,8},{1,13},{5,1},{9,5},{13,9},{2,14},{6,2},{... | collective-permute-start | bytes 294920 | tf_op jit(solution)/shard_map/ppermute | solution.py:707
  19.8 4.7 %collective-permute-start.6 = (bf16[144,256]{1,0:T(8,128)(2,1)S(1)}, bf16[144,256]{1,0:T(8,128)(2,1)S(1)}, u32[]{:S(2)}, u32[]{:S(2)}) collective-permute-start(bf16[144,256]{1,0:T(8,128)(2,1)S(1)} %get-tuple-element.87), channel_id=1, source_target_pairs={{2,0},{0,1},{3,2},{1,3},{6,4},{4,5},{7,6},{5,7},{10,8},{8,9},{11,1... | collective-permute-start | bytes 221192 | tf_op jit(solution)/shard_map/ppermute | solution.py:724
  19.8 4.6 %collective-permute-start.7 = (bf16[144,256]{1,0:T(8,128)(2,1)S(1)}, bf16[144,256]{1,0:T(8,128)(2,1)S(1)}, u32[]{:S(2)}, u32[]{:S(2)}) collective-permute-start(bf16[144,256]{1,0:T(8,128)(2,1)S(1)} %get-tuple-element.88), channel_id=1, source_target_pairs={{2,1},{1,2},{0,3},{3,0},{6,5},{5,6},{4,7},{7,4},{10,9},{9,10},{8,1... | collective-permute-start | bytes 221192 | tf_op jit(solution)/shard_map/ppermute | solution.py:724
  21.4 4.7 %copy-start = (bf16[18,3,1024]{2,1,0:T(4,128)(2,1)S(1)}, bf16[18,3,1024]{2,1,0:T(4,128)(2,1)}, u32[]{:S(2)}) copy-start(bf16[18,3,1024]{2,1,0:T(4,128)(2,1)} %convs_0_.1) | copy-start | bytes 331780
  21.4 4.7 %copy-start.2 = (f32[4,1024]{1,0:T(4,128)S(1)}, f32[4,1024]{1,0:T(4,128)}, u32[]{:S(2)}) copy-start(f32[4,1024]{1,0:T(4,128)} %refs_5_.3) | copy-start | bytes 49156
  21.4 4.7 %copy-start.4 = (f32[1024]{0:T(1024)S(1)}, f32[1024]{0:T(1024)}, u32[]{:S(2)}) copy-start(f32[1024]{0:T(1024)} %param.26) | copy-start | bytes 12292
  21.4 4.7 %copy-start.7 = (f32[16]{0:T(128)S(1)}, f32[16]{0:T(128)}, u32[]{:S(2)}) copy-start(f32[16]{0:T(128)} %param.25) | copy-start | bytes 196
  21.4 6.6 %slice-start.1 = ((s8[8388608]{0:T(1024)(128)(4,1)}), s8[4194304]{0:T(1024)(128)(4,1)S(1)}, s32[]{:S(2)}) async-start(s8[8388608]{0:T(1024)(128)(4,1)} %bitcast.8), calls=%async_computation.1 | async-start | bytes 8388608
  28.6 2.1 %collective-permute-start.8 = (bf16[128,1024]{1,0:T(8,128)(2,1)S(1)}, bf16[128,1024]{1,0:T(8,128)(2,1)S(1)}, u32[]{:S(2)}, u32[]{:S(2)}) collective-permute-start(bf16[128,1024]{1,0:T(8,128)(2,1)S(1)} %shard_map.199), channel_id=1, source_target_pairs={{0,1},{1,0},{2,3},{3,2},{4,5},{5,4},{6,7},{7,6},{8,9},{9,8},{10,11... | collective-permute-start | bytes 786440 | tf_op jit(solution)/shard_map/ppermute | solution.py:732
  31.2 6.9 %collective-permute-start.9 = (bf16[128,1024]{1,0:T(8,128)(2,1)S(1)}, bf16[128,1024]{1,0:T(8,128)(2,1)S(1)}, u32[]{:S(2)}, u32[]{:S(2)}) collective-permute-start(bf16[128,1024]{1,0:T(8,128)(2,1)S(1)} %shard_map.202), channel_id=1, source_target_pairs={{0,1},{1,0},{2,3},{3,2},{4,5},{5,4},{6,7},{7,6},{8,9},{9,8},{10,11... | collective-permute-start | bytes 786440 | tf_op jit(solution)/shard_map/ppermute | solution.py:746
  31.7 6.4 %collective-permute-start.10 = (bf16[128,512]{1,0:T(8,128)(2,1)S(1)}, bf16[128,512]{1,0:T(8,128)(2,1)S(1)}, u32[]{:S(2)}, u32[]{:S(2)}) collective-permute-start(bf16[128,512]{1,0:T(8,128)(2,1)S(1)} %get-tuple-element.125), channel_id=1, source_target_pairs={{0,2},{1,3},{2,0},{3,1},{4,6},{5,7},{6,4},{7,5},{8,10},{9,11},{10,... | collective-permute-start | bytes 393224 | tf_op jit(solution)/shard_map/ppermute | solution.py:739
  32.9 9.2 %collective-permute-start.14 = (bf16[128,512]{1,0:T(8,128)(2,1)S(1)}, bf16[128,512]{1,0:T(8,128)(2,1)S(1)}, u32[]{:S(2)}, u32[]{:S(2)}) collective-permute-start(bf16[128,512]{1,0:T(8,128)(2,1)S(1)} %get-tuple-element.124), channel_id=1, source_target_pairs={{0,2},{1,3},{2,0},{3,1},{4,6},{5,7},{6,4},{7,5},{8,10},{9,11},{10,... | collective-permute-start | bytes 393224 | tf_op jit(solution)/shard_map/ppermute | solution.py:739
  38.4 6.5 %collective-permute-start.11 = (bf16[48,512]{1,0:T(8,128)(2,1)S(1)}, bf16[48,512]{1,0:T(8,128)(2,1)S(1)}, u32[]{:S(2)}, u32[]{:S(2)}) collective-permute-start(bf16[48,512]{1,0:T(8,128)(2,1)S(1)} %get-tuple-element.104), channel_id=1, source_target_pairs={{4,0},{8,4},{12,8},{0,12},{5,1},{9,5},{13,9},{1,13},{6,2},{10,6},{... | collective-permute-start | bytes 147464 | tf_op jit(solution)/shard_map/ppermute | solution.py:712
  39.6 10.2 %collective-permute-start.12 = (bf16[48,512]{1,0:T(8,128)(2,1)S(1)}, bf16[48,512]{1,0:T(8,128)(2,1)S(1)}, u32[]{:S(2)}, u32[]{:S(2)}) collective-permute-start(bf16[48,512]{1,0:T(8,128)(2,1)S(1)} %get-tuple-element.105), channel_id=1, source_target_pairs={{8,0},{12,4},{0,8},{4,12},{9,1},{13,5},{1,9},{5,13},{10,2},{14,6},... | collective-permute-start | bytes 147464 | tf_op jit(solution)/shard_map/ppermute | solution.py:712
  40.3 9.5 %collective-permute-start.13 = (bf16[48,512]{1,0:T(8,128)(2,1)S(1)}, bf16[48,512]{1,0:T(8,128)(2,1)S(1)}, u32[]{:S(2)}, u32[]{:S(2)}) collective-permute-start(bf16[48,512]{1,0:T(8,128)(2,1)S(1)} %get-tuple-element.106), channel_id=1, source_target_pairs={{12,0},{0,4},{4,8},{8,12},{13,1},{1,5},{5,9},{9,13},{14,2},{2,6},{... | collective-permute-start | bytes 147464 | tf_op jit(solution)/shard_map/ppermute | solution.py:712
  42.4 7.4 %collective-permute-start.15 = (bf16[48,512]{1,0:T(8,128)(2,1)S(1)}, bf16[48,512]{1,0:T(8,128)(2,1)S(1)}, u32[]{:S(2)}, u32[]{:S(2)}) collective-permute-start(bf16[48,512]{1,0:T(8,128)(2,1)S(1)} %get-tuple-element.108), channel_id=1, source_target_pairs={{4,0},{8,4},{12,8},{0,12},{5,1},{9,5},{13,9},{1,13},{6,2},{10,6},{... | collective-permute-start | bytes 147464 | tf_op jit(solution)/shard_map/ppermute | solution.py:712
  44.5 5.4 %collective-permute-start.16 = (bf16[48,512]{1,0:T(8,128)(2,1)S(1)}, bf16[48,512]{1,0:T(8,128)(2,1)S(1)}, u32[]{:S(2)}, u32[]{:S(2)}) collective-permute-start(bf16[48,512]{1,0:T(8,128)(2,1)S(1)} %get-tuple-element.109), channel_id=1, source_target_pairs={{8,0},{12,4},{0,8},{4,12},{9,1},{13,5},{1,9},{5,13},{10,2},{14,6},... | collective-permute-start | bytes 147464 | tf_op jit(solution)/shard_map/ppermute | solution.py:712
  44.9 5.9 %collective-permute-start.17 = (bf16[48,512]{1,0:T(8,128)(2,1)S(1)}, bf16[48,512]{1,0:T(8,128)(2,1)S(1)}, u32[]{:S(2)}, u32[]{:S(2)}) collective-permute-start(bf16[48,512]{1,0:T(8,128)(2,1)S(1)} %get-tuple-element.110), channel_id=1, source_target_pairs={{12,0},{0,4},{4,8},{8,12},{13,1},{1,5},{5,9},{9,13},{14,2},{2,6},{... | collective-permute-start | bytes 147464 | tf_op jit(solution)/shard_map/ppermute | solution.py:712

commit v4 on v3

--- a/solution.py
+++ b/solution.py
@@ -15,6 +15,7 @@
 SHIFT = 3
 EPS = 1e-05
 FAR = 4096.0
+HEAD_PART = 4
 
 F32 = jnp.float32
 BF16 = jnp.bfloat16
@@ -50,8 +51,14 @@
     return jnp.sum(jnp.where(eye, jnp.broadcast_to(row, (n, n)), 0.0), axis=1, keepdims=True)
 
 
-def wrap(value, n):
-    return jnp.where(value < 0, value + n, value)
+def partner_step(n, i, s):
+    return (i + s) % n
+
+
+def step_to(n, owner, requester):
+    owner, requester = owner.astype(jnp.int32), requester.astype(jnp.int32)
+    step = owner - requester
+    return jnp.where(step < 0, step + n, step).astype(F32)
 
 
 def block_shift(req):
@@ -76,7 +83,7 @@
     ocol = as_col(orow)
     _, rank_col = ranks(orow, ocol, req)
     total, tokens = orow.shape[1], req * DRAFT
-    place_col = wrap(ocol - me.astype(F32), n_pool) * cr + rank_col * DRAFT
+    place_col = step_to(n_pool, ocol, me) * cr + rank_col * DRAFT
     token = iota((total, tokens), 1)
     mine = (iota((total, tokens), 0) - me * req) == (token >> SHIFT)
     place = jnp.sum(jnp.where(mine, jnp.broadcast_to(place_col, (total, tokens)), 0.0), axis=0, keepdims=True)
@@ -88,7 +95,7 @@
     ocol = as_col(orow)
     rank_row, _ = ranks(orow, ocol, req)
     total, tokens = orow.shape[1], req * DRAFT
-    place_row = wrap(orow - me.astype(F32), n_pool) * cr + rank_row * DRAFT
+    place_row = step_to(n_pool, orow, me) * cr + rank_row * DRAFT
     token = iota((tokens, total), 0)
     mine = (iota((tokens, total), 1) - me * req) == (token >> SHIFT)
     place = jnp.sum(jnp.where(mine, jnp.broadcast_to(place_row, (tokens, total)), 0.0), axis=1, keepdims=True)
@@ -101,7 +108,7 @@
     rank_row, _ = ranks(orow, ocol, req)
     total, rows = orow.shape[1], slots * DRAFT
     block = (iota((1, total), 1) >> block_shift(req)).astype(F32)
-    place_row = wrap(me.astype(F32) - block, n_pool) * cr + rank_row * DRAFT + FAR
+    place_row = step_to(n_pool, me, block) * cr + rank_row * DRAFT + FAR
     slot = (iota((rows, total), 0) >> SHIFT).astype(F32)
     match = (orow == me.astype(F32)) & (srow == slot)
     place = jnp.sum(jnp.where(match, jnp.broadcast_to(place_row, (rows, total)), 0.0), axis=1, keepdims=True)
@@ -123,7 +130,7 @@
     at = at + (iota((1, rows), 1) & (DRAFT - 1)).astype(F32)
     pack = hot(iota((tokens, rows), 0).astype(F32) == at)
     block = (iota((total, 1), 0) >> block_shift(req)).astype(F32)
-    place_col = wrap(mine - block, n_pool) * cr + rank_col * DRAFT + FAR
+    place_col = step_to(n_pool, me, block) * cr + rank_col * DRAFT + FAR
     match = (ocol == mine) & (index == (iota((total, tokens), 1) >> SHIFT).astype(F32))
     at = jnp.sum(jnp.where(match, jnp.broadcast_to(place_col, (total, tokens)), 0.0), axis=0, keepdims=True) - FAR
     at = at + (iota((1, tokens), 1) & (DRAFT - 1)).astype(F32)
@@ -189,10 +196,10 @@
     return [pltpu.make_async_copy(src, dst, sems.at[row, k]) for k, (src, dst) in enumerate(pairs)]
 
 
-def project_bc_kernel(n_pool, req, cr, chunk, slots, owners, places, takes, hidden, w, w_dt, *refs):
+def project_bc_kernel(n_pool, req, cr, chunk, slots, owners, places, takes, hidden, w, w_dt, w_x, *refs):
     outs, refs = refs[:n_pool], refs[n_pool:]
-    hbuf, send_ref, owner_ref, pack_ref, return_ref, collect_ref, accepts_ref = refs[:7]
-    meta_buf, wbuf, dt_buf, sems = refs[7:]
+    hbuf, head, send_ref, owner_ref, pack_ref, return_ref, collect_ref, accepts_ref = refs[:8]
+    meta_buf, wbuf, dt_buf, sems = refs[8:]
     steps = hidden.shape[1] // chunk
     parts = [pl.ds(k * chunk, chunk) for k in range(steps)]
     copies = list(
@@ -208,6 +215,8 @@
     for group in copies:
         for copy in group:
             copy.start()
+    ahead = pltpu.make_async_copy(w_x.at[pl.ds(0, head.shape[0])], head, sems.at[3, len(tables)])
+    ahead.start()
     for copy in tables:
         copy.wait()
     me = lax.axis_index("pool").astype(jnp.int32)
@@ -239,13 +248,14 @@
     for s in range(n_pool):
         outs[s][:, :width] = placed[s * cr : (s + 1) * cr]
         outs[s][:, width:] = placed_dt[s * cr : (s + 1) * cr]
+    ahead.wait()
 
 
 def in_hbm(*arrays):
     return [pltpu.with_memory_space_constraint(v, pltpu.HBM) for v in arrays]
 
 
-def project_bc(tables, hidden, w, w_dt, slots, n_pool, req, cr):
+def project_bc(tables, hidden, w, w_dt, w_x, slots, n_pool, req, cr):
     tokens, depth = hidden.shape
     chunk = min(512, depth)
     width, rows = w.shape[1], slots * DRAFT
@@ -254,6 +264,7 @@
         out_shape=[jax.ShapeDtypeStruct((cr, width + 128), BF16)] * n_pool
         + [
             jax.ShapeDtypeStruct((tokens, depth), BF16),
+            jax.ShapeDtypeStruct((depth // HEAD_PART, w_x.shape[1]), BF16),
             jax.ShapeDtypeStruct((n_pool * cr, tokens), BF16),
             jax.ShapeDtypeStruct((rows, n_pool * cr), BF16),
             jax.ShapeDtypeStruct((tokens, rows), BF16),
@@ -261,54 +272,54 @@
             jax.ShapeDtypeStruct((tokens, n_pool * cr), BF16),
             jax.ShapeDtypeStruct((rows, 1), F32),
         ],
-        in_specs=[HBM] * 6,
-        out_specs=[VMEM] * (n_pool + 7),
+        in_specs=[HBM] * 7,
+        out_specs=[VMEM] * (n_pool + 8),
         scratch_shapes=[
             pltpu.VMEM((3,) + tables[0].shape, jnp.int32),
             pltpu.VMEM((depth, width), BF16),
             pltpu.VMEM(w_dt.shape, BF16),
-            pltpu.SemaphoreType.DMA((4, max(3, depth // chunk))),
+            pltpu.SemaphoreType.DMA((4, max(4, depth // chunk))),
         ],
         compiler_params=params(12),
         cost_estimate=cost(2 * tokens * depth * width, depth * (width + 128 + tokens) * 2),
-    )(*in_hbm(*tables, hidden, w, w_dt))
+    )(*in_hbm(*tables, hidden, w, w_dt, w_x))
     return outs[:n_pool], outs[n_pool:]
 
 
-def project_x_kernel(n_pool, cr, chunk, hbuf, w, send_ref, *refs):
+def project_x_kernel(n_pool, cr, chunk, hbuf, head, w, send_ref, *refs):
     outs, (wbuf, sems) = refs[:n_pool], refs[n_pool:]
-    steps = w.shape[0] // chunk
-    parts = [pl.ds(k * chunk, chunk) for k in range(steps)]
-    copies = dma([(w.at[p], wbuf.at[p]) for p in parts], sems, 0)
+    first = head.shape[0]
+    steps = (w.shape[0] - first) // chunk
+    copies = dma([(w.at[pl.ds(first + k * chunk, chunk)], wbuf.at[k]) for k in range(steps)], sems, 0)
     for copy in copies:
         copy.start()
-    total = None
+    total = dot(hbuf[:, :first], head[...])
     for k in range(steps):
         copies[k].wait()
-        here = slice(k * chunk, (k + 1) * chunk)
-        added = dot(hbuf[:, here], wbuf[here])
-        total = added if total is None else total + added
+        here = slice(first + k * chunk, first + (k + 1) * chunk)
+        total = total + dot(hbuf[:, here], wbuf[k])
     placed = dot(send_ref[...], total.astype(BF16)).astype(BF16)
     for s in range(n_pool):
         outs[s][...] = placed[s * cr : (s + 1) * cr]
 
 
-def project_x(hidden, w, send, n_pool, cr):
+def project_x(hidden, head, w, send, n_pool, cr):
     tokens, depth = hidden.shape
     chunk = min(512, depth)
     width = w.shape[1]
+    steps = (depth - head.shape[0]) // chunk
     return pl.pallas_call(
         functools.partial(project_x_kernel, n_pool, cr, chunk),
         out_shape=[jax.ShapeDtypeStruct((cr, width), BF16)] * n_pool,
-        in_specs=[VMEM, HBM, VMEM],
+        in_specs=[VMEM, VMEM, HBM, VMEM],
         out_specs=[VMEM] * n_pool,
         scratch_shapes=[
-            pltpu.VMEM((depth, width), BF16),
-            pltpu.SemaphoreType.DMA((1, depth // chunk)),
+            pltpu.VMEM((steps, chunk, width), BF16),
+            pltpu.SemaphoreType.DMA((1, steps)),
         ],
         compiler_params=params(14),
         cost_estimate=cost(2 * tokens * depth * width, depth * (width + tokens) * 2),
-    )(hidden, *in_hbm(w), send)
+    )(hidden, head, *in_hbm(w), send)
 
 
 def pick(rank, table):
@@ -397,12 +408,9 @@
     )(owner, *got, pool, weight)
 
 
-def pre_kernel(accepts_ref, raw_ref, bias_ref, alog_ref, pool, m_ref, fade_ref, w_ref, d_ref, states, sems):
-    slots, heads = pool.shape[:2]
+def pre_kernel(slots, accepts_ref, raw_ref, conv_ref, bias_ref, alog_ref, kept_ref, m_ref, fade_ref, w_ref, d_ref):
+    heads = w_ref.shape[1]
     rows = slots * DRAFT
-    copies = [pltpu.make_async_copy(pool.at[j], states.at[j], sems.at[j]) for j in range(slots)]
-    for copy in copies:
-        copy.start()
     accepts = accepts_ref[...]
     width = raw_ref.shape[1] - 128
     shape = (128, heads)
@@ -441,28 +449,26 @@
     for h in range(heads):
         m_ref[h] = dot(fade, hot(same & (head == h))).astype(BF16)
     fade_ref[...] = spread(jnp.exp(logs), spread_matrix(heads))
-    for copy in copies:
-        copy.wait()
-
-
-def pre_stage(accepts, raw, bias, a_log, pool):
+    kept_ref[...] = kept_rows(raw_ref[:, :width], conv_ref[...], accepts)
+
+
+def pre_stage(accepts, raw, conv_pool, bias, a_log, pool):
     slots, heads = pool.shape[:2]
     rows = slots * DRAFT
     return pl.pallas_call(
-        pre_kernel,
+        functools.partial(pre_kernel, slots),
         out_shape=[
+            jax.ShapeDtypeStruct(conv_pool.shape, BF16),
             jax.ShapeDtypeStruct((heads, rows, rows), BF16),
             jax.ShapeDtypeStruct((rows, heads * HEAD_DIM), F32),
             jax.ShapeDtypeStruct((rows, heads), F32),
             jax.ShapeDtypeStruct((slots, heads), F32),
-            jax.ShapeDtypeStruct(pool.shape, BF16),
         ],
-        in_specs=[VMEM] * 4 + [HBM],
+        in_specs=[VMEM] * 5,
         out_specs=[VMEM] * 5,
-        scratch_shapes=[pltpu.SemaphoreType.DMA((slots,))],
-        compiler_params=params(20),
-        cost_estimate=cost(1e6, 2 * pool.size),
-    )(accepts, raw, bias, a_log, *in_hbm(pool))
+        compiler_params=params(10),
+        cost_estimate=cost(1e6, 1e6),
+    )(accepts, raw, conv_pool, bias, a_log)
 
 
 def mix_kernel(kinds, fade_m_ref, fade_ref, states, *refs):
@@ -554,77 +560,114 @@
     )(owner, pack, *got, pool, weight, y, m, skip, gain)
 
 
-def state_kernel(span_of, again, d_ref, x_ref, w_ref, b_ref, pool, accepts_ref, raws, convs, *refs):
-    new_pool, kepts, buf, out_sems = refs[1:] if again else refs
+def fill_states(span_of, d_ref, turned, b_ref, pool, new_pool, buf, out_sems):
     slots, heads = pool.shape[:2]
     rows = slots * DRAFT
     span = b_ref.shape[1] // STATE
     per = heads // span
-    backs = {j: pltpu.make_async_copy(buf.at[j], new_pool.at[j], out_sems.at[j]) for j in span_of}
-    weighted = x_ref[...] * spread(w_ref[...], spread_matrix(heads))
-    high = weighted.T.astype(BF16)
-    b = b_ref[...]
+    backs = [pltpu.make_async_copy(buf.at[j], new_pool.at[j], out_sems.at[j]) for j in span_of]
+    b = b_ref[...].astype(F32)
     slot = iota((rows, STATE), 0) >> SHIFT
-    for j in span_of:
+    for at in range(0, len(span_of), 2):
+        pair = span_of[at : at + 2]
         for g in range(span):
-            rhs = jnp.where(slot == j, b[:, g * STATE : (g + 1) * STATE].astype(F32), 0.0).astype(BF16)
-            added = dot(high[g * per * HEAD_DIM : (g + 1) * per * HEAD_DIM], rhs)
-            for i in range(per):
-                h = g * per + i
-                kept = pool[j, h].astype(F32) * d_ref[j, h] + added[i * HEAD_DIM : (i + 1) * HEAD_DIM]
-                buf[j, h] = kept.astype(BF16)
-        backs[j].start()
-    for raw, conv, kept in zip(raws, convs, kepts):
-        kept[...] = kept_rows(raw[:, : conv.shape[2]], conv[...], accepts_ref[...])
-    for copy in backs.values():
+            part = b[:, g * STATE : (g + 1) * STATE]
+            rhs = jnp.concatenate([jnp.where(slot == j, part, 0.0) for j in pair], axis=1).astype(BF16)
+            added = dot(turned[g * per * HEAD_DIM : (g + 1) * per * HEAD_DIM], rhs)
+            for n, j in enumerate(pair):
+                for i in range(per):
+                    h = g * per + i
+                    more = added[i * HEAD_DIM : (i + 1) * HEAD_DIM, n * STATE : (n + 1) * STATE]
+                    buf[j, h] = (pool[j, h].astype(F32) * d_ref[j, h] + more).astype(BF16)
+        for back in backs[at : at + 2]:
+            back.start()
+    return backs
+
+
+def first_state_kernel(span_of, d_ref, x_ref, w_ref, b_ref, pool, new_pool, turned_ref, buf, out_sems):
+    weighted = x_ref[...] * spread(w_ref[...], spread_matrix(pool.shape[1]))
+    turned_ref[...] = weighted.T.astype(BF16)
+    for copy in fill_states(span_of, d_ref, turned_ref, b_ref, pool, new_pool, buf, out_sems):
         copy.wait()
 
 
-def state_stage(span_of, d, x, w, b, pool, accepts, raws, convs, begun):
-    slots = pool.shape[0]
-    again = begun is not None
-    operands = [d, x, w, b, pool, accepts, raws, convs] + ([begun] if again else [])
-    at = 6 + len(raws) + len(convs)
-    return pl.pallas_call(
-        functools.partial(state_kernel, span_of, again),
-        out_shape=[jax.ShapeDtypeStruct(pool.shape, BF16), [jax.ShapeDtypeStruct(v.shape, BF16) for v in convs]],
-        in_specs=[SMEM] + [VMEM] * 5 + [[VMEM] * len(raws), [VMEM] * len(convs)] + ([HBM] if again else []),
-        out_specs=[HBM, [VMEM] * len(convs)],
-        scratch_shapes=[
-            pltpu.VMEM(pool.shape, BF16),
-            pltpu.SemaphoreType.DMA((slots,)),
-        ],
-        input_output_aliases={at: 0} if again else {},
+def first_state_stage(span_of, d, x, w, b, pool):
+    return pl.pallas_call(
+        functools.partial(first_state_kernel, span_of),
+        out_shape=[jax.ShapeDtypeStruct(pool.shape, BF16), jax.ShapeDtypeStruct(x.shape[::-1], BF16)],
+        in_specs=[SMEM] + [VMEM] * 4,
+        out_specs=[HBM, VMEM],
+        scratch_shapes=[pltpu.VMEM(pool.shape, BF16), pltpu.SemaphoreType.DMA((pool.shape[0],))],
         compiler_params=params(16),
         cost_estimate=cost(2 * pool.size * DRAFT, 2 * pool.size),
-    )(*operands)
-
-
-def out_kernel(chunks, n_line, other_core, rows, w, *outs):
+    )(d, x, w, b, pool)
+
+
+def last_state_kernel(span_of, d_ref, turned_ref, b_ref, pool, accepts_ref, raw_ref, conv_ref, begun, *refs):
+    del begun
+    new_pool, kept_ref, buf, out_sems = refs
+    backs = fill_states(span_of, d_ref, turned_ref, b_ref, pool, new_pool, buf, out_sems)
+    kept_ref[...] = kept_rows(raw_ref[...], conv_ref[...], accepts_ref[...])
+    for copy in backs:
+        copy.wait()
+
+
+def last_state_stage(span_of, d, turned, b, pool, accepts, raw, conv, begun):
+    return pl.pallas_call(
+        functools.partial(last_state_kernel, span_of),
+        out_shape=[jax.ShapeDtypeStruct(pool.shape, BF16), jax.ShapeDtypeStruct(conv.shape, BF16)],
+        in_specs=[SMEM] + [VMEM] * 6 + [HBM],
+        out_specs=[HBM, VMEM],
+        scratch_shapes=[pltpu.VMEM(pool.shape, BF16), pltpu.SemaphoreType.DMA((pool.shape[0],))],
+        input_output_aliases={7: 0},
+        compiler_params=params(16),
+        cost_estimate=cost(2 * pool.size * DRAFT, 2 * pool.size),
+    )(d, turned, b, pool, accepts, raw, conv, begun)
+
+
+def out_kernel(wants, n_line, rows, w, *outs):
     width = outs[0].shape[1]
     rank = lax.axis_index("tensor").astype(jnp.int32)
     core, line = rank & 1, rank >> 1
-    if other_core:
-        core = 1 - core
-    for i, out in zip(chunks, outs):
+    for (i, other_core), out in zip(wants, outs):
         there = line + i
         there = jnp.where(there >= n_line, there - n_line, there)
-        column = pl.multiple_of((2 * there + core) * width, 128)
+        column = pl.multiple_of((2 * there + (1 - core if other_core else core)) * width, 128)
         out[...] = dot(rows[...], w[:, pl.ds(column, width)]).astype(out.dtype)
 
 
-def out_stage(rows, w, chunks, n_line, other_core):
+def out_stage(rows, w, wants, n_line):
     depth, total = w.shape
     width = total // (2 * n_line)
     tokens = rows.shape[0]
     return pl.pallas_call(
-        functools.partial(out_kernel, chunks, n_line, other_core),
-        out_shape=[jax.ShapeDtypeStruct((tokens, width), BF16 if other_core else F32)] * len(chunks),
+        functools.partial(out_kernel, wants, n_line),
+        out_shape=[jax.ShapeDtypeStruct((tokens, width), BF16 if other else F32) for _, other in wants],
         in_specs=[VMEM] * 2,
-        out_specs=[VMEM] * len(chunks),
+        out_specs=[VMEM] * len(wants),
         compiler_params=params(8),
-        cost_estimate=cost(2 * tokens * depth * width * len(chunks), 2 * depth * width * len(chunks)),
+        cost_estimate=cost(2 * tokens * depth * width * len(wants), 2 * depth * width * len(wants)),
     )(rows, w)
+
+
+def sum_kernel(n, parts, *refs):
+    for i in range(n):
+        for p, part in enumerate(parts):
+            refs[2 * n + p * n + i][...] = (refs[i][:, part] + refs[n + i][:, part].astype(F32)).astype(BF16)
+
+
+def sum_stage(keeps, gots, parts):
+    n = len(keeps)
+    shape = jax.ShapeDtypeStruct((keeps[0].shape[0], parts[0].stop), BF16)
+    outs = pl.pallas_call(
+        functools.partial(sum_kernel, n, parts),
+        out_shape=[shape] * (n * len(parts)),
+        in_specs=[VMEM] * (2 * n),
+        out_specs=[VMEM] * (n * len(parts)),
+        compiler_params=params(8),
+        cost_estimate=cost(1e6, 1e6),
+    )(*keeps, *gots)
+    return [outs[p * n : (p + 1) * n] for p in range(len(parts))]
 
 
 def place_kernel(part, n_pool, cr, keep, core, return_ref, *refs):
@@ -702,58 +745,58 @@
     def row(v):
         return v.reshape(1, -1)
 
-    def to_owner(parts):
-        return [parts[0]] + [
-            lax.ppermute(parts[s], "pool", [(i, (i + s) % n_pool) for i in range(n_pool)]) for s in range(1, n_pool)
-        ]
-
-    def to_requester(parts):
-        return [parts[0]] + [
-            lax.ppermute(parts[s], "pool", [((i + s) % n_pool, i) for i in range(n_pool)]) for s in range(1, n_pool)
-        ]
-
-    bc_sent, routes = project_bc([row(owners), row(slots), row(accepted)], hidden, w_bc, w_dt.T, ssm_pool.shape[0], n_pool, req, cr)
-    hidden_kept, send, owner, pack, back, collect, accepts = routes
-    bc_got = to_owner(bc_sent)
-    x_sent = project_x(hidden_kept, w_x, send, n_pool, cr)
-    x_got = to_owner(x_sent)
+    def over_pool(parts, home):
+        moved = list(parts)
+        for step in range(1, n_pool):
+            pairs = [(i, partner_step(n_pool, i, step)) for i in range(n_pool)]
+            pairs = [(b, a) for a, b in pairs] if home else pairs
+            moved[step] = lax.ppermute(parts[step], "pool", pairs)
+        return moved
+
+    bc_sent, routes = project_bc([row(owners), row(slots), row(accepted)], hidden, w_bc, w_dt.T, w_x, ssm_pool.shape[0], n_pool, req, cr)
+    hidden_kept, head, send, owner, pack, back, collect, accepts = routes
+    bc_got = over_pool(bc_sent, False)
+    x_sent = project_x(hidden_kept, head, w_x, send, n_pool, cr)
+    x_got = over_pool(x_sent, False)
     bc_got, _ = lax.optimization_barrier((bc_got, x_sent))
     plan = exchange_plan(n_tensor, w_bc.shape[1], span)
     raw_bc, *pieces = bc_stage(owner, bc_got, conv_pool_bc, conv_bc, plan, span, n_pool, n_tensor)
     for i in range(1, len(plan)):
         pieces[i] = lax.ppermute(pieces[i], "tensor", completed(plan[i], n_tensor))
-    fade_m, fade, w, d, states = pre_stage(accepts, raw_bc, row(dt_bias), row(a_log), ssm_pool)
+    new_conv_bc, fade_m, fade, w, d = pre_stage(accepts, raw_bc, conv_pool_bc, row(dt_bias), row(a_log), ssm_pool)
+    states, _ = lax.optimization_barrier((ssm_pool, x_sent))
+    states = pltpu.with_memory_space_constraint(states, pltpu.VMEM)
     pieces, _ = lax.optimization_barrier((pieces, fade))
     y, m, b = mix_stage(fade_m, fade, states, pieces, plan, n_tensor)
     normed, x, raw_x = x_stage(owner, pack, x_got, conv_pool_x, conv_x, y, m, row(d_skip), row(norm_gain), n_pool)
     ahead = list(range(1, n_line))
     swap = [(i, i ^ 1) for i in range(n_tensor)]
-    sends = out_stage(normed, w_out, ahead, n_line, True)
+    sends = out_stage(normed, w_out, [(i, True) for i in ahead], n_line)
     core_got = [lax.ppermute(v, "tensor", swap) for v in sends]
-    keeps = out_stage(normed, w_out, ahead, n_line, False)
-    summed = [(k + g.astype(F32)).astype(BF16) for k, g in zip(keeps, core_got)]
+    *keeps, send_0, keep_0 = out_stage(normed, w_out, [(i, False) for i in ahead] + [(0, True), (0, False)], n_line)
     width = w_out.shape[1] // n_tensor
     parts = [slice(0, width // 2), slice(width // 2, width)]
-    arrived = [
-        [
-            lax.ppermute(v[:, part], "tensor", [(r, ((r // 2 + i) % n_line) * 2 + r % 2) for r in range(n_tensor)])
-            for i, v in zip(ahead, summed)
+    summed = sum_stage(keeps, core_got, parts)
+
+    def over_line(values):
+        return [
+            lax.ppermute(v, "tensor", [(r, ((r // 2 + i) % n_line) * 2 + r % 2) for r in range(n_tensor)])
+            for i, v in zip(ahead, values)
         ]
-        for part in parts
-    ]
-    normed, _ = lax.optimization_barrier((normed, summed))
-    (send_0,) = out_stage(normed, w_out, [0], n_line, True)
+
+    arrived = [over_line(summed[0])]
     core_0 = lax.ppermute(send_0, "tensor", swap)
-    (keep_0,) = out_stage(normed, w_out, [0], n_line, False)
     half = states.shape[0] // 2
-    x, _ = lax.optimization_barrier((x, keep_0))
-    begun, _ = state_stage(range(half), d, x, w, b, states, accepts, [], [], None)
+    x, _ = lax.optimization_barrier((x, summed))
+    begun, turned = first_state_stage(range(half), d, x, w, b, states)
+    second, _ = lax.optimization_barrier((summed[1], begun))
+    arrived.append(over_line(second))
     keep_0, _ = lax.optimization_barrier((keep_0, begun))
     placed = [place_stage(part, keep_0, core_0, back, one, n_pool, cr) for part, one in zip(parts, arrived)]
-    returned = [to_requester(one) for one in placed]
-    x, _ = lax.optimization_barrier((x, placed[-1]))
-    new_pool, (new_conv_x, new_conv_bc) = state_stage(
-        range(half, states.shape[0]), d, x, w, b, states, accepts, [raw_x, raw_bc], [conv_pool_x, conv_pool_bc], begun
+    returned = [over_pool(one, True) for one in placed]
+    turned, _ = lax.optimization_barrier((turned, placed[-1]))
+    new_pool, new_conv_x = last_state_stage(
+        range(half, states.shape[0]), d, turned, b, states, accepts, raw_x, conv_pool_x, begun
     )
     returned, _ = lax.optimization_barrier((returned, new_conv_x))
     mixed = collect_stage(collect, returned)

time: 51.9 us -> 50 us (0.963)
  Pallas kernels: 25.4 us -> 22.3 us
  waiting for transfers between devices: 2.2 us -> 3.23 us
    pallas_call x7 -> x6, Pallas kernels: 12.3 us -> 9.69 us  [the longest x1 3.25 us: last_state_stage(): pl.pallas_call(functools.partial(last_state_kernel, span_of), out_shape=[...]
    ppermute x2, waiting for transfers between devices: 0.04 us -> 1.12 us  [body(): pieces[i] = lax.ppermute(pieces[i], 'tensor', completed(plan[i], n_tensor))]
    ppermute x1, waiting for transfers between devices: 0.71 us -> 0.06 us  [body(): core_got = [lax.ppermute(v, 'tensor', swap) for v in sends]]
    pallas_call x1, Pallas kernels: 4.13 us -> 3.51 us  [project_x(): pl.pallas_call(functools.partial(project_x_kernel, n_pool, cr, chunk), ou...]
    ppermute x14, starting transfers between devices: 20.1 us -> 20.7 us  [the longest x12 18.5 us: over_pool(): moved[step] = lax.ppermute(parts[step], 'pool', pairs)]
    ppermute x14, waiting for transfers between devices: 1.45 us -> 2.05 us  [the longest x12 1.3 us: over_pool(): moved[step] = lax.ppermute(parts[step], 'pool', pairs)]
  transfers between devices with their start and end apart: 18 -> 18, of which waited for: 3 -> 5; matrix products, arithmetic and copies ran while one was open for 0% -> 0% of each run, Pallas kernels for 35% -> 31%
where the time goes in v4:
time: 50 us; the launch traced here: 49.9 us
  starting transfers between devices  23.4 us (47%)
  Pallas kernels  22.3 us (45%)
  waiting for transfers between devices  3.23 us (6%)
  between operations  0.9 us (2%)
    ppermute x12, starting transfers between devices, over_pool(): moved[step] = lax.ppermute(parts[step], 'pool', pairs)  18.5 us
    pallas_call x1, Pallas kernels, project_bc(): pl.pallas_call(functools.partial(project_bc_kernel, n_pool, req, cr, chun...  3.75 us
    pallas_call x1, Pallas kernels, project_x(): pl.pallas_call(functools.partial(project_x_kernel, n_pool, cr, chunk), ou...  3.51 us
    pallas_call x1, Pallas kernels, last_state_stage(): pl.pallas_call(functools.partial(last_state_kernel, span_of), out_shape=[...  3.25 us
    pallas_call x1, Pallas kernels, first_state_stage(): pl.pallas_call(functools.partial(first_state_kernel, span_of), out_shape=...  3 us
    ppermute x2, starting transfers between devices, over_line(): lax.ppermute(v, 'tensor', [(r, (r // 2 + i) % n_line * 2 + r % 2) for r i...  2.15 us
    pallas_call x1, Pallas kernels, x_stage(): pl.pallas_call(functools.partial(x_kernel, n_pool), out_shape=[jax.ShapeD...  1.96 us
    pallas_call x1, Pallas kernels, pre_stage(): pl.pallas_call(functools.partial(pre_kernel, slots), out_shape=[jax.Shape...  1.92 us
  transfers between devices with their start and end apart: 18, of which 5 were waited for; matrix products, arithmetic and copies ran while one was open for 0% of the time, Pallas kernels for 31%

profile of v4, /device:TPU:0, one launch (start us, length us, event | category | flops | bytes accessed | tf_op | source)
XLA Modules:
  0.0 49.9 jit_solution(14945732791516851678)
XLA Ops:
  0.6 0.0 slice-start
  0.6 3.8 %shard_map.192 = (bf16[48,640]{1,0:T(8,128)(2,1)S(1)}, bf16[48,640]{1,0:T(8,128)(2,1)S(1)}, bf16[48,640]{1,0:T(8,128)(2,1)S(1)}, bf16[48,640]{1,0:T(8,128)(2,1)S...) custom-call(s32[1,64]{1,0:T(1,128)} %bitcast.15, ...), custom_call_target="tpu_custom_call" | custom-call | flops 536870912 | bytes 6291456 | tf_op jit(solution)/shard_map/pallas_call | solution.py:262
  4.4 3.1 %collective-permute-start.3 = (bf16[48,640]{1,0:T(8,128)(2,1)S(1)}, bf16[48,640]{1,0:T(8,128)(2,1)S(1)}, u32[]{:S(2)}, u32[]{:S(2)}) collective-permute-start(bf16[48,640]{1,0:T(8,128)(2,1)S(1)} %get-tuple-element.84), channel_id=1, source_target_pairs={{0,4},{4,8},{8,12},{12,0},{1,5},{5,9},{9,13},{13,1},{2,6},{6,10},{... | collective-permute-start | bytes 184328 | tf_op jit(solution)/shard_map/ppermute | solution.py:753
  7.5 2.6 %collective-permute-start.4 = (bf16[48,640]{1,0:T(8,128)(2,1)S(1)}, bf16[48,640]{1,0:T(8,128)(2,1)S(1)}, u32[]{:S(2)}, u32[]{:S(2)}) collective-permute-start(bf16[48,640]{1,0:T(8,128)(2,1)S(1)} %get-tuple-element.85), channel_id=1, source_target_pairs={{0,8},{4,12},{8,0},{12,4},{1,9},{5,13},{9,1},{13,5},{2,10},{6,14},... | collective-permute-start | bytes 184328 | tf_op jit(solution)/shard_map/ppermute | solution.py:753
  10.1 1.3 %collective-permute-start.5 = (bf16[48,640]{1,0:T(8,128)(2,1)S(1)}, bf16[48,640]{1,0:T(8,128)(2,1)S(1)}, u32[]{:S(2)}, u32[]{:S(2)}) collective-permute-start(bf16[48,640]{1,0:T(8,128)(2,1)S(1)} %get-tuple-element.86), channel_id=1, source_target_pairs={{0,12},{4,0},{8,4},{12,8},{1,13},{5,1},{9,5},{13,9},{2,14},{6,2},{... | collective-permute-start | bytes 184328 | tf_op jit(solution)/shard_map/ppermute | solution.py:753
  11.4 0.0 copy-start
  11.4 0.0 slice-start.1
  11.5 3.5 %shard_map.193 = (bf16[48,1024]{1,0:T(8,128)(2,1)S(1)}, bf16[48,1024]{1,0:T(8,128)(2,1)S(1)}, bf16[48,1024]{1,0:T(8,128)(2,1)S(1)}, bf16[48,1024]{1,0:T(8,128)(2,1)S(1)}) custom-call(bf16[128,4096]{1,0:T(8,128)(2,1)S(1)} %get-tuple-element.75.hbuf, bf16[1024,1024]{1,0:T(8,128)(2,1)S(1)} %get-tuple-element.76.head, bf16[4096,1024]{1,0:T(8,128)(2,1)} %w.5, ...), custom_call_target="tpu_custom_call" | custom-call | flops 1073741824 | bytes 9437184 | tf_op jit(solution)/shard_map/pallas_call | solution.py:311
  15.0 0.0 copy-start.1
  15.0 0.0 copy-start.3
  15.0 0.0 copy-start.5
  15.0 0.0 copy-start.8
  15.0 0.7 %collective-permute-start = (bf16[48,1024]{1,0:T(8,128)(2,1)S(1)}, bf16[48,1024]{1,0:T(8,128)(2,1)S(1)}, u32[]{:S(2)}, u32[]{:S(2)}) collective-permute-start(bf16[48,1024]{1,0:T(8,128)(2,1)S(1)} %get-tuple-element.79), channel_id=1, source_target_pairs={{0,4},{4,8},{8,12},{12,0},{1,5},{5,9},{9,13},{13,1},{2,6},{6,10},{... | collective-permute-start | bytes 294920 | tf_op jit(solution)/shard_map/ppermute | solution.py:753
  15.8 0.3 collective-permute-start.1
  16.1 2.8 %collective-permute-start.2 = (bf16[48,1024]{1,0:T(8,128)(2,1)S(1)}, bf16[48,1024]{1,0:T(8,128)(2,1)S(1)}, u32[]{:S(2)}, u32[]{:S(2)}) collective-permute-start(bf16[48,1024]{1,0:T(8,128)(2,1)S(1)} %get-tuple-element.81), channel_id=1, source_target_pairs={{0,12},{4,0},{8,4},{12,8},{1,13},{5,1},{9,5},{13,9},{2,14},{6,2},{... | collective-permute-start | bytes 294920 | tf_op jit(solution)/shard_map/ppermute | solution.py:753
  18.9 0.5 shard_map.194
  19.4 0.0 collective-permute-start.6
  19.4 1.6 %collective-permute-start.7 = (bf16[144,256]{1,0:T(8,128)(2,1)S(1)}, bf16[144,256]{1,0:T(8,128)(2,1)S(1)}, u32[]{:S(2)}, u32[]{:S(2)}) collective-permute-start(bf16[144,256]{1,0:T(8,128)(2,1)S(1)} %get-tuple-element.97), channel_id=1, source_target_pairs={{2,1},{1,2},{0,3},{3,0},{6,5},{5,6},{4,7},{7,4},{10,9},{9,10},{8,1... | collective-permute-start | bytes 221192 | tf_op jit(solution)/shard_map/ppermute | solution.py:765
  21.0 1.9 %shard_map.195 = (bf16[18,3,512]{2,1,0:T(4,128)(2,1)}, bf16[16,144,144]{2,1,0:T(8,128)(2,1)S(1)}, f32[144,1024]{1,0:T(8,128)S(1)}, f32[144,16]{1,0:T(8,128)S(1)}, f32[18,16]{1,0:T(8,128)S(1)}) custom-call(f32[144,1]{1,0:T(8,128)S(1)} %get-tuple-element.82.accepts_ref, f32[144,640]{1,0:T(8,128)S(1)} %get-tuple-element.91.raw_ref, ...), custom_call_target="tpu_custom_call" | custom-call | flops 1000000 | bytes 1000000 | tf_op jit(solution)/shard_map/pallas_call | solution.py:458
  22.9 1.1 %collective-permute-done.6.refs_1_ = bf16[144,256]{1,0:T(8,128)(2,1)S(1)} collective-permute-done((bf16[144,256]{1,0:T(8,128)(2,1)S(1)}, bf16[144,256]{1,0:T(8,128)(2,1)S(1)}, u32[]{:S(2)}, u32[]{:S(2)}) %collective-permute-start.6) | collective-permute-done | bytes 73760 | tf_op jit(solution)/shard_map/ppermute | solution.py:765
  24.1 0.0 collective-permute-done.7.refs_2_
  24.1 1.6 %shard_map.196 = (f32[144,1024]{1,0:T(8,128)S(1)}, bf16[16,144,144]{2,1,0:T(8,128)(2,1)S(1)}, bf16[144,256]{1,0:T(8,128)(2,1)S(1)}) custom-call(bf16[16,144,144]{2,1,0:T(8,128)(2,1)S(1)} %get-tuple-element.92.fade_m_ref, f32[144,1024]{1,0:T(8,128)S(1)} %get-tuple-element.93.fade_ref, bf16[18,16,64,128]{3,2,1,0:T(8,128)(2,1)S(1)} %copy-done, ...), custom_call_target="tpu_custom_call" | custom-call | flops 37748736 | bytes 4718592 | tf_op jit(solution)/shard_map/pallas_call | solution.py:516
  25.6 0.0 collective-permute-done.2.refs_3_
  25.7 2.0 %shard_map.197 = (bf16[128,1024]{1,0:T(8,128)(2,1)S(1)}, f32[144,1024]{1,0:T(8,128)S(1)}, f32[144,1024]{1,0:T(8,128)S(1)}) custom-call(bf16[144,192]{1,0:T(8,128)(2,1)S(1)} %get-tuple-element.73.owner_ref, bf16[128,144]{1,0:T(8,128)(2,1)S(1)} %get-tuple-element.74.pack_ref, bf16[48,1024]{1,0:T(8,128)(2,1)S(1)} %get-tuple-element.78.refs_0_, ...), custom_call_target="tpu_custom_call" | custom-call | flops 42467328 | bytes 4000000 | tf_op jit(solution)/shard_map/pallas_call | solution.py:553
  27.7 0.5 shard_map.199
  28.2 1.0 %collective-permute-start.8 = (bf16[128,1024]{1,0:T(8,128)(2,1)S(1)}, bf16[128,1024]{1,0:T(8,128)(2,1)S(1)}, u32[]{:S(2)}, u32[]{:S(2)}) collective-permute-start(bf16[128,1024]{1,0:T(8,128)(2,1)S(1)} %shard_map.199), channel_id=1, source_target_pairs={{0,1},{1,0},{2,3},{3,2},{4,5},{5,4},{6,7},{7,6},{8,9},{9,8},{10,11... | collective-permute-start | bytes 786440 | tf_op jit(solution)/shard_map/ppermute | solution.py:775
  29.2 1.0 %shard_map.198 = (f32[128,1024]{1,0:T(8,128)S(1)}, bf16[128,1024]{1,0:T(8,128)(2,1)S(1)}, f32[128,1024]{1,0:T(8,128)S(1)}) custom-call(bf16[128,1024]{1,0:T(8,128)(2,1)S(1)} %get-tuple-element.103.rows, bf16[1024,4096]{1,0:T(8,128)(2,1)S(1)} %bitcast.9), custom_call_target="tpu_custom_call" | custom-call | flops 805306368 | bytes 6291456 | tf_op jit(solution)/shard_map/pallas_call | solution.py:643
  30.2 0.1 collective-permute-start.9
  30.3 0.1 collective-permute-done.8.refs_1_
  30.3 0.1 shard_map.200
  30.4 1.4 %collective-permute-start.10 = (bf16[128,512]{1,0:T(8,128)(2,1)S(1)}, bf16[128,512]{1,0:T(8,128)(2,1)S(1)}, u32[]{:S(2)}, u32[]{:S(2)}) collective-permute-start(bf16[128,512]{1,0:T(8,128)(2,1)S(1)} %get-tuple-element.108), channel_id=1, source_target_pairs={{0,2},{1,3},{2,0},{3,1},{4,6},{5,7},{6,4},{7,5},{8,10},{9,11},{10,... | collective-permute-start | bytes 393224 | tf_op jit(solution)/shard_map/ppermute | solution.py:783
  31.8 3.0 %shard_map.201 = (bf16[18,16,64,128]{3,2,1,0:T(8,128)(2,1)}, bf16[1024,144]{1,0:T(8,128)(2,1)S(1)}) custom-call(f32[18,16]{1,0:T(8,128)S(1)} %get-tuple-element.105.d_ref, f32[144,1024]{1,0:T(8,128)S(1)} %get-tuple-element.110.x_ref, f32[144,16]{1,0:T(8,128)S(1)} %get-tuple-element.111.w_ref, bf16[144,256]{1,0:T(8,128)(2,1)S(1)} %get-tuple-element.112.b_ref, ...), custom_call_target="tpu_custom_call" | custom-call | flops 37748736 | bytes 4718592 | tf_op jit(solution)/shard_map/pallas_call | solution.py:595
  34.8 0.8 %collective-permute-start.14 = (bf16[128,512]{1,0:T(8,128)(2,1)S(1)}, bf16[128,512]{1,0:T(8,128)(2,1)S(1)}, u32[]{:S(2)}, u32[]{:S(2)}) collective-permute-start(bf16[128,512]{1,0:T(8,128)(2,1)S(1)} %get-tuple-element.121), channel_id=1, source_target_pairs={{0,2},{1,3},{2,0},{3,1},{4,6},{5,7},{6,4},{7,5},{8,10},{9,11},{10,... | collective-permute-start | bytes 393224 | tf_op jit(solution)/shard_map/ppermute | solution.py:783
  35.5 0.7 %collective-permute-done.10.refs_0_ = bf16[128,512]{1,0:T(8,128)(2,1)S(1)} collective-permute-done((bf16[128,512]{1,0:T(8,128)(2,1)S(1)}, bf16[128,512]{1,0:T(8,128)(2,1)S(1)}, u32[]{:S(2)}, u32[]{:S(2)}) %collective-permute-start.10) | collective-permute-done | bytes 131104 | tf_op jit(solution)/shard_map/ppermute | solution.py:783
  36.3 0.2 shard_map.202
  36.5 1.3 %collective-permute-start.11 = (bf16[48,512]{1,0:T(8,128)(2,1)S(1)}, bf16[48,512]{1,0:T(8,128)(2,1)S(1)}, u32[]{:S(2)}, u32[]{:S(2)}) collective-permute-start(bf16[48,512]{1,0:T(8,128)(2,1)S(1)} %get-tuple-element.118), channel_id=1, source_target_pairs={{4,0},{8,4},{12,8},{0,12},{5,1},{9,5},{13,9},{1,13},{6,2},{10,6},{... | collective-permute-start | bytes 147464 | tf_op jit(solution)/shard_map/ppermute | solution.py:753
  37.8 0.7 %collective-permute-start.12 = (bf16[48,512]{1,0:T(8,128)(2,1)S(1)}, bf16[48,512]{1,0:T(8,128)(2,1)S(1)}, u32[]{:S(2)}, u32[]{:S(2)}) collective-permute-start(bf16[48,512]{1,0:T(8,128)(2,1)S(1)} %get-tuple-element.119), channel_id=1, source_target_pairs={{8,0},{12,4},{0,8},{4,12},{9,1},{13,5},{1,9},{5,13},{10,2},{14,6},... | collective-permute-start | bytes 147464 | tf_op jit(solution)/shard_map/ppermute | solution.py:753
  38.5 1.9 %collective-permute-start.13 = (bf16[48,512]{1,0:T(8,128)(2,1)S(1)}, bf16[48,512]{1,0:T(8,128)(2,1)S(1)}, u32[]{:S(2)}, u32[]{:S(2)}) collective-permute-start(bf16[48,512]{1,0:T(8,128)(2,1)S(1)} %get-tuple-element.120), channel_id=1, source_target_pairs={{12,0},{0,4},{4,8},{8,12},{13,1},{1,5},{5,9},{9,13},{14,2},{2,6},{... | collective-permute-start | bytes 147464 | tf_op jit(solution)/shard_map/ppermute | solution.py:753
  40.3 0.0 collective-permute-done.14.refs_0_
  40.3 0.2 shard_map.203
  40.6 2.0 %collective-permute-start.15 = (bf16[48,512]{1,0:T(8,128)(2,1)S(1)}, bf16[48,512]{1,0:T(8,128)(2,1)S(1)}, u32[]{:S(2)}, u32[]{:S(2)}) collective-permute-start(bf16[48,512]{1,0:T(8,128)(2,1)S(1)} %get-tuple-element.123), channel_id=1, source_target_pairs={{4,0},{8,4},{12,8},{0,12},{5,1},{9,5},{13,9},{1,13},{6,2},{10,6},{... | collective-permute-start | bytes 147464 | tf_op jit(solution)/shard_map/ppermute | solution.py:753
  42.6 0.5 collective-permute-start.16
  43.1 0.0 collective-permute-done.11.parts_0__1_
  43.1 1.3 %collective-permute-start.17 = (bf16[48,512]{1,0:T(8,128)(2,1)S(1)}, bf16[48,512]{1,0:T(8,128)(2,1)S(1)}, u32[]{:S(2)}, u32[]{:S(2)}) collective-permute-start(bf16[48,512]{1,0:T(8,128)(2,1)S(1)} %get-tuple-element.125), channel_id=1, source_target_pairs={{12,0},{0,4},{4,8},{8,12},{13,1},{1,5},{5,9},{9,13},{14,2},{2,6},{... | collective-permute-start | bytes 147464 | tf_op jit(solution)/shard_map/ppermute | solution.py:753
  44.4 3.2 %shard_map.204 = (bf16[18,16,64,128]{3,2,1,0:T(8,128)(2,1)}, bf16[18,3,1024]{2,1,0:T(4,128)(2,1)}) custom-call(f32[18,16]{1,0:T(8,128)S(1)} %get-tuple-element.105.d_ref, bf16[1024,144]{1,0:T(8,128)(2,1)S(1)} %get-tuple-element.127.turned_ref, bf16[144,256]{1,0:T(8,128)(2,1)S(1)} %get-tuple-element.112.b_ref, ...), custom_call_target="tpu_custom_call", output_to_operand_aliasing={{0}: (7, {})} | custom-call | flops 37748736 | bytes 4718592 | tf_op jit(solution)/shard_map/pallas_call | solution.py:616
  47.7 0.2 collective-permute-done.16.parts_1__2_
  47.9 1.0 %collective-permute-done.17.parts_1__3_ = bf16[48,512]{1,0:T(8,128)(2,1)S(1)} collective-permute-done((bf16[48,512]{1,0:T(8,128)(2,1)S(1)}, bf16[48,512]{1,0:T(8,128)(2,1)S(1)}, u32[]{:S(2)}, u32[]{:S(2)}) %collective-permute-start.17) | collective-permute-done | bytes 49184 | tf_op jit(solution)/shard_map/ppermute | solution.py:753
  48.9 0.9 %shard_map.205 = bf16[128,1024]{1,0:T(8,128)(2,1)} custom-call(bf16[128,192]{1,0:T(8,128)(2,1)S(1)} %get-tuple-element.72.collect_ref, bf16[48,512]{1,0:T(8,128)(2,1)S(1)} %get-tuple-element.130.parts_0__0_, bf16[48,512]{1,0:T(8,128)(2,1)S(1)} %collective-permute-done.11.parts_0__1_, bf16[48,512]{1,0:T(8,128)(2,1)S(1)} %collective-permute-done.12.parts_0__2_, ...), custom_call_target="tpu_custom_call" | custom-call | flops 1000000 | bytes 1000000 | tf_op jit(solution)/shard_map/pallas_call | solution.py:706
  (25 shorter events, 0.1 us)
Async XLA Ops:
  0.6 27.1 %slice-start = ((s8[8388608]{0:T(1024)(128)(4,1)}), s8[4194304]{0:T(1024)(128)(4,1)S(1)}, s32[]{:S(2)}) async-start(s8[8388608]{0:T(1024)(128)(4,1)} %bitcast.8), calls=%async_computation | async-start | bytes 8388608
  4.4 11.7 %collective-permute-start.3 = (bf16[48,640]{1,0:T(8,128)(2,1)S(1)}, bf16[48,640]{1,0:T(8,128)(2,1)S(1)}, u32[]{:S(2)}, u32[]{:S(2)}) collective-permute-start(bf16[48,640]{1,0:T(8,128)(2,1)S(1)} %get-tuple-element.84), channel_id=1, source_target_pairs={{0,4},{4,8},{8,12},{12,0},{1,5},{5,9},{9,13},{13,1},{2,6},{6,10},{... | collective-permute-start | bytes 184328 | tf_op jit(solution)/shard_map/ppermute | solution.py:753
  7.5 11.4 %collective-permute-start.4 = (bf16[48,640]{1,0:T(8,128)(2,1)S(1)}, bf16[48,640]{1,0:T(8,128)(2,1)S(1)}, u32[]{:S(2)}, u32[]{:S(2)}) collective-permute-start(bf16[48,640]{1,0:T(8,128)(2,1)S(1)} %get-tuple-element.85), channel_id=1, source_target_pairs={{0,8},{4,12},{8,0},{12,4},{1,9},{5,13},{9,1},{13,5},{2,10},{6,14},... | collective-permute-start | bytes 184328 | tf_op jit(solution)/shard_map/ppermute | solution.py:753
  10.1 8.8 %collective-permute-start.5 = (bf16[48,640]{1,0:T(8,128)(2,1)S(1)}, bf16[48,640]{1,0:T(8,128)(2,1)S(1)}, u32[]{:S(2)}, u32[]{:S(2)}) collective-permute-start(bf16[48,640]{1,0:T(8,128)(2,1)S(1)} %get-tuple-element.86), channel_id=1, source_target_pairs={{0,12},{4,0},{8,4},{12,8},{1,13},{5,1},{9,5},{13,9},{2,14},{6,2},{... | collective-permute-start | bytes 184328 | tf_op jit(solution)/shard_map/ppermute | solution.py:753
  11.4 7.5 %copy-start.2 = (bf16[18,3,512]{2,1,0:T(4,128)(2,1)S(1)}, bf16[18,3,512]{2,1,0:T(4,128)(2,1)}, u32[]{:S(2)}) copy-start(bf16[18,3,512]{2,1,0:T(4,128)(2,1)} %conv_ref.2) | copy-start | bytes 165892
  11.4 7.5 %copy-start.4 = (f32[4,512]{1,0:T(4,128)S(1)}, f32[4,512]{1,0:T(4,128)}, u32[]{:S(2)}) copy-start(f32[4,512]{1,0:T(4,128)} %refs_5_.2) | copy-start | bytes 24580
  11.4 9.6 %copy-start.6 = (f32[16]{0:T(128)S(1)}, f32[16]{0:T(128)}, u32[]{:S(2)}) copy-start(f32[16]{0:T(128)} %param.23) | copy-start | bytes 196
  11.4 9.6 %copy-start.7 = (f32[16]{0:T(128)S(1)}, f32[16]{0:T(128)}, u32[]{:S(2)}) copy-start(f32[16]{0:T(128)} %param.24) | copy-start | bytes 196
  11.4 12.6 %copy-start = (bf16[18,16,64,128]{3,2,1,0:T(8,128)(2,1)S(1)}, bf16[18,16,64,128]{3,2,1,0:T(8,128)(2,1)}, u32[]{:S(2)}) copy-start(bf16[18,16,64,128]{3,2,1,0:T(8,128)(2,1)} %pool.1) | copy-start | bytes 14155780
  11.4 16.3 %slice-start.1 = ((s8[8388608]{0:T(1024)(128)(4,1)}), s8[4194304]{0:T(1024)(128)(4,1)S(1)}, s32[]{:S(2)}) async-start(s8[8388608]{0:T(1024)(128)(4,1)} %bitcast.8), calls=%async_computation.1 | async-start | bytes 8388608
  15.0 10.7 %copy-start.1 = (bf16[18,3,1024]{2,1,0:T(4,128)(2,1)S(1)}, bf16[18,3,1024]{2,1,0:T(4,128)(2,1)}, u32[]{:S(2)}) copy-start(bf16[18,3,1024]{2,1,0:T(4,128)(2,1)} %conv_ref.3) | copy-start | bytes 331780
  15.0 10.7 %copy-start.3 = (f32[4,1024]{1,0:T(4,128)S(1)}, f32[4,1024]{1,0:T(4,128)}, u32[]{:S(2)}) copy-start(f32[4,1024]{1,0:T(4,128)} %refs_5_.3) | copy-start | bytes 49156
  15.0 10.7 %copy-start.5 = (f32[1024]{0:T(1024)S(1)}, f32[1024]{0:T(1024)}, u32[]{:S(2)}) copy-start(f32[1024]{0:T(1024)} %param.26) | copy-start | bytes 12292
  15.0 10.7 %copy-start.8 = (f32[16]{0:T(128)S(1)}, f32[16]{0:T(128)}, u32[]{:S(2)}) copy-start(f32[16]{0:T(128)} %param.25) | copy-start | bytes 196
  15.0 10.6 %collective-permute-start = (bf16[48,1024]{1,0:T(8,128)(2,1)S(1)}, bf16[48,1024]{1,0:T(8,128)(2,1)S(1)}, u32[]{:S(2)}, u32[]{:S(2)}) collective-permute-start(bf16[48,1024]{1,0:T(8,128)(2,1)S(1)} %get-tuple-element.79), channel_id=1, source_target_pairs={{0,4},{4,8},{8,12},{12,0},{1,5},{5,9},{9,13},{13,1},{2,6},{6,10},{... | collective-permute-start | bytes 294920 | tf_op jit(solution)/shard_map/ppermute | solution.py:753
  15.8 9.9 %collective-permute-start.1 = (bf16[48,1024]{1,0:T(8,128)(2,1)S(1)}, bf16[48,1024]{1,0:T(8,128)(2,1)S(1)}, u32[]{:S(2)}, u32[]{:S(2)}) collective-permute-start(bf16[48,1024]{1,0:T(8,128)(2,1)S(1)} %get-tuple-element.80), channel_id=1, source_target_pairs={{0,8},{4,12},{8,0},{12,4},{1,9},{5,13},{9,1},{13,5},{2,10},{6,14},... | collective-permute-start | bytes 294920 | tf_op jit(solution)/shard_map/ppermute | solution.py:753
  16.1 9.6 %collective-permute-start.2 = (bf16[48,1024]{1,0:T(8,128)(2,1)S(1)}, bf16[48,1024]{1,0:T(8,128)(2,1)S(1)}, u32[]{:S(2)}, u32[]{:S(2)}) collective-permute-start(bf16[48,1024]{1,0:T(8,128)(2,1)S(1)} %get-tuple-element.81), channel_id=1, source_target_pairs={{0,12},{4,0},{8,4},{12,8},{1,13},{5,1},{9,5},{13,9},{2,14},{6,2},{... | collective-permute-start | bytes 294920 | tf_op jit(solution)/shard_map/ppermute | solution.py:753
  19.4 4.7 %collective-permute-start.6 = (bf16[144,256]{1,0:T(8,128)(2,1)S(1)}, bf16[144,256]{1,0:T(8,128)(2,1)S(1)}, u32[]{:S(2)}, u32[]{:S(2)}) collective-permute-start(bf16[144,256]{1,0:T(8,128)(2,1)S(1)} %get-tuple-element.96), channel_id=1, source_target_pairs={{2,0},{0,1},{3,2},{1,3},{6,4},{4,5},{7,6},{5,7},{10,8},{8,9},{11,1... | collective-permute-start | bytes 221192 | tf_op jit(solution)/shard_map/ppermute | solution.py:765
  19.4 4.6 %collective-permute-start.7 = (bf16[144,256]{1,0:T(8,128)(2,1)S(1)}, bf16[144,256]{1,0:T(8,128)(2,1)S(1)}, u32[]{:S(2)}, u32[]{:S(2)}) collective-permute-start(bf16[144,256]{1,0:T(8,128)(2,1)S(1)} %get-tuple-element.97), channel_id=1, source_target_pairs={{2,1},{1,2},{0,3},{3,0},{6,5},{5,6},{4,7},{7,4},{10,9},{9,10},{8,1... | collective-permute-start | bytes 221192 | tf_op jit(solution)/shard_map/ppermute | solution.py:765
  28.2 2.1 %collective-permute-start.8 = (bf16[128,1024]{1,0:T(8,128)(2,1)S(1)}, bf16[128,1024]{1,0:T(8,128)(2,1)S(1)}, u32[]{:S(2)}, u32[]{:S(2)}) collective-permute-start(bf16[128,1024]{1,0:T(8,128)(2,1)S(1)} %shard_map.199), channel_id=1, source_target_pairs={{0,1},{1,0},{2,3},{3,2},{4,5},{5,4},{6,7},{7,6},{8,9},{9,8},{10,11... | collective-permute-start | bytes 786440 | tf_op jit(solution)/shard_map/ppermute | solution.py:775
  30.2 5.4 %collective-permute-start.9 = (bf16[128,1024]{1,0:T(8,128)(2,1)S(1)}, bf16[128,1024]{1,0:T(8,128)(2,1)S(1)}, u32[]{:S(2)}, u32[]{:S(2)}) collective-permute-start(bf16[128,1024]{1,0:T(8,128)(2,1)S(1)} %get-tuple-element.115), channel_id=1, source_target_pairs={{0,1},{1,0},{2,3},{3,2},{4,5},{5,4},{6,7},{7,6},{8,9},{9,8},{10,11... | collective-permute-start | bytes 786440 | tf_op jit(solution)/shard_map/ppermute | solution.py:788
  30.4 5.9 %collective-permute-start.10 = (bf16[128,512]{1,0:T(8,128)(2,1)S(1)}, bf16[128,512]{1,0:T(8,128)(2,1)S(1)}, u32[]{:S(2)}, u32[]{:S(2)}) collective-permute-start(bf16[128,512]{1,0:T(8,128)(2,1)S(1)} %get-tuple-element.108), channel_id=1, source_target_pairs={{0,2},{1,3},{2,0},{3,1},{4,6},{5,7},{6,4},{7,5},{8,10},{9,11},{10,... | collective-permute-start | bytes 393224 | tf_op jit(solution)/shard_map/ppermute | solution.py:783
  34.8 5.6 %collective-permute-start.14 = (bf16[128,512]{1,0:T(8,128)(2,1)S(1)}, bf16[128,512]{1,0:T(8,128)(2,1)S(1)}, u32[]{:S(2)}, u32[]{:S(2)}) collective-permute-start(bf16[128,512]{1,0:T(8,128)(2,1)S(1)} %get-tuple-element.121), channel_id=1, source_target_pairs={{0,2},{1,3},{2,0},{3,1},{4,6},{5,7},{6,4},{7,5},{8,10},{9,11},{10,... | collective-permute-start | bytes 393224 | tf_op jit(solution)/shard_map/ppermute | solution.py:783
  36.5 6.5 %collective-permute-start.11 = (bf16[48,512]{1,0:T(8,128)(2,1)S(1)}, bf16[48,512]{1,0:T(8,128)(2,1)S(1)}, u32[]{:S(2)}, u32[]{:S(2)}) collective-permute-start(bf16[48,512]{1,0:T(8,128)(2,1)S(1)} %get-tuple-element.118), channel_id=1, source_target_pairs={{4,0},{8,4},{12,8},{0,12},{5,1},{9,5},{13,9},{1,13},{6,2},{10,6},{... | collective-permute-start | bytes 147464 | tf_op jit(solution)/shard_map/ppermute | solution.py:753
  37.8 9.8 %collective-permute-start.12 = (bf16[48,512]{1,0:T(8,128)(2,1)S(1)}, bf16[48,512]{1,0:T(8,128)(2,1)S(1)}, u32[]{:S(2)}, u32[]{:S(2)}) collective-permute-start(bf16[48,512]{1,0:T(8,128)(2,1)S(1)} %get-tuple-element.119), channel_id=1, source_target_pairs={{8,0},{12,4},{0,8},{4,12},{9,1},{13,5},{1,9},{5,13},{10,2},{14,6},... | collective-permute-start | bytes 147464 | tf_op jit(solution)/shard_map/ppermute | solution.py:753
  38.5 9.2 %collective-permute-start.13 = (bf16[48,512]{1,0:T(8,128)(2,1)S(1)}, bf16[48,512]{1,0:T(8,128)(2,1)S(1)}, u32[]{:S(2)}, u32[]{:S(2)}) collective-permute-start(bf16[48,512]{1,0:T(8,128)(2,1)S(1)} %get-tuple-element.120), channel_id=1, source_target_pairs={{12,0},{0,4},{4,8},{8,12},{13,1},{1,5},{5,9},{9,13},{14,2},{2,6},{... | collective-permute-start | bytes 147464 | tf_op jit(solution)/shard_map/ppermute | solution.py:753
  40.6 7.1 %collective-permute-start.15 = (bf16[48,512]{1,0:T(8,128)(2,1)S(1)}, bf16[48,512]{1,0:T(8,128)(2,1)S(1)}, u32[]{:S(2)}, u32[]{:S(2)}) collective-permute-start(bf16[48,512]{1,0:T(8,128)(2,1)S(1)} %get-tuple-element.123), channel_id=1, source_target_pairs={{4,0},{8,4},{12,8},{0,12},{5,1},{9,5},{13,9},{1,13},{6,2},{10,6},{... | collective-permute-start | bytes 147464 | tf_op jit(solution)/shard_map/ppermute | solution.py:753
  42.6 5.4 %collective-permute-start.16 = (bf16[48,512]{1,0:T(8,128)(2,1)S(1)}, bf16[48,512]{1,0:T(8,128)(2,1)S(1)}, u32[]{:S(2)}, u32[]{:S(2)}) collective-permute-start(bf16[48,512]{1,0:T(8,128)(2,1)S(1)} %get-tuple-element.124), channel_id=1, source_target_pairs={{8,0},{12,4},{0,8},{4,12},{9,1},{13,5},{1,9},{5,13},{10,2},{14,6},... | collective-permute-start | bytes 147464 | tf_op jit(solution)/shard_map/ppermute | solution.py:753
  43.1 5.9 %collective-permute-start.17 = (bf16[48,512]{1,0:T(8,128)(2,1)S(1)}, bf16[48,512]{1,0:T(8,128)(2,1)S(1)}, u32[]{:S(2)}, u32[]{:S(2)}) collective-permute-start(bf16[48,512]{1,0:T(8,128)(2,1)S(1)} %get-tuple-element.125), channel_id=1, source_target_pairs={{12,0},{0,4},{4,8},{8,12},{13,1},{1,5},{5,9},{9,13},{14,2},{2,6},{... | collective-permute-start | bytes 147464 | tf_op jit(solution)/shard_map/ppermute | solution.py:753

commit v5 on v4

--- a/solution.py
+++ b/solution.py
@@ -150,16 +150,24 @@
     return old.reshape(slots * DRAFT, width)
 
 
-def conv_slots(raw, pool, weight):
-    rows, width = raw.shape
-    window = pool.shape[1]
+def conv_old(pool, weight):
+    slots, window, width = pool.shape
+    rows = slots * DRAFT
     old = padded_pool(pool, width)
     position = iota((rows, width), 0) & (DRAFT - 1)
+    summed = jnp.zeros((rows, width), F32)
+    for back in range(1, window + 1):
+        part = pltpu.roll(old, (back - window) % rows, 0)
+        summed = summed + weight[window - back] * jnp.where(position < back, part, 0.0)
+    return summed
+
+
+def conv_new(raw, weight, window):
+    position = iota(raw.shape, 0) & (DRAFT - 1)
     summed = weight[window] * raw
     for back in range(1, window + 1):
-        new_part = pltpu.roll(raw, back, 0)
-        old_part = pltpu.roll(old, (back - window) % rows, 0)
-        summed = summed + weight[window - back] * jnp.where(position < back, old_part, new_part)
+        part = pltpu.roll(raw, back, 0)
+        summed = summed + weight[window - back] * jnp.where(position < back, 0.0, part)
     return summed
 
 
@@ -257,7 +265,7 @@
 
 def project_bc(tables, hidden, w, w_dt, w_x, slots, n_pool, req, cr):
     tokens, depth = hidden.shape
-    chunk = min(512, depth)
+    chunk = min(1024, depth)
     width, rows = w.shape[1], slots * DRAFT
     outs = pl.pallas_call(
         functools.partial(project_bc_kernel, n_pool, req, cr, chunk, slots),
@@ -380,7 +388,9 @@
     rank = lax.axis_index("tensor").astype(jnp.int32)
     raw = dot(owner_ref[...], jnp.concatenate([g[...] for g in got], axis=0))
     raw_ref[...] = raw
-    act_ref[...] = silu(conv_slots(raw[:, :width], pool_ref[...], weight_ref[...])).astype(BF16)
+    window = pool_ref.shape[1]
+    summed = conv_old(pool_ref[...], weight_ref[...]) + conv_new(raw[:, :width], weight_ref[...], window)
+    act_ref[...] = silu(summed).astype(BF16)
     for table, out in zip(parts, outs):
         piece = out.shape[1]
         out[...] = act_ref[:, pl.ds(pl.multiple_of(pick(rank, table) * piece, 128), piece)]
@@ -408,7 +418,7 @@
     )(owner, *got, pool, weight)
 
 
-def pre_kernel(slots, accepts_ref, raw_ref, conv_ref, bias_ref, alog_ref, kept_ref, m_ref, fade_ref, w_ref, d_ref):
+def pre_kernel(slots, accepts_ref, raw_ref, conv_ref, bias_ref, alog_ref, x_pool_ref, x_weight_ref, old_ref, kept_ref, m_ref, fade_ref, w_ref, d_ref):
     heads = w_ref.shape[1]
     rows = slots * DRAFT
     accepts = accepts_ref[...]
@@ -449,26 +459,28 @@
     for h in range(heads):
         m_ref[h] = dot(fade, hot(same & (head == h))).astype(BF16)
     fade_ref[...] = spread(jnp.exp(logs), spread_matrix(heads))
+    old_ref[...] = conv_old(x_pool_ref[...], x_weight_ref[...])
     kept_ref[...] = kept_rows(raw_ref[:, :width], conv_ref[...], accepts)
 
 
-def pre_stage(accepts, raw, conv_pool, bias, a_log, pool):
+def pre_stage(accepts, raw, conv_pool, bias, a_log, x_pool, x_weight, pool):
     slots, heads = pool.shape[:2]
     rows = slots * DRAFT
     return pl.pallas_call(
         functools.partial(pre_kernel, slots),
         out_shape=[
+            jax.ShapeDtypeStruct((rows, heads * HEAD_DIM), F32),
             jax.ShapeDtypeStruct(conv_pool.shape, BF16),
             jax.ShapeDtypeStruct((heads, rows, rows), BF16),
             jax.ShapeDtypeStruct((rows, heads * HEAD_DIM), F32),
             jax.ShapeDtypeStruct((rows, heads), F32),
             jax.ShapeDtypeStruct((slots, heads), F32),
         ],
-        in_specs=[VMEM] * 5,
-        out_specs=[VMEM] * 5,
+        in_specs=[VMEM] * 7,
+        out_specs=[VMEM] * 6,
         compiler_params=params(10),
         cost_estimate=cost(1e6, 1e6),
-    )(accepts, raw, conv_pool, bias, a_log)
+    )(accepts, raw, conv_pool, bias, a_log, x_pool, x_weight)
 
 
 def mix_kernel(kinds, fade_m_ref, fade_ref, states, *refs):
@@ -530,16 +542,22 @@
 
 def x_kernel(n_pool, owner_ref, pack_ref, *refs):
     got, refs = refs[:n_pool], refs[n_pool:]
-    pool_ref, weight_ref, y_ref, m_ref, skip_ref, gain_ref = refs[:6]
+    old_ref, weight_ref, y_ref, m_ref, skip_ref, gain_ref = refs[:6]
     normed_ref, x_ref, raw_ref = refs[6:]
-    heads = pool_ref.shape[2] // HEAD_DIM
+    heads = old_ref.shape[1] // HEAD_DIM
     raw = dot(owner_ref[...], jnp.concatenate([g[...] for g in got], axis=0))
     raw_ref[...] = raw
-    x = silu(conv_slots(raw, pool_ref[...], weight_ref[...]))
+    x = silu(old_ref[...] + conv_new(raw, weight_ref[...], weight_ref.shape[0] - 1))
     x_ref[...] = x
     matrix = spread_matrix(heads)
     small = x.astype(BF16)
-    parts = [dot(m_ref[h], small[:, h * HEAD_DIM : (h + 1) * HEAD_DIM]) for h in range(heads)]
+    rows = x.shape[0]
+    left = iota((rows, 2 * HEAD_DIM), 1) < HEAD_DIM
+    parts = []
+    for h in range(0, heads, 2):
+        both = m_ref[h : h + 2].reshape(2 * rows, rows)
+        both = dot(both, small[:, h * HEAD_DIM : (h + 2) * HEAD_DIM])
+        parts.append(jnp.where(left, both[:rows], both[rows:]))
     y = jnp.concatenate(parts, axis=1) + y_ref[...] + spread(skip_ref[...], matrix) * x
     square = (y * y).astype(BF16)
     scale = lax.rsqrt(dot_t(square, matrix) * (1.0 / HEAD_DIM) + EPS)
@@ -547,9 +565,8 @@
     normed_ref[...] = dot(pack_ref[...], normed).astype(BF16)
 
 
-def x_stage(owner, pack, got, pool, weight, y, m, skip, gain, n_pool):
-    slots, _, width = pool.shape
-    rows = slots * DRAFT
+def x_stage(owner, pack, got, old, weight, y, m, skip, gain, n_pool):
+    rows, width = old.shape
     return pl.pallas_call(
         functools.partial(x_kernel, n_pool),
         out_shape=[jax.ShapeDtypeStruct((pack.shape[0], width), BF16)] + [jax.ShapeDtypeStruct((rows, width), F32)] * 2,
@@ -557,7 +574,7 @@
         out_specs=[VMEM] * 3,
         compiler_params=params(16),
         cost_estimate=cost(2 * rows * rows * width, 4e6),
-    )(owner, pack, *got, pool, weight, y, m, skip, gain)
+    )(owner, pack, *got, old, weight, y, m, skip, gain)
 
 
 def fill_states(span_of, d_ref, turned, b_ref, pool, new_pool, buf, out_sems):
@@ -763,12 +780,14 @@
     raw_bc, *pieces = bc_stage(owner, bc_got, conv_pool_bc, conv_bc, plan, span, n_pool, n_tensor)
     for i in range(1, len(plan)):
         pieces[i] = lax.ppermute(pieces[i], "tensor", completed(plan[i], n_tensor))
-    new_conv_bc, fade_m, fade, w, d = pre_stage(accepts, raw_bc, conv_pool_bc, row(dt_bias), row(a_log), ssm_pool)
+    old_x, new_conv_bc, fade_m, fade, w, d = pre_stage(
+        accepts, raw_bc, conv_pool_bc, row(dt_bias), row(a_log), conv_pool_x, conv_x, ssm_pool
+    )
     states, _ = lax.optimization_barrier((ssm_pool, x_sent))
     states = pltpu.with_memory_space_constraint(states, pltpu.VMEM)
     pieces, _ = lax.optimization_barrier((pieces, fade))
     y, m, b = mix_stage(fade_m, fade, states, pieces, plan, n_tensor)
-    normed, x, raw_x = x_stage(owner, pack, x_got, conv_pool_x, conv_x, y, m, row(d_skip), row(norm_gain), n_pool)
+    normed, x, raw_x = x_stage(owner, pack, x_got, old_x, conv_x, y, m, row(d_skip), row(norm_gain), n_pool)
     ahead = list(range(1, n_line))
     swap = [(i, i ^ 1) for i in range(n_tensor)]
     sends = out_stage(normed, w_out, [(i, True) for i in ahead], n_line)

time: 50 us -> 49.8 us (level)
  no operation moved by 1% of the time
where the time goes in v5:
time: 49.8 us; the launch traced here: 49.7 us
  starting transfers between devices  23.4 us (47%)
  Pallas kernels  22.4 us (45%)
  waiting for transfers between devices  2.95 us (6%)
  between operations  0.88 us (2%)
    ppermute x12, starting transfers between devices, over_pool(): moved[step] = lax.ppermute(parts[step], 'pool', pairs)  18.6 us
    pallas_call x1, Pallas kernels, project_bc(): pl.pallas_call(functools.partial(project_bc_kernel, n_pool, req, cr, chun...  3.61 us
    pallas_call x1, Pallas kernels, project_x(): pl.pallas_call(functools.partial(project_x_kernel, n_pool, cr, chunk), ou...  3.5 us
    pallas_call x1, Pallas kernels, last_state_stage(): pl.pallas_call(functools.partial(last_state_kernel, span_of), out_shape=[...  3.25 us
    pallas_call x1, Pallas kernels, first_state_stage(): pl.pallas_call(functools.partial(first_state_kernel, span_of), out_shape=...  3 us
    pallas_call x1, Pallas kernels, pre_stage(): pl.pallas_call(functools.partial(pre_kernel, slots), out_shape=[jax.Shape...  2.18 us
    ppermute x2, starting transfers between devices, over_line(): lax.ppermute(v, 'tensor', [(r, (r // 2 + i) % n_line * 2 + r % 2) for r i...  2.15 us
    pallas_call x1, Pallas kernels, x_stage(): pl.pallas_call(functools.partial(x_kernel, n_pool), out_shape=[jax.ShapeD...  1.87 us
  transfers between devices with their start and end apart: 18, of which 5 were waited for; matrix products, arithmetic and copies ran while one was open for 0% of the time, Pallas kernels for 31%

profile of v5, /device:TPU:0, one launch (start us, length us, event | category | flops | bytes accessed | tf_op | source)
XLA Modules:
  0.0 49.7 jit_solution(17126138670517623234)
XLA Ops:
  0.6 0.0 slice-start
  0.6 3.6 %shard_map.192 = (bf16[48,640]{1,0:T(8,128)(2,1)S(1)}, bf16[48,640]{1,0:T(8,128)(2,1)S(1)}, bf16[48,640]{1,0:T(8,128)(2,1)S(1)}, bf16[48,640]{1,0:T(8,128)(2,1)S...) custom-call(s32[1,64]{1,0:T(1,128)} %bitcast.15, ...), custom_call_target="tpu_custom_call" | custom-call | flops 536870912 | bytes 6291456 | tf_op jit(solution)/shard_map/pallas_call | solution.py:270
  4.3 3.1 %collective-permute-start.3 = (bf16[48,640]{1,0:T(8,128)(2,1)S(1)}, bf16[48,640]{1,0:T(8,128)(2,1)S(1)}, u32[]{:S(2)}, u32[]{:S(2)}) collective-permute-start(bf16[48,640]{1,0:T(8,128)(2,1)S(1)} %get-tuple-element.85), channel_id=1, source_target_pairs={{0,4},{4,8},{8,12},{12,0},{1,5},{5,9},{9,13},{13,1},{2,6},{6,10},{... | collective-permute-start | bytes 184328 | tf_op jit(solution)/shard_map/ppermute | solution.py:770
  7.3 2.6 %collective-permute-start.4 = (bf16[48,640]{1,0:T(8,128)(2,1)S(1)}, bf16[48,640]{1,0:T(8,128)(2,1)S(1)}, u32[]{:S(2)}, u32[]{:S(2)}) collective-permute-start(bf16[48,640]{1,0:T(8,128)(2,1)S(1)} %get-tuple-element.86), channel_id=1, source_target_pairs={{0,8},{4,12},{8,0},{12,4},{1,9},{5,13},{9,1},{13,5},{2,10},{6,14},... | collective-permute-start | bytes 184328 | tf_op jit(solution)/shard_map/ppermute | solution.py:770
  9.9 1.3 %collective-permute-start.5 = (bf16[48,640]{1,0:T(8,128)(2,1)S(1)}, bf16[48,640]{1,0:T(8,128)(2,1)S(1)}, u32[]{:S(2)}, u32[]{:S(2)}) collective-permute-start(bf16[48,640]{1,0:T(8,128)(2,1)S(1)} %get-tuple-element.87), channel_id=1, source_target_pairs={{0,12},{4,0},{8,4},{12,8},{1,13},{5,1},{9,5},{13,9},{2,14},{6,2},{... | collective-permute-start | bytes 184328 | tf_op jit(solution)/shard_map/ppermute | solution.py:770
  11.3 0.0 copy-start.7
  11.3 0.0 copy-start.8
  11.3 0.0 copy-start
  11.3 0.0 slice-start.1
  11.3 3.5 %shard_map.193 = (bf16[48,1024]{1,0:T(8,128)(2,1)S(1)}, bf16[48,1024]{1,0:T(8,128)(2,1)S(1)}, bf16[48,1024]{1,0:T(8,128)(2,1)S(1)}, bf16[48,1024]{1,0:T(8,128)(2,1)S(1)}) custom-call(bf16[128,4096]{1,0:T(8,128)(2,1)S(1)} %get-tuple-element.76.hbuf, bf16[1024,1024]{1,0:T(8,128)(2,1)S(1)} %get-tuple-element.77.head, bf16[4096,1024]{1,0:T(8,128)(2,1)} %w.5, ...), custom_call_target="tpu_custom_call" | custom-call | flops 1073741824 | bytes 9437184 | tf_op jit(solution)/shard_map/pallas_call | solution.py:319
  14.9 0.0 copy-start.5
  14.9 0.0 copy-start.6
  14.9 0.7 %collective-permute-start = (bf16[48,1024]{1,0:T(8,128)(2,1)S(1)}, bf16[48,1024]{1,0:T(8,128)(2,1)S(1)}, u32[]{:S(2)}, u32[]{:S(2)}) collective-permute-start(bf16[48,1024]{1,0:T(8,128)(2,1)S(1)} %get-tuple-element.80), channel_id=1, source_target_pairs={{0,4},{4,8},{8,12},{12,0},{1,5},{5,9},{9,13},{13,1},{2,6},{6,10},{... | collective-permute-start | bytes 294920 | tf_op jit(solution)/shard_map/ppermute | solution.py:770
  15.6 0.3 collective-permute-start.1
  15.9 0.0 collective-permute-done.3.refs_1_
  15.9 2.8 %collective-permute-start.2 = (bf16[48,1024]{1,0:T(8,128)(2,1)S(1)}, bf16[48,1024]{1,0:T(8,128)(2,1)S(1)}, u32[]{:S(2)}, u32[]{:S(2)}) collective-permute-start(bf16[48,1024]{1,0:T(8,128)(2,1)S(1)} %get-tuple-element.82), channel_id=1, source_target_pairs={{0,12},{4,0},{8,4},{12,8},{1,13},{5,1},{9,5},{13,9},{2,14},{6,2},{... | collective-permute-start | bytes 294920 | tf_op jit(solution)/shard_map/ppermute | solution.py:770
  18.8 0.5 %shard_map.194 = (f32[144,640]{1,0:T(8,128)S(1)}, bf16[144,256]{1,0:T(8,128)(2,1)S(1)}, bf16[144,256]{1,0:T(8,128)(2,1)S(1)}, bf16[144,256]{1,0:T(8,128)(2,1)S(1)}) custom-call(bf16[144,192]{1,0:T(8,128)(2,1)S(1)} %get-tuple-element.74.owner_ref, bf16[48,640]{1,0:T(8,128)(2,1)S(1)} %get-tuple-element.88.refs_0_, ...), custom_call_target="tpu_custom_call" | custom-call | flops 2000000 | bytes 1000000 | tf_op jit(solution)/shard_map/pallas_call | solution.py:409
  19.3 0.0 collective-permute-start.6
  19.3 1.6 %collective-permute-start.7 = (bf16[144,256]{1,0:T(8,128)(2,1)S(1)}, bf16[144,256]{1,0:T(8,128)(2,1)S(1)}, u32[]{:S(2)}, u32[]{:S(2)}) collective-permute-start(bf16[144,256]{1,0:T(8,128)(2,1)S(1)} %get-tuple-element.99), channel_id=1, source_target_pairs={{2,1},{1,2},{0,3},{3,0},{6,5},{5,6},{4,7},{7,4},{10,9},{9,10},{8,1... | collective-permute-start | bytes 221192 | tf_op jit(solution)/shard_map/ppermute | solution.py:782
  20.9 2.2 %shard_map.195 = (f32[144,1024]{1,0:T(8,128)S(1)}, bf16[18,3,512]{2,1,0:T(4,128)(2,1)}, bf16[16,144,144]{2,1,0:T(8,128)(2,1)S(1)}, f32[144,1024]{1,0:T(8,128)S(1...) custom-call(f32[144,1]{1,0:T(8,128)S(1)} %get-tuple-element.83.accepts_ref, f32[144,640]{1,0:T(8,128)S(1)} %get-tuple-element.92.raw_ref, ...), custom_call_target="tpu_custom_call" | custom-call | flops 1000000 | bytes 1000000 | tf_op jit(solution)/shard_map/pallas_call | solution.py:469
  23.1 0.9 %collective-permute-done.6.refs_1_ = bf16[144,256]{1,0:T(8,128)(2,1)S(1)} collective-permute-done((bf16[144,256]{1,0:T(8,128)(2,1)S(1)}, bf16[144,256]{1,0:T(8,128)(2,1)S(1)}, u32[]{:S(2)}, u32[]{:S(2)}) %collective-permute-start.6) | collective-permute-done | bytes 73760 | tf_op jit(solution)/shard_map/ppermute | solution.py:782
  24.0 0.0 collective-permute-done.7.refs_2_
  24.0 1.6 %shard_map.196 = (f32[144,1024]{1,0:T(8,128)S(1)}, bf16[16,144,144]{2,1,0:T(8,128)(2,1)S(1)}, bf16[144,256]{1,0:T(8,128)(2,1)S(1)}) custom-call(bf16[16,144,144]{2,1,0:T(8,128)(2,1)S(1)} %get-tuple-element.94.fade_m_ref, f32[144,1024]{1,0:T(8,128)S(1)} %get-tuple-element.95.fade_ref, bf16[18,16,64,128]{3,2,1,0:T(8,128)(2,1)S(1)} %copy-done, ...), custom_call_target="tpu_custom_call" | custom-call | flops 37748736 | bytes 4718592 | tf_op jit(solution)/shard_map/pallas_call | solution.py:528
  25.6 0.0 collective-permute-done.2.refs_3_
  25.6 1.9 %shard_map.197 = (bf16[128,1024]{1,0:T(8,128)(2,1)S(1)}, f32[144,1024]{1,0:T(8,128)S(1)}, f32[144,1024]{1,0:T(8,128)S(1)}) custom-call(bf16[144,192]{1,0:T(8,128)(2,1)S(1)} %get-tuple-element.74.owner_ref, bf16[128,144]{1,0:T(8,128)(2,1)S(1)} %get-tuple-element.75.pack_ref, bf16[48,1024]{1,0:T(8,128)(2,1)S(1)} %get-tuple-element.79.refs_0_, ...), custom_call_target="tpu_custom_call" | custom-call | flops 42467328 | bytes 4000000 | tf_op jit(solution)/shard_map/pallas_call | solution.py:570
  27.5 0.5 shard_map.199
  28.0 1.0 %collective-permute-start.8 = (bf16[128,1024]{1,0:T(8,128)(2,1)S(1)}, bf16[128,1024]{1,0:T(8,128)(2,1)S(1)}, u32[]{:S(2)}, u32[]{:S(2)}) collective-permute-start(bf16[128,1024]{1,0:T(8,128)(2,1)S(1)} %shard_map.199), channel_id=1, source_target_pairs={{0,1},{1,0},{2,3},{3,2},{4,5},{5,4},{6,7},{7,6},{8,9},{9,8},{10,11... | collective-permute-start | bytes 786440 | tf_op jit(solution)/shard_map/ppermute | solution.py:794
  29.0 1.0 %shard_map.198 = (f32[128,1024]{1,0:T(8,128)S(1)}, bf16[128,1024]{1,0:T(8,128)(2,1)S(1)}, f32[128,1024]{1,0:T(8,128)S(1)}) custom-call(bf16[128,1024]{1,0:T(8,128)(2,1)S(1)} %get-tuple-element.105.rows, bf16[1024,4096]{1,0:T(8,128)(2,1)S(1)} %bitcast.9), custom_call_target="tpu_custom_call" | custom-call | flops 805306368 | bytes 6291456 | tf_op jit(solution)/shard_map/pallas_call | solution.py:660
  30.0 0.1 collective-permute-start.9
  30.1 0.1 collective-permute-done.8.refs_1_
  30.2 1.4 %collective-permute-start.10 = (bf16[128,512]{1,0:T(8,128)(2,1)S(1)}, bf16[128,512]{1,0:T(8,128)(2,1)S(1)}, u32[]{:S(2)}, u32[]{:S(2)}) collective-permute-start(bf16[128,512]{1,0:T(8,128)(2,1)S(1)} %get-tuple-element.110), channel_id=1, source_target_pairs={{0,2},{1,3},{2,0},{3,1},{4,6},{5,7},{6,4},{7,5},{8,10},{9,11},{10,... | collective-permute-start | bytes 393224 | tf_op jit(solution)/shard_map/ppermute | solution.py:802
  31.6 3.0 %shard_map.201 = (bf16[18,16,64,128]{3,2,1,0:T(8,128)(2,1)}, bf16[1024,144]{1,0:T(8,128)(2,1)S(1)}) custom-call(f32[18,16]{1,0:T(8,128)S(1)} %get-tuple-element.107.d_ref, f32[144,1024]{1,0:T(8,128)S(1)} %get-tuple-element.112.x_ref, f32[144,16]{1,0:T(8,128)S(1)} %get-tuple-element.113.w_ref, bf16[144,256]{1,0:T(8,128)(2,1)S(1)} %get-tuple-element.114.b_ref, ...), custom_call_target="tpu_custom_call" | custom-call | flops 37748736 | bytes 4718592 | tf_op jit(solution)/shard_map/pallas_call | solution.py:612
  34.6 0.8 %collective-permute-start.14 = (bf16[128,512]{1,0:T(8,128)(2,1)S(1)}, bf16[128,512]{1,0:T(8,128)(2,1)S(1)}, u32[]{:S(2)}, u32[]{:S(2)}) collective-permute-start(bf16[128,512]{1,0:T(8,128)(2,1)S(1)} %get-tuple-element.123), channel_id=1, source_target_pairs={{0,2},{1,3},{2,0},{3,1},{4,6},{5,7},{6,4},{7,5},{8,10},{9,11},{10,... | collective-permute-start | bytes 393224 | tf_op jit(solution)/shard_map/ppermute | solution.py:802
  35.3 0.7 %collective-permute-done.10.refs_0_ = bf16[128,512]{1,0:T(8,128)(2,1)S(1)} collective-permute-done((bf16[128,512]{1,0:T(8,128)(2,1)S(1)}, bf16[128,512]{1,0:T(8,128)(2,1)S(1)}, u32[]{:S(2)}, u32[]{:S(2)}) %collective-permute-start.10) | collective-permute-done | bytes 131104 | tf_op jit(solution)/shard_map/ppermute | solution.py:802
  36.1 0.2 shard_map.202
  36.3 1.3 %collective-permute-start.11 = (bf16[48,512]{1,0:T(8,128)(2,1)S(1)}, bf16[48,512]{1,0:T(8,128)(2,1)S(1)}, u32[]{:S(2)}, u32[]{:S(2)}) collective-permute-start(bf16[48,512]{1,0:T(8,128)(2,1)S(1)} %get-tuple-element.120), channel_id=1, source_target_pairs={{4,0},{8,4},{12,8},{0,12},{5,1},{9,5},{13,9},{1,13},{6,2},{10,6},{... | collective-permute-start | bytes 147464 | tf_op jit(solution)/shard_map/ppermute | solution.py:770
  37.6 0.6 %collective-permute-start.12 = (bf16[48,512]{1,0:T(8,128)(2,1)S(1)}, bf16[48,512]{1,0:T(8,128)(2,1)S(1)}, u32[]{:S(2)}, u32[]{:S(2)}) collective-permute-start(bf16[48,512]{1,0:T(8,128)(2,1)S(1)} %get-tuple-element.121), channel_id=1, source_target_pairs={{8,0},{12,4},{0,8},{4,12},{9,1},{13,5},{1,9},{5,13},{10,2},{14,6},... | collective-permute-start | bytes 147464 | tf_op jit(solution)/shard_map/ppermute | solution.py:770
  38.2 1.9 %collective-permute-start.13 = (bf16[48,512]{1,0:T(8,128)(2,1)S(1)}, bf16[48,512]{1,0:T(8,128)(2,1)S(1)}, u32[]{:S(2)}, u32[]{:S(2)}) collective-permute-start(bf16[48,512]{1,0:T(8,128)(2,1)S(1)} %get-tuple-element.122), channel_id=1, source_target_pairs={{12,0},{0,4},{4,8},{8,12},{13,1},{1,5},{5,9},{9,13},{14,2},{2,6},{... | collective-permute-start | bytes 147464 | tf_op jit(solution)/shard_map/ppermute | solution.py:770
  40.1 0.0 collective-permute-done.14.refs_0_
  40.1 0.2 shard_map.203
  40.4 2.0 %collective-permute-start.15 = (bf16[48,512]{1,0:T(8,128)(2,1)S(1)}, bf16[48,512]{1,0:T(8,128)(2,1)S(1)}, u32[]{:S(2)}, u32[]{:S(2)}) collective-permute-start(bf16[48,512]{1,0:T(8,128)(2,1)S(1)} %get-tuple-element.125), channel_id=1, source_target_pairs={{4,0},{8,4},{12,8},{0,12},{5,1},{9,5},{13,9},{1,13},{6,2},{10,6},{... | collective-permute-start | bytes 147464 | tf_op jit(solution)/shard_map/ppermute | solution.py:770
  42.3 0.5 %collective-permute-start.16 = (bf16[48,512]{1,0:T(8,128)(2,1)S(1)}, bf16[48,512]{1,0:T(8,128)(2,1)S(1)}, u32[]{:S(2)}, u32[]{:S(2)}) collective-permute-start(bf16[48,512]{1,0:T(8,128)(2,1)S(1)} %get-tuple-element.126), channel_id=1, source_target_pairs={{8,0},{12,4},{0,8},{4,12},{9,1},{13,5},{1,9},{5,13},{10,2},{14,6},... | collective-permute-start | bytes 147464 | tf_op jit(solution)/shard_map/ppermute | solution.py:770
  42.8 0.0 collective-permute-done.11.parts_0__1_
  42.9 1.4 %collective-permute-start.17 = (bf16[48,512]{1,0:T(8,128)(2,1)S(1)}, bf16[48,512]{1,0:T(8,128)(2,1)S(1)}, u32[]{:S(2)}, u32[]{:S(2)}) collective-permute-start(bf16[48,512]{1,0:T(8,128)(2,1)S(1)} %get-tuple-element.127), channel_id=1, source_target_pairs={{12,0},{0,4},{4,8},{8,12},{13,1},{1,5},{5,9},{9,13},{14,2},{2,6},{... | collective-permute-start | bytes 147464 | tf_op jit(solution)/shard_map/ppermute | solution.py:770
  44.2 3.3 %shard_map.204 = (bf16[18,16,64,128]{3,2,1,0:T(8,128)(2,1)}, bf16[18,3,1024]{2,1,0:T(4,128)(2,1)}) custom-call(f32[18,16]{1,0:T(8,128)S(1)} %get-tuple-element.107.d_ref, bf16[1024,144]{1,0:T(8,128)(2,1)S(1)} %get-tuple-element.129.turned_ref, bf16[144,256]{1,0:T(8,128)(2,1)S(1)} %get-tuple-element.114.b_ref, ...), custom_call_target="tpu_custom_call", output_to_operand_aliasing={{0}: (7, {})} | custom-call | flops 37748736 | bytes 4718592 | tf_op jit(solution)/shard_map/pallas_call | solution.py:633
  47.5 0.2 collective-permute-done.16.parts_1__2_
  47.7 1.0 %collective-permute-done.17.parts_1__3_ = bf16[48,512]{1,0:T(8,128)(2,1)S(1)} collective-permute-done((bf16[48,512]{1,0:T(8,128)(2,1)S(1)}, bf16[48,512]{1,0:T(8,128)(2,1)S(1)}, u32[]{:S(2)}, u32[]{:S(2)}) %collective-permute-start.17) | collective-permute-done | bytes 49184 | tf_op jit(solution)/shard_map/ppermute | solution.py:770
  48.7 0.9 %shard_map.205 = bf16[128,1024]{1,0:T(8,128)(2,1)} custom-call(bf16[128,192]{1,0:T(8,128)(2,1)S(1)} %get-tuple-element.73.collect_ref, bf16[48,512]{1,0:T(8,128)(2,1)S(1)} %get-tuple-element.132.parts_0__0_, bf16[48,512]{1,0:T(8,128)(2,1)S(1)} %collective-permute-done.11.parts_0__1_, bf16[48,512]{1,0:T(8,128)(2,1)S(1)} %collective-permute-done.12.parts_0__2_, ...), custom_call_target="tpu_custom_call" | custom-call | flops 1000000 | bytes 1000000 | tf_op jit(solution)/shard_map/pallas_call | solution.py:723
  (25 shorter events, 0.1 us)
Async XLA Ops:
  0.6 26.9 %slice-start = ((s8[8388608]{0:T(1024)(128)(4,1)}), s8[4194304]{0:T(1024)(128)(4,1)S(1)}, s32[]{:S(2)}) async-start(s8[8388608]{0:T(1024)(128)(4,1)} %bitcast.8), calls=%async_computation | async-start | bytes 8388608
  4.3 11.7 %collective-permute-start.3 = (bf16[48,640]{1,0:T(8,128)(2,1)S(1)}, bf16[48,640]{1,0:T(8,128)(2,1)S(1)}, u32[]{:S(2)}, u32[]{:S(2)}) collective-permute-start(bf16[48,640]{1,0:T(8,128)(2,1)S(1)} %get-tuple-element.85), channel_id=1, source_target_pairs={{0,4},{4,8},{8,12},{12,0},{1,5},{5,9},{9,13},{13,1},{2,6},{6,10},{... | collective-permute-start | bytes 184328 | tf_op jit(solution)/shard_map/ppermute | solution.py:770
  7.3 11.4 %collective-permute-start.4 = (bf16[48,640]{1,0:T(8,128)(2,1)S(1)}, bf16[48,640]{1,0:T(8,128)(2,1)S(1)}, u32[]{:S(2)}, u32[]{:S(2)}) collective-permute-start(bf16[48,640]{1,0:T(8,128)(2,1)S(1)} %get-tuple-element.86), channel_id=1, source_target_pairs={{0,8},{4,12},{8,0},{12,4},{1,9},{5,13},{9,1},{13,5},{2,10},{6,14},... | collective-permute-start | bytes 184328 | tf_op jit(solution)/shard_map/ppermute | solution.py:770
  9.9 8.8 %collective-permute-start.5 = (bf16[48,640]{1,0:T(8,128)(2,1)S(1)}, bf16[48,640]{1,0:T(8,128)(2,1)S(1)}, u32[]{:S(2)}, u32[]{:S(2)}) collective-permute-start(bf16[48,640]{1,0:T(8,128)(2,1)S(1)} %get-tuple-element.87), channel_id=1, source_target_pairs={{0,12},{4,0},{8,4},{12,8},{1,13},{5,1},{9,5},{13,9},{2,14},{6,2},{... | collective-permute-start | bytes 184328 | tf_op jit(solution)/shard_map/ppermute | solution.py:770
  11.3 7.5 %copy-start.2 = (bf16[18,3,512]{2,1,0:T(4,128)(2,1)S(1)}, bf16[18,3,512]{2,1,0:T(4,128)(2,1)}, u32[]{:S(2)}) copy-start(bf16[18,3,512]{2,1,0:T(4,128)(2,1)} %conv_ref.2) | copy-start | bytes 165892
  11.3 7.5 %copy-start.4 = (f32[4,512]{1,0:T(4,128)S(1)}, f32[4,512]{1,0:T(4,128)}, u32[]{:S(2)}) copy-start(f32[4,512]{1,0:T(4,128)} %refs_5_.2) | copy-start | bytes 24580
  11.3 9.6 %copy-start.1 = (bf16[18,3,1024]{2,1,0:T(4,128)(2,1)S(1)}, bf16[18,3,1024]{2,1,0:T(4,128)(2,1)}, u32[]{:S(2)}) copy-start(bf16[18,3,1024]{2,1,0:T(4,128)(2,1)} %conv_ref.3) | copy-start | bytes 331780
  11.3 9.6 %copy-start.3 = (f32[4,1024]{1,0:T(4,128)S(1)}, f32[4,1024]{1,0:T(4,128)}, u32[]{:S(2)}) copy-start(f32[4,1024]{1,0:T(4,128)} %refs_5_.3) | copy-start | bytes 49156
  11.3 9.6 %copy-start.7 = (f32[16]{0:T(128)S(1)}, f32[16]{0:T(128)}, u32[]{:S(2)}) copy-start(f32[16]{0:T(128)} %param.23) | copy-start | bytes 196
  11.3 9.6 %copy-start.8 = (f32[16]{0:T(128)S(1)}, f32[16]{0:T(128)}, u32[]{:S(2)}) copy-start(f32[16]{0:T(128)} %param.24) | copy-start | bytes 196
  11.3 12.7 %copy-start = (bf16[18,16,64,128]{3,2,1,0:T(8,128)(2,1)S(1)}, bf16[18,16,64,128]{3,2,1,0:T(8,128)(2,1)}, u32[]{:S(2)}) copy-start(bf16[18,16,64,128]{3,2,1,0:T(8,128)(2,1)} %pool.1) | copy-start | bytes 14155780
  11.3 16.2 %slice-start.1 = ((s8[8388608]{0:T(1024)(128)(4,1)}), s8[4194304]{0:T(1024)(128)(4,1)S(1)}, s32[]{:S(2)}) async-start(s8[8388608]{0:T(1024)(128)(4,1)} %bitcast.8), calls=%async_computation.1 | async-start | bytes 8388608
  14.9 10.7 %copy-start.5 = (f32[1024]{0:T(1024)S(1)}, f32[1024]{0:T(1024)}, u32[]{:S(2)}) copy-start(f32[1024]{0:T(1024)} %param.26) | copy-start | bytes 12292
  14.9 10.7 %copy-start.6 = (f32[16]{0:T(128)S(1)}, f32[16]{0:T(128)}, u32[]{:S(2)}) copy-start(f32[16]{0:T(128)} %param.25) | copy-start | bytes 196
  14.9 10.7 %collective-permute-start = (bf16[48,1024]{1,0:T(8,128)(2,1)S(1)}, bf16[48,1024]{1,0:T(8,128)(2,1)S(1)}, u32[]{:S(2)}, u32[]{:S(2)}) collective-permute-start(bf16[48,1024]{1,0:T(8,128)(2,1)S(1)} %get-tuple-element.80), channel_id=1, source_target_pairs={{0,4},{4,8},{8,12},{12,0},{1,5},{5,9},{9,13},{13,1},{2,6},{6,10},{... | collective-permute-start | bytes 294920 | tf_op jit(solution)/shard_map/ppermute | solution.py:770
  15.6 9.9 %collective-permute-start.1 = (bf16[48,1024]{1,0:T(8,128)(2,1)S(1)}, bf16[48,1024]{1,0:T(8,128)(2,1)S(1)}, u32[]{:S(2)}, u32[]{:S(2)}) collective-permute-start(bf16[48,1024]{1,0:T(8,128)(2,1)S(1)} %get-tuple-element.81), channel_id=1, source_target_pairs={{0,8},{4,12},{8,0},{12,4},{1,9},{5,13},{9,1},{13,5},{2,10},{6,14},... | collective-permute-start | bytes 294920 | tf_op jit(solution)/shard_map/ppermute | solution.py:770
  15.9 9.6 %collective-permute-start.2 = (bf16[48,1024]{1,0:T(8,128)(2,1)S(1)}, bf16[48,1024]{1,0:T(8,128)(2,1)S(1)}, u32[]{:S(2)}, u32[]{:S(2)}) collective-permute-start(bf16[48,1024]{1,0:T(8,128)(2,1)S(1)} %get-tuple-element.82), channel_id=1, source_target_pairs={{0,12},{4,0},{8,4},{12,8},{1,13},{5,1},{9,5},{13,9},{2,14},{6,2},{... | collective-permute-start | bytes 294920 | tf_op jit(solution)/shard_map/ppermute | solution.py:770
  19.3 4.7 %collective-permute-start.6 = (bf16[144,256]{1,0:T(8,128)(2,1)S(1)}, bf16[144,256]{1,0:T(8,128)(2,1)S(1)}, u32[]{:S(2)}, u32[]{:S(2)}) collective-permute-start(bf16[144,256]{1,0:T(8,128)(2,1)S(1)} %get-tuple-element.98), channel_id=1, source_target_pairs={{2,0},{0,1},{3,2},{1,3},{6,4},{4,5},{7,6},{5,7},{10,8},{8,9},{11,1... | collective-permute-start | bytes 221192 | tf_op jit(solution)/shard_map/ppermute | solution.py:782
  19.3 4.6 %collective-permute-start.7 = (bf16[144,256]{1,0:T(8,128)(2,1)S(1)}, bf16[144,256]{1,0:T(8,128)(2,1)S(1)}, u32[]{:S(2)}, u32[]{:S(2)}) collective-permute-start(bf16[144,256]{1,0:T(8,128)(2,1)S(1)} %get-tuple-element.99), channel_id=1, source_target_pairs={{2,1},{1,2},{0,3},{3,0},{6,5},{5,6},{4,7},{7,4},{10,9},{9,10},{8,1... | collective-permute-start | bytes 221192 | tf_op jit(solution)/shard_map/ppermute | solution.py:782
  28.0 2.1 %collective-permute-start.8 = (bf16[128,1024]{1,0:T(8,128)(2,1)S(1)}, bf16[128,1024]{1,0:T(8,128)(2,1)S(1)}, u32[]{:S(2)}, u32[]{:S(2)}) collective-permute-start(bf16[128,1024]{1,0:T(8,128)(2,1)S(1)} %shard_map.199), channel_id=1, source_target_pairs={{0,1},{1,0},{2,3},{3,2},{4,5},{5,4},{6,7},{7,6},{8,9},{9,8},{10,11... | collective-permute-start | bytes 786440 | tf_op jit(solution)/shard_map/ppermute | solution.py:794
  30.0 5.4 %collective-permute-start.9 = (bf16[128,1024]{1,0:T(8,128)(2,1)S(1)}, bf16[128,1024]{1,0:T(8,128)(2,1)S(1)}, u32[]{:S(2)}, u32[]{:S(2)}) collective-permute-start(bf16[128,1024]{1,0:T(8,128)(2,1)S(1)} %get-tuple-element.117), channel_id=1, source_target_pairs={{0,1},{1,0},{2,3},{3,2},{4,5},{5,4},{6,7},{7,6},{8,9},{9,8},{10,11... | collective-permute-start | bytes 786440 | tf_op jit(solution)/shard_map/ppermute | solution.py:807
  30.2 5.9 %collective-permute-start.10 = (bf16[128,512]{1,0:T(8,128)(2,1)S(1)}, bf16[128,512]{1,0:T(8,128)(2,1)S(1)}, u32[]{:S(2)}, u32[]{:S(2)}) collective-permute-start(bf16[128,512]{1,0:T(8,128)(2,1)S(1)} %get-tuple-element.110), channel_id=1, source_target_pairs={{0,2},{1,3},{2,0},{3,1},{4,6},{5,7},{6,4},{7,5},{8,10},{9,11},{10,... | collective-permute-start | bytes 393224 | tf_op jit(solution)/shard_map/ppermute | solution.py:802
  34.6 5.5 %collective-permute-start.14 = (bf16[128,512]{1,0:T(8,128)(2,1)S(1)}, bf16[128,512]{1,0:T(8,128)(2,1)S(1)}, u32[]{:S(2)}, u32[]{:S(2)}) collective-permute-start(bf16[128,512]{1,0:T(8,128)(2,1)S(1)} %get-tuple-element.123), channel_id=1, source_target_pairs={{0,2},{1,3},{2,0},{3,1},{4,6},{5,7},{6,4},{7,5},{8,10},{9,11},{10,... | collective-permute-start | bytes 393224 | tf_op jit(solution)/shard_map/ppermute | solution.py:802
  36.3 6.5 %collective-permute-start.11 = (bf16[48,512]{1,0:T(8,128)(2,1)S(1)}, bf16[48,512]{1,0:T(8,128)(2,1)S(1)}, u32[]{:S(2)}, u32[]{:S(2)}) collective-permute-start(bf16[48,512]{1,0:T(8,128)(2,1)S(1)} %get-tuple-element.120), channel_id=1, source_target_pairs={{4,0},{8,4},{12,8},{0,12},{5,1},{9,5},{13,9},{1,13},{6,2},{10,6},{... | collective-permute-start | bytes 147464 | tf_op jit(solution)/shard_map/ppermute | solution.py:770
  37.6 9.9 %collective-permute-start.12 = (bf16[48,512]{1,0:T(8,128)(2,1)S(1)}, bf16[48,512]{1,0:T(8,128)(2,1)S(1)}, u32[]{:S(2)}, u32[]{:S(2)}) collective-permute-start(bf16[48,512]{1,0:T(8,128)(2,1)S(1)} %get-tuple-element.121), channel_id=1, source_target_pairs={{8,0},{12,4},{0,8},{4,12},{9,1},{13,5},{1,9},{5,13},{10,2},{14,6},... | collective-permute-start | bytes 147464 | tf_op jit(solution)/shard_map/ppermute | solution.py:770
  38.2 9.3 %collective-permute-start.13 = (bf16[48,512]{1,0:T(8,128)(2,1)S(1)}, bf16[48,512]{1,0:T(8,128)(2,1)S(1)}, u32[]{:S(2)}, u32[]{:S(2)}) collective-permute-start(bf16[48,512]{1,0:T(8,128)(2,1)S(1)} %get-tuple-element.122), channel_id=1, source_target_pairs={{12,0},{0,4},{4,8},{8,12},{13,1},{1,5},{5,9},{9,13},{14,2},{2,6},{... | collective-permute-start | bytes 147464 | tf_op jit(solution)/shard_map/ppermute | solution.py:770
  40.4 7.1 %collective-permute-start.15 = (bf16[48,512]{1,0:T(8,128)(2,1)S(1)}, bf16[48,512]{1,0:T(8,128)(2,1)S(1)}, u32[]{:S(2)}, u32[]{:S(2)}) collective-permute-start(bf16[48,512]{1,0:T(8,128)(2,1)S(1)} %get-tuple-element.125), channel_id=1, source_target_pairs={{4,0},{8,4},{12,8},{0,12},{5,1},{9,5},{13,9},{1,13},{6,2},{10,6},{... | collective-permute-start | bytes 147464 | tf_op jit(solution)/shard_map/ppermute | solution.py:770
  42.3 5.4 %collective-permute-start.16 = (bf16[48,512]{1,0:T(8,128)(2,1)S(1)}, bf16[48,512]{1,0:T(8,128)(2,1)S(1)}, u32[]{:S(2)}, u32[]{:S(2)}) collective-permute-start(bf16[48,512]{1,0:T(8,128)(2,1)S(1)} %get-tuple-element.126), channel_id=1, source_target_pairs={{8,0},{12,4},{0,8},{4,12},{9,1},{13,5},{1,9},{5,13},{10,2},{14,6},... | collective-permute-start | bytes 147464 | tf_op jit(solution)/shard_map/ppermute | solution.py:770
  42.9 5.9 %collective-permute-start.17 = (bf16[48,512]{1,0:T(8,128)(2,1)S(1)}, bf16[48,512]{1,0:T(8,128)(2,1)S(1)}, u32[]{:S(2)}, u32[]{:S(2)}) collective-permute-start(bf16[48,512]{1,0:T(8,128)(2,1)S(1)} %get-tuple-element.127), channel_id=1, source_target_pairs={{12,0},{0,4},{4,8},{8,12},{13,1},{1,5},{5,9},{9,13},{14,2},{2,6},{... | collective-permute-start | bytes 147464 | tf_op jit(solution)/shard_map/ppermute | solution.py:770

commit v6 on v5

--- a/solution.py
+++ b/solution.py
@@ -709,22 +709,29 @@
     )(keep, core, back, *arrived)
 
 
-def collect_kernel(collect_ref, parts, out):
-    at = 0
-    for got in parts:
+def collect_kernel(collect_ref, parts, out, buf, sems):
+    at, copies = 0, []
+    for k, got in enumerate(parts):
         width = got[0].shape[1]
         rows = jnp.concatenate([g[...] for g in got], axis=0)
-        out[:, at : at + width] = dot(collect_ref[...], rows).astype(BF16)
+        buf[:, at : at + width] = dot(collect_ref[...], rows).astype(BF16)
+        here = pl.ds(at, width)
+        copies.append(pltpu.make_async_copy(buf.at[:, here], out.at[:, here], sems.at[k]))
+        copies[-1].start()
         at += width
+    for copy in copies:
+        copy.wait()
 
 
 def collect_stage(collect, parts):
     width = sum(got[0].shape[1] for got in parts)
+    shape = (collect.shape[0], width)
     return pl.pallas_call(
         collect_kernel,
-        out_shape=jax.ShapeDtypeStruct((collect.shape[0], width), BF16),
+        out_shape=jax.ShapeDtypeStruct(shape, BF16),
         in_specs=[VMEM, [[VMEM] * len(got) for got in parts]],
-        out_specs=VMEM,
+        out_specs=HBM,
+        scratch_shapes=[pltpu.VMEM(shape, BF16), pltpu.SemaphoreType.DMA((len(parts),))],
         compiler_params=params(8),
         cost_estimate=cost(1e6, 1e6),
     )(collect, parts)

time: 49.8 us -> 49.8 us (level)
  no operation moved by 1% of the time
where the time goes in v6:
time: 49.8 us; the launch traced here: 49.6 us
  starting transfers between devices  23.4 us (47%)
  Pallas kernels  22.4 us (45%)
  waiting for transfers between devices  2.95 us (6%)
  between operations  0.88 us (2%)
    ppermute x12, starting transfers between devices, over_pool(): moved[step] = lax.ppermute(parts[step], 'pool', pairs)  18.6 us
    pallas_call x1, Pallas kernels, project_bc(): pl.pallas_call(functools.partial(project_bc_kernel, n_pool, req, cr, chun...  3.61 us
    pallas_call x1, Pallas kernels, project_x(): pl.pallas_call(functools.partial(project_x_kernel, n_pool, cr, chunk), ou...  3.5 us
    pallas_call x1, Pallas kernels, last_state_stage(): pl.pallas_call(functools.partial(last_state_kernel, span_of), out_shape=[...  3.25 us
    pallas_call x1, Pallas kernels, first_state_stage(): pl.pallas_call(functools.partial(first_state_kernel, span_of), out_shape=...  3 us
    pallas_call x1, Pallas kernels, pre_stage(): pl.pallas_call(functools.partial(pre_kernel, slots), out_shape=[jax.Shape...  2.18 us
    ppermute x2, starting transfers between devices, over_line(): lax.ppermute(v, 'tensor', [(r, (r // 2 + i) % n_line * 2 + r % 2) for r i...  2.15 us
    pallas_call x1, Pallas kernels, x_stage(): pl.pallas_call(functools.partial(x_kernel, n_pool), out_shape=[jax.ShapeD...  1.87 us
  transfers between devices with their start and end apart: 18, of which 5 were waited for; matrix products, arithmetic and copies ran while one was open for 0% of the time, Pallas kernels for 31%

profile of v6, /device:TPU:0, one launch (start us, length us, event | category | flops | bytes accessed | tf_op | source)
XLA Modules:
  0.0 49.6 jit_solution(14841925692421758810)
XLA Ops:
  0.6 0.0 slice-start
  0.6 3.6 %shard_map.192 = (bf16[48,640]{1,0:T(8,128)(2,1)S(1)}, bf16[48,640]{1,0:T(8,128)(2,1)S(1)}, bf16[48,640]{1,0:T(8,128)(2,1)S(1)}, bf16[48,640]{1,0:T(8,128)(2,1)S...) custom-call(s32[1,64]{1,0:T(1,128)} %bitcast.15, ...), custom_call_target="tpu_custom_call" | custom-call | flops 536870912 | bytes 6291456 | tf_op jit(solution)/shard_map/pallas_call | solution.py:270
  4.3 3.1 %collective-permute-start.3 = (bf16[48,640]{1,0:T(8,128)(2,1)S(1)}, bf16[48,640]{1,0:T(8,128)(2,1)S(1)}, u32[]{:S(2)}, u32[]{:S(2)}) collective-permute-start(bf16[48,640]{1,0:T(8,128)(2,1)S(1)} %get-tuple-element.85), channel_id=1, source_target_pairs={{0,4},{4,8},{8,12},{12,0},{1,5},{5,9},{9,13},{13,1},{2,6},{6,10},{... | collective-permute-start | bytes 184328 | tf_op jit(solution)/shard_map/ppermute | solution.py:777
  7.3 2.6 %collective-permute-start.4 = (bf16[48,640]{1,0:T(8,128)(2,1)S(1)}, bf16[48,640]{1,0:T(8,128)(2,1)S(1)}, u32[]{:S(2)}, u32[]{:S(2)}) collective-permute-start(bf16[48,640]{1,0:T(8,128)(2,1)S(1)} %get-tuple-element.86), channel_id=1, source_target_pairs={{0,8},{4,12},{8,0},{12,4},{1,9},{5,13},{9,1},{13,5},{2,10},{6,14},... | collective-permute-start | bytes 184328 | tf_op jit(solution)/shard_map/ppermute | solution.py:777
  9.9 1.3 %collective-permute-start.5 = (bf16[48,640]{1,0:T(8,128)(2,1)S(1)}, bf16[48,640]{1,0:T(8,128)(2,1)S(1)}, u32[]{:S(2)}, u32[]{:S(2)}) collective-permute-start(bf16[48,640]{1,0:T(8,128)(2,1)S(1)} %get-tuple-element.87), channel_id=1, source_target_pairs={{0,12},{4,0},{8,4},{12,8},{1,13},{5,1},{9,5},{13,9},{2,14},{6,2},{... | collective-permute-start | bytes 184328 | tf_op jit(solution)/shard_map/ppermute | solution.py:777
  11.3 0.0 copy-start.7
  11.3 0.0 copy-start.8
  11.3 0.0 copy-start
  11.3 0.0 slice-start.1
  11.3 3.5 %shard_map.193 = (bf16[48,1024]{1,0:T(8,128)(2,1)S(1)}, bf16[48,1024]{1,0:T(8,128)(2,1)S(1)}, bf16[48,1024]{1,0:T(8,128)(2,1)S(1)}, bf16[48,1024]{1,0:T(8,128)(2,1)S(1)}) custom-call(bf16[128,4096]{1,0:T(8,128)(2,1)S(1)} %get-tuple-element.76.hbuf, bf16[1024,1024]{1,0:T(8,128)(2,1)S(1)} %get-tuple-element.77.head, bf16[4096,1024]{1,0:T(8,128)(2,1)} %w.5, ...), custom_call_target="tpu_custom_call" | custom-call | flops 1073741824 | bytes 9437184 | tf_op jit(solution)/shard_map/pallas_call | solution.py:319
  14.9 0.0 copy-start.5
  14.9 0.0 copy-start.6
  14.9 0.7 %collective-permute-start = (bf16[48,1024]{1,0:T(8,128)(2,1)S(1)}, bf16[48,1024]{1,0:T(8,128)(2,1)S(1)}, u32[]{:S(2)}, u32[]{:S(2)}) collective-permute-start(bf16[48,1024]{1,0:T(8,128)(2,1)S(1)} %get-tuple-element.80), channel_id=1, source_target_pairs={{0,4},{4,8},{8,12},{12,0},{1,5},{5,9},{9,13},{13,1},{2,6},{6,10},{... | collective-permute-start | bytes 294920 | tf_op jit(solution)/shard_map/ppermute | solution.py:777
  15.6 0.3 collective-permute-start.1
  15.9 2.8 %collective-permute-start.2 = (bf16[48,1024]{1,0:T(8,128)(2,1)S(1)}, bf16[48,1024]{1,0:T(8,128)(2,1)S(1)}, u32[]{:S(2)}, u32[]{:S(2)}) collective-permute-start(bf16[48,1024]{1,0:T(8,128)(2,1)S(1)} %get-tuple-element.82), channel_id=1, source_target_pairs={{0,12},{4,0},{8,4},{12,8},{1,13},{5,1},{9,5},{13,9},{2,14},{6,2},{... | collective-permute-start | bytes 294920 | tf_op jit(solution)/shard_map/ppermute | solution.py:777
  18.8 0.0 collective-permute-done.4.refs_2_
  18.8 0.0 collective-permute-done.5.refs_3_
  18.8 0.5 %shard_map.194 = (f32[144,640]{1,0:T(8,128)S(1)}, bf16[144,256]{1,0:T(8,128)(2,1)S(1)}, bf16[144,256]{1,0:T(8,128)(2,1)S(1)}, bf16[144,256]{1,0:T(8,128)(2,1)S(1)}) custom-call(bf16[144,192]{1,0:T(8,128)(2,1)S(1)} %get-tuple-element.74.owner_ref, bf16[48,640]{1,0:T(8,128)(2,1)S(1)} %get-tuple-element.88.refs_0_, ...), custom_call_target="tpu_custom_call" | custom-call | flops 2000000 | bytes 1000000 | tf_op jit(solution)/shard_map/pallas_call | solution.py:409
  19.3 0.0 collective-permute-start.6
  19.3 1.6 %collective-permute-start.7 = (bf16[144,256]{1,0:T(8,128)(2,1)S(1)}, bf16[144,256]{1,0:T(8,128)(2,1)S(1)}, u32[]{:S(2)}, u32[]{:S(2)}) collective-permute-start(bf16[144,256]{1,0:T(8,128)(2,1)S(1)} %get-tuple-element.99), channel_id=1, source_target_pairs={{2,1},{1,2},{0,3},{3,0},{6,5},{5,6},{4,7},{7,4},{10,9},{9,10},{8,1... | collective-permute-start | bytes 221192 | tf_op jit(solution)/shard_map/ppermute | solution.py:789
  20.9 2.2 %shard_map.195 = (f32[144,1024]{1,0:T(8,128)S(1)}, bf16[18,3,512]{2,1,0:T(4,128)(2,1)}, bf16[16,144,144]{2,1,0:T(8,128)(2,1)S(1)}, f32[144,1024]{1,0:T(8,128)S(1...) custom-call(f32[144,1]{1,0:T(8,128)S(1)} %get-tuple-element.83.accepts_ref, f32[144,640]{1,0:T(8,128)S(1)} %get-tuple-element.92.raw_ref, ...), custom_call_target="tpu_custom_call" | custom-call | flops 1000000 | bytes 1000000 | tf_op jit(solution)/shard_map/pallas_call | solution.py:469
  23.1 0.9 %collective-permute-done.6.refs_1_ = bf16[144,256]{1,0:T(8,128)(2,1)S(1)} collective-permute-done((bf16[144,256]{1,0:T(8,128)(2,1)S(1)}, bf16[144,256]{1,0:T(8,128)(2,1)S(1)}, u32[]{:S(2)}, u32[]{:S(2)}) %collective-permute-start.6) | collective-permute-done | bytes 73760 | tf_op jit(solution)/shard_map/ppermute | solution.py:789
  24.0 0.0 collective-permute-done.7.refs_2_
  24.0 1.6 %shard_map.196 = (f32[144,1024]{1,0:T(8,128)S(1)}, bf16[16,144,144]{2,1,0:T(8,128)(2,1)S(1)}, bf16[144,256]{1,0:T(8,128)(2,1)S(1)}) custom-call(bf16[16,144,144]{2,1,0:T(8,128)(2,1)S(1)} %get-tuple-element.94.fade_m_ref, f32[144,1024]{1,0:T(8,128)S(1)} %get-tuple-element.95.fade_ref, bf16[18,16,64,128]{3,2,1,0:T(8,128)(2,1)S(1)} %copy-done, ...), custom_call_target="tpu_custom_call" | custom-call | flops 37748736 | bytes 4718592 | tf_op jit(solution)/shard_map/pallas_call | solution.py:528
  25.6 0.0 collective-permute-done.refs_1_
  25.6 0.0 collective-permute-done.2.refs_3_
  25.6 1.9 %shard_map.197 = (bf16[128,1024]{1,0:T(8,128)(2,1)S(1)}, f32[144,1024]{1,0:T(8,128)S(1)}, f32[144,1024]{1,0:T(8,128)S(1)}) custom-call(bf16[144,192]{1,0:T(8,128)(2,1)S(1)} %get-tuple-element.74.owner_ref, bf16[128,144]{1,0:T(8,128)(2,1)S(1)} %get-tuple-element.75.pack_ref, bf16[48,1024]{1,0:T(8,128)(2,1)S(1)} %get-tuple-element.79.refs_0_, ...), custom_call_target="tpu_custom_call" | custom-call | flops 42467328 | bytes 4000000 | tf_op jit(solution)/shard_map/pallas_call | solution.py:570
  27.5 0.5 shard_map.199
  28.0 1.0 %collective-permute-start.8 = (bf16[128,1024]{1,0:T(8,128)(2,1)S(1)}, bf16[128,1024]{1,0:T(8,128)(2,1)S(1)}, u32[]{:S(2)}, u32[]{:S(2)}) collective-permute-start(bf16[128,1024]{1,0:T(8,128)(2,1)S(1)} %shard_map.199), channel_id=1, source_target_pairs={{0,1},{1,0},{2,3},{3,2},{4,5},{5,4},{6,7},{7,6},{8,9},{9,8},{10,11... | collective-permute-start | bytes 786440 | tf_op jit(solution)/shard_map/ppermute | solution.py:801
  29.0 1.0 %shard_map.198 = (f32[128,1024]{1,0:T(8,128)S(1)}, bf16[128,1024]{1,0:T(8,128)(2,1)S(1)}, f32[128,1024]{1,0:T(8,128)S(1)}) custom-call(bf16[128,1024]{1,0:T(8,128)(2,1)S(1)} %get-tuple-element.105.rows, bf16[1024,4096]{1,0:T(8,128)(2,1)S(1)} %bitcast.9), custom_call_target="tpu_custom_call" | custom-call | flops 805306368 | bytes 6291456 | tf_op jit(solution)/shard_map/pallas_call | solution.py:660
  30.0 0.1 collective-permute-start.9
  30.1 0.1 collective-permute-done.8.refs_1_
  30.2 1.4 %collective-permute-start.10 = (bf16[128,512]{1,0:T(8,128)(2,1)S(1)}, bf16[128,512]{1,0:T(8,128)(2,1)S(1)}, u32[]{:S(2)}, u32[]{:S(2)}) collective-permute-start(bf16[128,512]{1,0:T(8,128)(2,1)S(1)} %get-tuple-element.110), channel_id=1, source_target_pairs={{0,2},{1,3},{2,0},{3,1},{4,6},{5,7},{6,4},{7,5},{8,10},{9,11},{10,... | collective-permute-start | bytes 393224 | tf_op jit(solution)/shard_map/ppermute | solution.py:809
  31.6 3.0 %shard_map.201 = (bf16[18,16,64,128]{3,2,1,0:T(8,128)(2,1)}, bf16[1024,144]{1,0:T(8,128)(2,1)S(1)}) custom-call(f32[18,16]{1,0:T(8,128)S(1)} %get-tuple-element.107.d_ref, f32[144,1024]{1,0:T(8,128)S(1)} %get-tuple-element.112.x_ref, f32[144,16]{1,0:T(8,128)S(1)} %get-tuple-element.113.w_ref, bf16[144,256]{1,0:T(8,128)(2,1)S(1)} %get-tuple-element.114.b_ref, ...), custom_call_target="tpu_custom_call" | custom-call | flops 37748736 | bytes 4718592 | tf_op jit(solution)/shard_map/pallas_call | solution.py:612
  34.6 0.8 %collective-permute-start.14 = (bf16[128,512]{1,0:T(8,128)(2,1)S(1)}, bf16[128,512]{1,0:T(8,128)(2,1)S(1)}, u32[]{:S(2)}, u32[]{:S(2)}) collective-permute-start(bf16[128,512]{1,0:T(8,128)(2,1)S(1)} %get-tuple-element.123), channel_id=1, source_target_pairs={{0,2},{1,3},{2,0},{3,1},{4,6},{5,7},{6,4},{7,5},{8,10},{9,11},{10,... | collective-permute-start | bytes 393224 | tf_op jit(solution)/shard_map/ppermute | solution.py:809
  35.3 0.7 %collective-permute-done.10.refs_0_ = bf16[128,512]{1,0:T(8,128)(2,1)S(1)} collective-permute-done((bf16[128,512]{1,0:T(8,128)(2,1)S(1)}, bf16[128,512]{1,0:T(8,128)(2,1)S(1)}, u32[]{:S(2)}, u32[]{:S(2)}) %collective-permute-start.10) | collective-permute-done | bytes 131104 | tf_op jit(solution)/shard_map/ppermute | solution.py:809
  36.1 0.2 shard_map.202
  36.3 1.3 %collective-permute-start.11 = (bf16[48,512]{1,0:T(8,128)(2,1)S(1)}, bf16[48,512]{1,0:T(8,128)(2,1)S(1)}, u32[]{:S(2)}, u32[]{:S(2)}) collective-permute-start(bf16[48,512]{1,0:T(8,128)(2,1)S(1)} %get-tuple-element.120), channel_id=1, source_target_pairs={{4,0},{8,4},{12,8},{0,12},{5,1},{9,5},{13,9},{1,13},{6,2},{10,6},{... | collective-permute-start | bytes 147464 | tf_op jit(solution)/shard_map/ppermute | solution.py:777
  37.6 0.6 %collective-permute-start.12 = (bf16[48,512]{1,0:T(8,128)(2,1)S(1)}, bf16[48,512]{1,0:T(8,128)(2,1)S(1)}, u32[]{:S(2)}, u32[]{:S(2)}) collective-permute-start(bf16[48,512]{1,0:T(8,128)(2,1)S(1)} %get-tuple-element.121), channel_id=1, source_target_pairs={{8,0},{12,4},{0,8},{4,12},{9,1},{13,5},{1,9},{5,13},{10,2},{14,6},... | collective-permute-start | bytes 147464 | tf_op jit(solution)/shard_map/ppermute | solution.py:777
  38.2 1.9 %collective-permute-start.13 = (bf16[48,512]{1,0:T(8,128)(2,1)S(1)}, bf16[48,512]{1,0:T(8,128)(2,1)S(1)}, u32[]{:S(2)}, u32[]{:S(2)}) collective-permute-start(bf16[48,512]{1,0:T(8,128)(2,1)S(1)} %get-tuple-element.122), channel_id=1, source_target_pairs={{12,0},{0,4},{4,8},{8,12},{13,1},{1,5},{5,9},{9,13},{14,2},{2,6},{... | collective-permute-start | bytes 147464 | tf_op jit(solution)/shard_map/ppermute | solution.py:777
  40.1 0.2 shard_map.203
  40.4 2.0 %collective-permute-start.15 = (bf16[48,512]{1,0:T(8,128)(2,1)S(1)}, bf16[48,512]{1,0:T(8,128)(2,1)S(1)}, u32[]{:S(2)}, u32[]{:S(2)}) collective-permute-start(bf16[48,512]{1,0:T(8,128)(2,1)S(1)} %get-tuple-element.125), channel_id=1, source_target_pairs={{4,0},{8,4},{12,8},{0,12},{5,1},{9,5},{13,9},{1,13},{6,2},{10,6},{... | collective-permute-start | bytes 147464 | tf_op jit(solution)/shard_map/ppermute | solution.py:777
  42.3 0.5 %collective-permute-start.16 = (bf16[48,512]{1,0:T(8,128)(2,1)S(1)}, bf16[48,512]{1,0:T(8,128)(2,1)S(1)}, u32[]{:S(2)}, u32[]{:S(2)}) collective-permute-start(bf16[48,512]{1,0:T(8,128)(2,1)S(1)} %get-tuple-element.126), channel_id=1, source_target_pairs={{8,0},{12,4},{0,8},{4,12},{9,1},{13,5},{1,9},{5,13},{10,2},{14,6},... | collective-permute-start | bytes 147464 | tf_op jit(solution)/shard_map/ppermute | solution.py:777
  42.9 1.4 %collective-permute-start.17 = (bf16[48,512]{1,0:T(8,128)(2,1)S(1)}, bf16[48,512]{1,0:T(8,128)(2,1)S(1)}, u32[]{:S(2)}, u32[]{:S(2)}) collective-permute-start(bf16[48,512]{1,0:T(8,128)(2,1)S(1)} %get-tuple-element.127), channel_id=1, source_target_pairs={{12,0},{0,4},{4,8},{8,12},{13,1},{1,5},{5,9},{9,13},{14,2},{2,6},{... | collective-permute-start | bytes 147464 | tf_op jit(solution)/shard_map/ppermute | solution.py:777
  44.2 3.3 %shard_map.204 = (bf16[18,16,64,128]{3,2,1,0:T(8,128)(2,1)}, bf16[18,3,1024]{2,1,0:T(4,128)(2,1)}) custom-call(f32[18,16]{1,0:T(8,128)S(1)} %get-tuple-element.107.d_ref, bf16[1024,144]{1,0:T(8,128)(2,1)S(1)} %get-tuple-element.129.turned_ref, bf16[144,256]{1,0:T(8,128)(2,1)S(1)} %get-tuple-element.114.b_ref, ...), custom_call_target="tpu_custom_call", output_to_operand_aliasing={{0}: (7, {})} | custom-call | flops 37748736 | bytes 4718592 | tf_op jit(solution)/shard_map/pallas_call | solution.py:633
  47.5 0.2 collective-permute-done.16.parts_1__2_
  47.7 1.0 %collective-permute-done.17.parts_1__3_ = bf16[48,512]{1,0:T(8,128)(2,1)S(1)} collective-permute-done((bf16[48,512]{1,0:T(8,128)(2,1)S(1)}, bf16[48,512]{1,0:T(8,128)(2,1)S(1)}, u32[]{:S(2)}, u32[]{:S(2)}) %collective-permute-start.17) | collective-permute-done | bytes 49184 | tf_op jit(solution)/shard_map/ppermute | solution.py:777
  48.7 0.9 %shard_map.205 = bf16[128,1024]{1,0:T(8,128)(2,1)} custom-call(bf16[128,192]{1,0:T(8,128)(2,1)S(1)} %get-tuple-element.73.collect_ref, bf16[48,512]{1,0:T(8,128)(2,1)S(1)} %get-tuple-element.132.parts_0__0_, bf16[48,512]{1,0:T(8,128)(2,1)S(1)} %collective-permute-done.11.parts_0__1_, bf16[48,512]{1,0:T(8,128)(2,1)S(1)} %collective-permute-done.12.parts_0__2_, ...), custom_call_target="tpu_custom_call" | custom-call | flops 1000000 | bytes 1000000 | tf_op jit(solution)/shard_map/pallas_call | solution.py:729
  (25 shorter events, 0.1 us)
Async XLA Ops:
  0.6 26.9 %slice-start = ((s8[8388608]{0:T(1024)(128)(4,1)}), s8[4194304]{0:T(1024)(128)(4,1)S(1)}, s32[]{:S(2)}) async-start(s8[8388608]{0:T(1024)(128)(4,1)} %bitcast.8), calls=%async_computation | async-start | bytes 8388608
  4.3 11.7 %collective-permute-start.3 = (bf16[48,640]{1,0:T(8,128)(2,1)S(1)}, bf16[48,640]{1,0:T(8,128)(2,1)S(1)}, u32[]{:S(2)}, u32[]{:S(2)}) collective-permute-start(bf16[48,640]{1,0:T(8,128)(2,1)S(1)} %get-tuple-element.85), channel_id=1, source_target_pairs={{0,4},{4,8},{8,12},{12,0},{1,5},{5,9},{9,13},{13,1},{2,6},{6,10},{... | collective-permute-start | bytes 184328 | tf_op jit(solution)/shard_map/ppermute | solution.py:777
  7.3 11.4 %collective-permute-start.4 = (bf16[48,640]{1,0:T(8,128)(2,1)S(1)}, bf16[48,640]{1,0:T(8,128)(2,1)S(1)}, u32[]{:S(2)}, u32[]{:S(2)}) collective-permute-start(bf16[48,640]{1,0:T(8,128)(2,1)S(1)} %get-tuple-element.86), channel_id=1, source_target_pairs={{0,8},{4,12},{8,0},{12,4},{1,9},{5,13},{9,1},{13,5},{2,10},{6,14},... | collective-permute-start | bytes 184328 | tf_op jit(solution)/shard_map/ppermute | solution.py:777
  9.9 8.8 %collective-permute-start.5 = (bf16[48,640]{1,0:T(8,128)(2,1)S(1)}, bf16[48,640]{1,0:T(8,128)(2,1)S(1)}, u32[]{:S(2)}, u32[]{:S(2)}) collective-permute-start(bf16[48,640]{1,0:T(8,128)(2,1)S(1)} %get-tuple-element.87), channel_id=1, source_target_pairs={{0,12},{4,0},{8,4},{12,8},{1,13},{5,1},{9,5},{13,9},{2,14},{6,2},{... | collective-permute-start | bytes 184328 | tf_op jit(solution)/shard_map/ppermute | solution.py:777
  11.3 7.5 %copy-start.2 = (bf16[18,3,512]{2,1,0:T(4,128)(2,1)S(1)}, bf16[18,3,512]{2,1,0:T(4,128)(2,1)}, u32[]{:S(2)}) copy-start(bf16[18,3,512]{2,1,0:T(4,128)(2,1)} %conv_ref.2) | copy-start | bytes 165892
  11.3 7.5 %copy-start.4 = (f32[4,512]{1,0:T(4,128)S(1)}, f32[4,512]{1,0:T(4,128)}, u32[]{:S(2)}) copy-start(f32[4,512]{1,0:T(4,128)} %refs_5_.2) | copy-start | bytes 24580
  11.3 9.6 %copy-start.1 = (bf16[18,3,1024]{2,1,0:T(4,128)(2,1)S(1)}, bf16[18,3,1024]{2,1,0:T(4,128)(2,1)}, u32[]{:S(2)}) copy-start(bf16[18,3,1024]{2,1,0:T(4,128)(2,1)} %conv_ref.3) | copy-start | bytes 331780
  11.3 9.6 %copy-start.3 = (f32[4,1024]{1,0:T(4,128)S(1)}, f32[4,1024]{1,0:T(4,128)}, u32[]{:S(2)}) copy-start(f32[4,1024]{1,0:T(4,128)} %refs_5_.3) | copy-start | bytes 49156
  11.3 9.6 %copy-start.7 = (f32[16]{0:T(128)S(1)}, f32[16]{0:T(128)}, u32[]{:S(2)}) copy-start(f32[16]{0:T(128)} %param.23) | copy-start | bytes 196
  11.3 9.6 %copy-start.8 = (f32[16]{0:T(128)S(1)}, f32[16]{0:T(128)}, u32[]{:S(2)}) copy-start(f32[16]{0:T(128)} %param.24) | copy-start | bytes 196
  11.3 12.7 %copy-start = (bf16[18,16,64,128]{3,2,1,0:T(8,128)(2,1)S(1)}, bf16[18,16,64,128]{3,2,1,0:T(8,128)(2,1)}, u32[]{:S(2)}) copy-start(bf16[18,16,64,128]{3,2,1,0:T(8,128)(2,1)} %pool.1) | copy-start | bytes 14155780
  11.3 16.2 %slice-start.1 = ((s8[8388608]{0:T(1024)(128)(4,1)}), s8[4194304]{0:T(1024)(128)(4,1)S(1)}, s32[]{:S(2)}) async-start(s8[8388608]{0:T(1024)(128)(4,1)} %bitcast.8), calls=%async_computation.1 | async-start | bytes 8388608
  14.9 10.7 %copy-start.5 = (f32[1024]{0:T(1024)S(1)}, f32[1024]{0:T(1024)}, u32[]{:S(2)}) copy-start(f32[1024]{0:T(1024)} %param.26) | copy-start | bytes 12292
  14.9 10.7 %copy-start.6 = (f32[16]{0:T(128)S(1)}, f32[16]{0:T(128)}, u32[]{:S(2)}) copy-start(f32[16]{0:T(128)} %param.25) | copy-start | bytes 196
  14.9 10.7 %collective-permute-start = (bf16[48,1024]{1,0:T(8,128)(2,1)S(1)}, bf16[48,1024]{1,0:T(8,128)(2,1)S(1)}, u32[]{:S(2)}, u32[]{:S(2)}) collective-permute-start(bf16[48,1024]{1,0:T(8,128)(2,1)S(1)} %get-tuple-element.80), channel_id=1, source_target_pairs={{0,4},{4,8},{8,12},{12,0},{1,5},{5,9},{9,13},{13,1},{2,6},{6,10},{... | collective-permute-start | bytes 294920 | tf_op jit(solution)/shard_map/ppermute | solution.py:777
  15.6 9.9 %collective-permute-start.1 = (bf16[48,1024]{1,0:T(8,128)(2,1)S(1)}, bf16[48,1024]{1,0:T(8,128)(2,1)S(1)}, u32[]{:S(2)}, u32[]{:S(2)}) collective-permute-start(bf16[48,1024]{1,0:T(8,128)(2,1)S(1)} %get-tuple-element.81), channel_id=1, source_target_pairs={{0,8},{4,12},{8,0},{12,4},{1,9},{5,13},{9,1},{13,5},{2,10},{6,14},... | collective-permute-start | bytes 294920 | tf_op jit(solution)/shard_map/ppermute | solution.py:777
  15.9 9.6 %collective-permute-start.2 = (bf16[48,1024]{1,0:T(8,128)(2,1)S(1)}, bf16[48,1024]{1,0:T(8,128)(2,1)S(1)}, u32[]{:S(2)}, u32[]{:S(2)}) collective-permute-start(bf16[48,1024]{1,0:T(8,128)(2,1)S(1)} %get-tuple-element.82), channel_id=1, source_target_pairs={{0,12},{4,0},{8,4},{12,8},{1,13},{5,1},{9,5},{13,9},{2,14},{6,2},{... | collective-permute-start | bytes 294920 | tf_op jit(solution)/shard_map/ppermute | solution.py:777
  19.3 4.7 %collective-permute-start.6 = (bf16[144,256]{1,0:T(8,128)(2,1)S(1)}, bf16[144,256]{1,0:T(8,128)(2,1)S(1)}, u32[]{:S(2)}, u32[]{:S(2)}) collective-permute-start(bf16[144,256]{1,0:T(8,128)(2,1)S(1)} %get-tuple-element.98), channel_id=1, source_target_pairs={{2,0},{0,1},{3,2},{1,3},{6,4},{4,5},{7,6},{5,7},{10,8},{8,9},{11,1... | collective-permute-start | bytes 221192 | tf_op jit(solution)/shard_map/ppermute | solution.py:789
  19.3 4.6 %collective-permute-start.7 = (bf16[144,256]{1,0:T(8,128)(2,1)S(1)}, bf16[144,256]{1,0:T(8,128)(2,1)S(1)}, u32[]{:S(2)}, u32[]{:S(2)}) collective-permute-start(bf16[144,256]{1,0:T(8,128)(2,1)S(1)} %get-tuple-element.99), channel_id=1, source_target_pairs={{2,1},{1,2},{0,3},{3,0},{6,5},{5,6},{4,7},{7,4},{10,9},{9,10},{8,1... | collective-permute-start | bytes 221192 | tf_op jit(solution)/shard_map/ppermute | solution.py:789
  28.0 2.1 %collective-permute-start.8 = (bf16[128,1024]{1,0:T(8,128)(2,1)S(1)}, bf16[128,1024]{1,0:T(8,128)(2,1)S(1)}, u32[]{:S(2)}, u32[]{:S(2)}) collective-permute-start(bf16[128,1024]{1,0:T(8,128)(2,1)S(1)} %shard_map.199), channel_id=1, source_target_pairs={{0,1},{1,0},{2,3},{3,2},{4,5},{5,4},{6,7},{7,6},{8,9},{9,8},{10,11... | collective-permute-start | bytes 786440 | tf_op jit(solution)/shard_map/ppermute | solution.py:801
  30.0 5.4 %collective-permute-start.9 = (bf16[128,1024]{1,0:T(8,128)(2,1)S(1)}, bf16[128,1024]{1,0:T(8,128)(2,1)S(1)}, u32[]{:S(2)}, u32[]{:S(2)}) collective-permute-start(bf16[128,1024]{1,0:T(8,128)(2,1)S(1)} %get-tuple-element.117), channel_id=1, source_target_pairs={{0,1},{1,0},{2,3},{3,2},{4,5},{5,4},{6,7},{7,6},{8,9},{9,8},{10,11... | collective-permute-start | bytes 786440 | tf_op jit(solution)/shard_map/ppermute | solution.py:814
  30.2 5.9 %collective-permute-start.10 = (bf16[128,512]{1,0:T(8,128)(2,1)S(1)}, bf16[128,512]{1,0:T(8,128)(2,1)S(1)}, u32[]{:S(2)}, u32[]{:S(2)}) collective-permute-start(bf16[128,512]{1,0:T(8,128)(2,1)S(1)} %get-tuple-element.110), channel_id=1, source_target_pairs={{0,2},{1,3},{2,0},{3,1},{4,6},{5,7},{6,4},{7,5},{8,10},{9,11},{10,... | collective-permute-start | bytes 393224 | tf_op jit(solution)/shard_map/ppermute | solution.py:809
  34.6 5.5 %collective-permute-start.14 = (bf16[128,512]{1,0:T(8,128)(2,1)S(1)}, bf16[128,512]{1,0:T(8,128)(2,1)S(1)}, u32[]{:S(2)}, u32[]{:S(2)}) collective-permute-start(bf16[128,512]{1,0:T(8,128)(2,1)S(1)} %get-tuple-element.123), channel_id=1, source_target_pairs={{0,2},{1,3},{2,0},{3,1},{4,6},{5,7},{6,4},{7,5},{8,10},{9,11},{10,... | collective-permute-start | bytes 393224 | tf_op jit(solution)/shard_map/ppermute | solution.py:809
  36.3 6.5 %collective-permute-start.11 = (bf16[48,512]{1,0:T(8,128)(2,1)S(1)}, bf16[48,512]{1,0:T(8,128)(2,1)S(1)}, u32[]{:S(2)}, u32[]{:S(2)}) collective-permute-start(bf16[48,512]{1,0:T(8,128)(2,1)S(1)} %get-tuple-element.120), channel_id=1, source_target_pairs={{4,0},{8,4},{12,8},{0,12},{5,1},{9,5},{13,9},{1,13},{6,2},{10,6},{... | collective-permute-start | bytes 147464 | tf_op jit(solution)/shard_map/ppermute | solution.py:777
  37.6 9.9 %collective-permute-start.12 = (bf16[48,512]{1,0:T(8,128)(2,1)S(1)}, bf16[48,512]{1,0:T(8,128)(2,1)S(1)}, u32[]{:S(2)}, u32[]{:S(2)}) collective-permute-start(bf16[48,512]{1,0:T(8,128)(2,1)S(1)} %get-tuple-element.121), channel_id=1, source_target_pairs={{8,0},{12,4},{0,8},{4,12},{9,1},{13,5},{1,9},{5,13},{10,2},{14,6},... | collective-permute-start | bytes 147464 | tf_op jit(solution)/shard_map/ppermute | solution.py:777
  38.2 9.3 %collective-permute-start.13 = (bf16[48,512]{1,0:T(8,128)(2,1)S(1)}, bf16[48,512]{1,0:T(8,128)(2,1)S(1)}, u32[]{:S(2)}, u32[]{:S(2)}) collective-permute-start(bf16[48,512]{1,0:T(8,128)(2,1)S(1)} %get-tuple-element.122), channel_id=1, source_target_pairs={{12,0},{0,4},{4,8},{8,12},{13,1},{1,5},{5,9},{9,13},{14,2},{2,6},{... | collective-permute-start | bytes 147464 | tf_op jit(solution)/shard_map/ppermute | solution.py:777
  40.4 7.1 %collective-permute-start.15 = (bf16[48,512]{1,0:T(8,128)(2,1)S(1)}, bf16[48,512]{1,0:T(8,128)(2,1)S(1)}, u32[]{:S(2)}, u32[]{:S(2)}) collective-permute-start(bf16[48,512]{1,0:T(8,128)(2,1)S(1)} %get-tuple-element.125), channel_id=1, source_target_pairs={{4,0},{8,4},{12,8},{0,12},{5,1},{9,5},{13,9},{1,13},{6,2},{10,6},{... | collective-permute-start | bytes 147464 | tf_op jit(solution)/shard_map/ppermute | solution.py:777
  42.3 5.4 %collective-permute-start.16 = (bf16[48,512]{1,0:T(8,128)(2,1)S(1)}, bf16[48,512]{1,0:T(8,128)(2,1)S(1)}, u32[]{:S(2)}, u32[]{:S(2)}) collective-permute-start(bf16[48,512]{1,0:T(8,128)(2,1)S(1)} %get-tuple-element.126), channel_id=1, source_target_pairs={{8,0},{12,4},{0,8},{4,12},{9,1},{13,5},{1,9},{5,13},{10,2},{14,6},... | collective-permute-start | bytes 147464 | tf_op jit(solution)/shard_map/ppermute | solution.py:777
  42.9 5.9 %collective-permute-start.17 = (bf16[48,512]{1,0:T(8,128)(2,1)S(1)}, bf16[48,512]{1,0:T(8,128)(2,1)S(1)}, u32[]{:S(2)}, u32[]{:S(2)}) collective-permute-start(bf16[48,512]{1,0:T(8,128)(2,1)S(1)} %get-tuple-element.127), channel_id=1, source_target_pairs={{12,0},{0,4},{4,8},{8,12},{13,1},{1,5},{5,9},{9,13},{14,2},{2,6},{... | collective-permute-start | bytes 147464 | tf_op jit(solution)/shard_map/ppermute | solution.py:777
